TPU v7x, 512 devices: a whole 4x4x16 slice. The times are simulated.
512 devices in a mesh: gx: 64 (over z, x), gy: 4 (over y), ma: 2 (over core).
Axes of the slice: x: 4, y: 4, z: 16, core: 2. Of those that a mesh axis runs over, the one named last changes fastest.
Arguments:
- permeability: float32 [1024, 128, 128], P(('ma', 'gx'), 'gy'), parts along dimension 0, may hold values from 0.05 to 20
- storage: float32 [1024, 128, 128], P(('ma', 'gx'), 'gy'), parts along dimension 0, may hold values from 0.05 to 0.5
- source_term: float32 [1024, 128, 128], P(('ma', 'gx'), 'gy'), parts along dimension 0, may hold values from -24 to 24
Outputs:
- pressure: float32 [1024, 128, 128], P(('ma', 'gx'), 'gy'), parts along dimension 0
- residual: float32 [1024, 128, 128], P(('ma', 'gx'), 'gy'), parts along dimension 0
There are 2 independent parts, one for each index of `ma`. A program takes and returns all parts, laid end to end along the dimension named above; each array names one. Nothing has to cross between parts.
All inputs are finite; a program needn't handle non-finite values.
Results may differ from a plain program's by a relative error of at most 0.00014.
Values sent between devices are 32-bit elements; how exact they have to be, the bound alone decides.
No kernel may reach another device: no remote copies, remote signals or barrier semaphores. Data moves between devices by JAX's collectives and lax.ppermute only.
A program may use at most 64 MiB of HBM per device.

v0:
```python
import jax
import jax.numpy as jnp
from jax import lax
from jax.sharding import PartitionSpec as P

LEVELS = 4
COARSE = 8


OMEGA = 0.7


def padded_2(array, sides, width):
    for axis, dim in sides:
        size, length = (lax.axis_size(axis), array.shape[dim])
        up = [(i, (i + 1) % size) for i in range(size - 1)]
        down = [(j, i) for i, j in up]
        last = lax.slice_in_dim(array, length - width, length, axis=dim)
        initial = lax.slice_in_dim(array, 0, width, axis=dim)
        before = lax.ppermute(last, axis, up)
        after = lax.ppermute(initial, axis, down)
        array = jnp.concatenate([before, array, after], axis=dim)
    return array


def neighbours_of(padded):
    return (
        padded[:-2, 1:-1, 1:-1],
        padded[2:, 1:-1, 1:-1],
        padded[1:-1, :-2, 1:-1],
        padded[1:-1, 2:, 1:-1],
        padded[1:-1, 1:-1, :-2],
        padded[1:-1, 1:-1, 2:],
    )


def transmissibility(padded_perm, store_now, coarsening):
    factor = 2.0**coarsening
    middle = padded_perm[1:-1, 1:-1, 1:-1]
    transmit = tuple(
        (
            factor * 2.0 * middle * beside / (middle + beside)
            for beside in neighbours_of(padded_perm)
        )
    )
    diagonal = (
        store_now
        + transmit[0]
        + transmit[1]
        + transmit[2]
        + transmit[3]
        + transmit[4]
        + transmit[5]
    )
    return (transmit, diagonal)


def operate(padded, transmit, store_now):
    centre = padded[1:-1, 1:-1, 1:-1]
    beside_all = neighbours_of(padded)
    outflow = transmit[0] * (centre - beside_all[0])
    for position in range(1, 6):
        outflow = outflow + transmit[position] * (centre - beside_all[position])
    return store_now * centre + outflow


def restrict(field):
    length_x, length_y, length_z = field.shape
    return field.reshape(length_x // 2, 2, length_y // 2, 2, length_z // 2, 2).sum(axis=(1, 3, 5))


def prolong(field):
    length_x, length_y, length_z = field.shape
    spread_out = jnp.broadcast_to(
        field[:, None, :, None, :, None], (length_x, 2, length_y, 2, length_z, 2)
    )
    return spread_out.reshape(2 * length_x, 2 * length_y, 2 * length_z)


def extend(field, coarsening):
    if coarsening == 0:
        extended = padded_2(field, (("gx", 0), ("gy", 1)), 1)
    elif coarsening < LEVELS - 1:
        extended = padded_2(field, (("gx", 0), ("gy", 1)), 1)
    else:
        extended = padded_2(field, (("gx", 0), ("gy", 1)), 1)
    return jnp.pad(extended, ((0, 0), (0, 0), (1, 1)))


def relax(iterate, source, transmit, diagonal, store_now, coarsening):
    return (
        iterate
        + OMEGA * (source - operate(extend(iterate, coarsening), transmit, store_now)) / diagonal
    )


def body(permeability, storage, source_term):
    operators = []
    perm_now, store_now = (permeability, storage)
    for coarsening in range(LEVELS - 1):
        transmit, diagonal = transmissibility(extend(perm_now, coarsening), store_now, coarsening)
        operators.append((transmit, diagonal, store_now))
        perm_now = restrict(perm_now) * 0.125
        store_now = restrict(store_now)
    bottom_transmit, bottom_diagonal = transmissibility(
        extend(perm_now, LEVELS - 1), store_now, LEVELS - 1
    )

    def bottom_solve(source):
        iterate = OMEGA * source / bottom_diagonal
        for sweep_count in range(COARSE - 1):
            iterate = relax(
                iterate, source, bottom_transmit, bottom_diagonal, store_now, LEVELS - 1
            )
        return iterate

    def cycle(source, coarsening):
        if coarsening == LEVELS - 1:
            return bottom_solve(source)
        transmit, diagonal, store_here = operators[coarsening]
        iterate = OMEGA * source / diagonal
        iterate = relax(iterate, source, transmit, diagonal, store_here, coarsening)
        defect = source - operate(extend(iterate, coarsening), transmit, store_here)
        iterate = iterate + prolong(cycle(restrict(defect), coarsening + 1))
        iterate = relax(iterate, source, transmit, diagonal, store_here, coarsening)
        iterate = relax(iterate, source, transmit, diagonal, store_here, coarsening)
        return iterate

    pressure = cycle(source_term, 0)
    fine_transmit, fine_diagonal, fine_store = operators[0]
    residual = source_term - operate(extend(pressure, 0), fine_transmit, fine_store)
    return (pressure, residual)


def solution(mesh):
    return jax.shard_map(
        body,
        mesh=mesh,
        in_specs=(
            P(("ma", "gx"), "gy", None),
            P(("ma", "gx"), "gy", None),
            P(("ma", "gx"), "gy", None),
        ),
        out_specs=(P(("ma", "gx"), "gy", None), P(("ma", "gx"), "gy", None)),
        check_vma=False,
    )
```

profile of v0, /device:TPU:102, one launch (start us, length us, event | category | flops | bytes accessed | tf_op | source)
XLA Modules:
  0.0 490.7 jit_solution(6131324208390728455)
XLA Ops:
  9.2 6.1 %collective-permute-done.1 = f32[1,32,128]{2,1,0:T(8,128)S(1)} collective-permute-done((f32[1,32,128]{2,1,0:T(8,128)S(1)}, f32[1,32,128]{2,1,0:T(8,128)S(1)}, u32[]{:S(2)}, u32[]{:S(2)}) %collective-permute-start.1) | collective-permute-done | bytes 16416 | tf_op jit(solution)/shard_map/ppermute | solution.py:21
  21.3 10.5 %reshape.77 = f32[4,2,16,2,64,2]{5,4,3,2,1,0:T(8,128)} reshape(f32[8,32,128]{2,1,0:T(8,128)} %param.3) | data formatting | bytes 262144 | tf_op jit(solution)/shard_map/reshape | solution.py:69
  54.0 7.2 %collective-permute-start.12 = (f32[1,16,64]{2,1,0:T(8,128)S(1)}, f32[1,16,64]{2,1,0:T(8,128)S(1)}, u32[]{:S(2)}, u32[]{:S(2)}) collective-permute-start(f32[1,16,64]{2,1,0:T(8,128)S(1)} %get-tuple-element.73), channel_id=1, source_target_pairs={{0,8},{8,16},{16,24},{24,32},{32,40},{40,48},{48,56},{56,64},{64,7... | collective-permute-start | bytes 12296 | tf_op jit(solution)/shard_map/ppermute | solution.py:20
  61.2 9.8 %reshape.76 = f32[4,2,16,2,64,2]{5,4,3,2,1,0:T(8,128)} reshape(f32[8,32,128]{2,1,0:T(8,128)S(1)} %copy-done.1) | data formatting | bytes 262144 | tf_op jit(solution)/shard_map/reshape | solution.py:69
  84.0 5.2 %collective-permute-start.14 = (f32[6,1,64]{2,1,0:T(1,128)S(1)}, f32[6,1,64]{2,1,0:T(1,128)S(1)}, u32[]{:S(2)}, u32[]{:S(2)}) collective-permute-start(f32[6,1,64]{2,1,0:T(1,128)S(1)} %get-tuple-element.63), channel_id=1, source_target_pairs={{0,2},{2,4},{4,6},{1,3},{3,5},{5,7},{8,10},{10,12},{12,14},{9,11},... | collective-permute-start | bytes 4616 | tf_op jit(solution)/shard_map/ppermute | solution.py:20
  99.1 9.8 %reshape.75 = f32[4,2,16,2,64,2]{5,4,3,2,1,0:T(8,128)} reshape(f32[8,32,128]{2,1,0:T(8,128)S(1)} %fusion.61) | data formatting | bytes 262144 | tf_op jit(solution)/shard_map/reshape | solution.py:69
  113.0 5.2 %collective-permute-start.16 = (f32[1,16,64]{2,1,0:T(8,128)S(1)}, f32[1,16,64]{2,1,0:T(8,128)S(1)}, u32[]{:S(2)}, u32[]{:S(2)}) collective-permute-start(f32[1,16,64]{2,1,0:T(8,128)S(1)} %get-tuple-element.70), channel_id=1, source_target_pairs={{0,8},{8,16},{16,24},{24,32},{32,40},{40,48},{48,56},{56,64},{64,7... | collective-permute-start | bytes 12296 | tf_op jit(solution)/shard_map/ppermute | solution.py:20
  120.2 6.9 %collective-permute-done.17 = f32[1,16,64]{2,1,0:T(8,128)S(1)} collective-permute-done((f32[1,16,64]{2,1,0:T(8,128)S(1)}, f32[1,16,64]{2,1,0:T(8,128)S(1)}, u32[]{:S(2)}, u32[]{:S(2)}) %collective-permute-start.17) | collective-permute-done | bytes 4128 | tf_op jit(solution)/shard_map/ppermute | solution.py:21
  133.8 7.2 %collective-permute-start.24 = (f32[1,8,32]{2,1,0:T(8,128)S(1)}, f32[1,8,32]{2,1,0:T(8,128)S(1)}, u32[]{:S(2)}, u32[]{:S(2)}) collective-permute-start(f32[1,8,32]{2,1,0:T(8,128)S(1)} %get-tuple-element.94), channel_id=1, source_target_pairs={{0,8},{8,16},{16,24},{24,32},{32,40},{40,48},{48,56},{56,64},{64,7... | collective-permute-start | bytes 3080 | tf_op jit(solution)/shard_map/ppermute | solution.py:20
  149.8 5.2 %collective-permute-start.26 = (f32[4,1,32]{2,1,0:T(1,128)S(1)}, f32[4,1,32]{2,1,0:T(1,128)S(1)}, u32[]{:S(2)}, u32[]{:S(2)}) collective-permute-start(f32[4,1,32]{2,1,0:T(1,128)S(1)} %get-tuple-element.83), channel_id=1, source_target_pairs={{0,2},{2,4},{4,6},{1,3},{3,5},{5,7},{8,10},{10,12},{12,14},{9,11},... | collective-permute-start | bytes 1544 | tf_op jit(solution)/shard_map/ppermute | solution.py:20
  165.9 5.2 %collective-permute-start.28 = (f32[1,8,32]{2,1,0:T(8,128)S(1)}, f32[1,8,32]{2,1,0:T(8,128)S(1)}, u32[]{:S(2)}, u32[]{:S(2)}) collective-permute-start(f32[1,8,32]{2,1,0:T(8,128)S(1)} %get-tuple-element.91), channel_id=1, source_target_pairs={{0,8},{8,16},{16,24},{24,32},{32,40},{40,48},{48,56},{56,64},{64,7... | collective-permute-start | bytes 3080 | tf_op jit(solution)/shard_map/ppermute | solution.py:20
  185.2 7.2 %collective-permute-start.36 = (f32[1,4,16]{2,1,0:T(4,128)S(1)}, f32[1,4,16]{2,1,0:T(4,128)S(1)}, u32[]{:S(2)}, u32[]{:S(2)}) collective-permute-start(f32[1,4,16]{2,1,0:T(4,128)S(1)} %multiply_bitcast_fusion), channel_id=1, source_target_pairs={{0,8},{8,16},{16,24},{24,32},{32,40},{40,48},{48,56},{56,64},{64,7... | collective-permute-start | bytes 776 | tf_op jit(solution)/shard_map/ppermute | solution.py:20
  199.8 5.2 %collective-permute-start.38 = (f32[3,1,16]{2,1,0:T(1,128)S(1)}, f32[3,1,16]{2,1,0:T(1,128)S(1)}, u32[]{:S(2)}, u32[]{:S(2)}) collective-permute-start(f32[3,1,16]{2,1,0:T(1,128)S(1)} %get-tuple-element.110), channel_id=1, source_target_pairs={{0,2},{2,4},{4,6},{1,3},{3,5},{5,7},{8,10},{10,12},{12,14},{9,11},... | collective-permute-start | bytes 584 | tf_op jit(solution)/shard_map/ppermute | solution.py:20
  216.8 7.2 %collective-permute-start.40 = (f32[1,4,16]{2,1,0:T(4,128)S(1)}, f32[1,4,16]{2,1,0:T(4,128)S(1)}, u32[]{:S(2)}, u32[]{:S(2)}) collective-permute-start(f32[1,4,16]{2,1,0:T(4,128)S(1)} %get-tuple-element.2), channel_id=1, source_target_pairs={{0,8},{8,16},{16,24},{24,32},{32,40},{40,48},{48,56},{56,64},{64,7... | collective-permute-start | bytes 776 | tf_op jit(solution)/shard_map/ppermute | solution.py:20
  234.8 7.5 %collective-permute-start.44 = (f32[1,4,16]{2,1,0:T(4,128)S(1)}, f32[1,4,16]{2,1,0:T(4,128)S(1)}, u32[]{:S(2)}, u32[]{:S(2)}) collective-permute-start(f32[1,4,16]{2,1,0:T(4,128)S(1)} %fusion.370), channel_id=1, source_target_pairs={{0,8},{8,16},{16,24},{24,32},{32,40},{40,48},{48,56},{56,64},{64,7... | collective-permute-start | bytes 776 | tf_op jit(solution)/shard_map/ppermute | solution.py:20
  253.1 7.5 %collective-permute-start.48 = (f32[1,4,16]{2,1,0:T(4,128)S(1)}, f32[1,4,16]{2,1,0:T(4,128)S(1)}, u32[]{:S(2)}, u32[]{:S(2)}) collective-permute-start(f32[1,4,16]{2,1,0:T(4,128)S(1)} %fusion.355), channel_id=1, source_target_pairs={{0,8},{8,16},{16,24},{24,32},{32,40},{40,48},{48,56},{56,64},{64,7... | collective-permute-start | bytes 776 | tf_op jit(solution)/shard_map/ppermute | solution.py:20
  271.4 7.5 %collective-permute-start.52 = (f32[1,4,16]{2,1,0:T(4,128)S(1)}, f32[1,4,16]{2,1,0:T(4,128)S(1)}, u32[]{:S(2)}, u32[]{:S(2)}) collective-permute-start(f32[1,4,16]{2,1,0:T(4,128)S(1)} %fusion.340), channel_id=1, source_target_pairs={{0,8},{8,16},{16,24},{24,32},{32,40},{40,48},{48,56},{56,64},{64,7... | collective-permute-start | bytes 776 | tf_op jit(solution)/shard_map/ppermute | solution.py:20
  289.7 7.5 %collective-permute-start.56 = (f32[1,4,16]{2,1,0:T(4,128)S(1)}, f32[1,4,16]{2,1,0:T(4,128)S(1)}, u32[]{:S(2)}, u32[]{:S(2)}) collective-permute-start(f32[1,4,16]{2,1,0:T(4,128)S(1)} %fusion.325), channel_id=1, source_target_pairs={{0,8},{8,16},{16,24},{24,32},{32,40},{40,48},{48,56},{56,64},{64,7... | collective-permute-start | bytes 776 | tf_op jit(solution)/shard_map/ppermute | solution.py:20
  308.0 7.5 %collective-permute-start.60 = (f32[1,4,16]{2,1,0:T(4,128)S(1)}, f32[1,4,16]{2,1,0:T(4,128)S(1)}, u32[]{:S(2)}, u32[]{:S(2)}) collective-permute-start(f32[1,4,16]{2,1,0:T(4,128)S(1)} %fusion.310), channel_id=1, source_target_pairs={{0,8},{8,16},{16,24},{24,32},{32,40},{40,48},{48,56},{56,64},{64,7... | collective-permute-start | bytes 776 | tf_op jit(solution)/shard_map/ppermute | solution.py:20
  326.3 7.5 %collective-permute-start.64 = (f32[1,4,16]{2,1,0:T(4,128)S(1)}, f32[1,4,16]{2,1,0:T(4,128)S(1)}, u32[]{:S(2)}, u32[]{:S(2)}) collective-permute-start(f32[1,4,16]{2,1,0:T(4,128)S(1)} %fusion.295), channel_id=1, source_target_pairs={{0,8},{8,16},{16,24},{24,32},{32,40},{40,48},{48,56},{56,64},{64,7... | collective-permute-start | bytes 776 | tf_op jit(solution)/shard_map/ppermute | solution.py:20
  342.8 7.5 %collective-permute-start.68 = (f32[1,8,32]{2,1,0:T(8,128)S(1)}, f32[1,8,32]{2,1,0:T(8,128)S(1)}, u32[]{:S(2)}, u32[]{:S(2)}) collective-permute-start(f32[1,8,32]{2,1,0:T(8,128)S(1)} %get-tuple-element.86), channel_id=1, source_target_pairs={{0,8},{8,16},{16,24},{24,32},{32,40},{40,48},{48,56},{56,64},{64,7... | collective-permute-start | bytes 3080 | tf_op jit(solution)/shard_map/ppermute | solution.py:20
  352.3 6.9 %collective-permute-done.69 = f32[1,8,32]{2,1,0:T(8,128)S(1)} collective-permute-done((f32[1,8,32]{2,1,0:T(8,128)S(1)}, f32[1,8,32]{2,1,0:T(8,128)S(1)}, u32[]{:S(2)}, u32[]{:S(2)}) %collective-permute-start.69) | collective-permute-done | bytes 1056 | tf_op jit(solution)/shard_map/ppermute | solution.py:21
  426.8 6.9 %reshape.81 = f32[8,32,128]{2,1,0:T(8,128)S(1)} reshape(f32[4,2,16,2,64,2]{5,4,3,2,1,0:T(8,128)} %broadcast_in_dim.29) | data formatting | bytes 262144 | tf_op jit(solution)/shard_map/reshape | solution.py:77
  439.6 5.0 %collective-permute-done.85 = f32[1,32,128]{2,1,0:T(8,128)S(1)} collective-permute-done((f32[1,32,128]{2,1,0:T(8,128)S(1)}, f32[1,32,128]{2,1,0:T(8,128)S(1)}, u32[]{:S(2)}, u32[]{:S(2)}) %collective-permute-start.85) | collective-permute-done | bytes 16416 | tf_op jit(solution)/shard_map/ppermute | solution.py:21
  (301 shorter events, 318.9 us)
Async XLA Ops:
  15.3 20.6 %collective-permute-start.3 = (f32[10,1,128]{2,1,0:T(1,128)S(1)}, f32[10,1,128]{2,1,0:T(1,128)S(1)}, u32[]{:S(2)}, u32[]{:S(2)}) collective-permute-start(f32[10,1,128]{2,1,0:T(1,128)S(1)} %get-tuple-element.39), channel_id=1, source_target_pairs={{2,0},{4,2},{6,4},{3,1},{5,3},{7,5},{10,8},{12,10},{14,12},{11,9},... | collective-permute-start | bytes 15368 | tf_op jit(solution)/shard_map/ppermute | solution.py:21
  16.6 19.3 %collective-permute-start.2 = (f32[10,1,128]{2,1,0:T(1,128)S(1)}, f32[10,1,128]{2,1,0:T(1,128)S(1)}, u32[]{:S(2)}, u32[]{:S(2)}) collective-permute-start(f32[10,1,128]{2,1,0:T(1,128)S(1)} %get-tuple-element.40), channel_id=1, source_target_pairs={{0,2},{2,4},{4,6},{1,3},{3,5},{5,7},{8,10},{10,12},{12,14},{9,11},... | collective-permute-start | bytes 15368 | tf_op jit(solution)/shard_map/ppermute | solution.py:20
  47.3 29.0 %collective-permute-start.6 = (f32[10,1,128]{2,1,0:T(1,128)S(1)}, f32[10,1,128]{2,1,0:T(1,128)S(1)}, u32[]{:S(2)}, u32[]{:S(2)}) collective-permute-start(f32[10,1,128]{2,1,0:T(1,128)S(1)} %get-tuple-element.37), channel_id=1, source_target_pairs={{0,2},{2,4},{4,6},{1,3},{3,5},{5,7},{8,10},{10,12},{12,14},{9,11},... | collective-permute-start | bytes 15368 | tf_op jit(solution)/shard_map/ppermute | solution.py:20
  50.8 25.6 %collective-permute-start.7 = (f32[10,1,128]{2,1,0:T(1,128)S(1)}, f32[10,1,128]{2,1,0:T(1,128)S(1)}, u32[]{:S(2)}, u32[]{:S(2)}) collective-permute-start(f32[10,1,128]{2,1,0:T(1,128)S(1)} %get-tuple-element.38), channel_id=1, source_target_pairs={{2,0},{4,2},{6,4},{3,1},{5,3},{7,5},{10,8},{12,10},{14,12},{11,9},... | collective-permute-start | bytes 15368 | tf_op jit(solution)/shard_map/ppermute | solution.py:21
  52.1 30.6 %collective-permute-start.13 = (f32[1,16,64]{2,1,0:T(8,128)S(1)}, f32[1,16,64]{2,1,0:T(8,128)S(1)}, u32[]{:S(2)}, u32[]{:S(2)}) collective-permute-start(f32[1,16,64]{2,1,0:T(8,128)S(1)} %get-tuple-element.72), channel_id=1, source_target_pairs={{8,0},{16,8},{24,16},{32,24},{40,32},{48,40},{56,48},{64,56},{72,6... | collective-permute-start | bytes 12296 | tf_op jit(solution)/shard_map/ppermute | solution.py:21
  54.0 28.7 %collective-permute-start.12 = (f32[1,16,64]{2,1,0:T(8,128)S(1)}, f32[1,16,64]{2,1,0:T(8,128)S(1)}, u32[]{:S(2)}, u32[]{:S(2)}) collective-permute-start(f32[1,16,64]{2,1,0:T(8,128)S(1)} %get-tuple-element.73), channel_id=1, source_target_pairs={{0,8},{8,16},{16,24},{24,32},{32,40},{40,48},{48,56},{56,64},{64,7... | collective-permute-start | bytes 12296 | tf_op jit(solution)/shard_map/ppermute | solution.py:20
  76.8 12.4 %collective-permute-start.8 = (f32[1,32,128]{2,1,0:T(8,128)S(1)}, f32[1,32,128]{2,1,0:T(8,128)S(1)}, u32[]{:S(2)}, u32[]{:S(2)}) collective-permute-start(f32[1,32,128]{2,1,0:T(8,128)S(1)} %get-tuple-element.48), channel_id=1, source_target_pairs={{0,8},{8,16},{16,24},{24,32},{32,40},{40,48},{48,56},{56,64},{64,7... | collective-permute-start | bytes 49160 | tf_op jit(solution)/shard_map/ppermute | solution.py:20
  78.7 10.5 %collective-permute-start.9 = (f32[1,32,128]{2,1,0:T(8,128)S(1)}, f32[1,32,128]{2,1,0:T(8,128)S(1)}, u32[]{:S(2)}, u32[]{:S(2)}) collective-permute-start(f32[1,32,128]{2,1,0:T(8,128)S(1)} %get-tuple-element.49), channel_id=1, source_target_pairs={{8,0},{16,8},{24,16},{32,24},{40,32},{48,40},{56,48},{64,56},{72,6... | collective-permute-start | bytes 49160 | tf_op jit(solution)/shard_map/ppermute | solution.py:21
  82.7 11.8 %collective-permute-start.15 = (f32[6,1,64]{2,1,0:T(1,128)S(1)}, f32[6,1,64]{2,1,0:T(1,128)S(1)}, u32[]{:S(2)}, u32[]{:S(2)}) collective-permute-start(f32[6,1,64]{2,1,0:T(1,128)S(1)} %get-tuple-element.62), channel_id=1, source_target_pairs={{2,0},{4,2},{6,4},{3,1},{5,3},{7,5},{10,8},{12,10},{14,12},{11,9},... | collective-permute-start | bytes 4616 | tf_op jit(solution)/shard_map/ppermute | solution.py:21
  84.0 10.5 %collective-permute-start.14 = (f32[6,1,64]{2,1,0:T(1,128)S(1)}, f32[6,1,64]{2,1,0:T(1,128)S(1)}, u32[]{:S(2)}, u32[]{:S(2)}) collective-permute-start(f32[6,1,64]{2,1,0:T(1,128)S(1)} %get-tuple-element.63), channel_id=1, source_target_pairs={{0,2},{2,4},{4,6},{1,3},{3,5},{5,7},{8,10},{10,12},{12,14},{9,11},... | collective-permute-start | bytes 4616 | tf_op jit(solution)/shard_map/ppermute | solution.py:20
  127.1 15.2 %collective-permute-start.18 = (f32[6,1,64]{2,1,0:T(1,128)S(1)}, f32[6,1,64]{2,1,0:T(1,128)S(1)}, u32[]{:S(2)}, u32[]{:S(2)}) collective-permute-start(f32[6,1,64]{2,1,0:T(1,128)S(1)} %get-tuple-element.60), channel_id=1, source_target_pairs={{0,2},{2,4},{4,6},{1,3},{3,5},{5,7},{8,10},{10,12},{12,14},{9,11},... | collective-permute-start | bytes 4616 | tf_op jit(solution)/shard_map/ppermute | solution.py:20
  130.6 11.7 %collective-permute-start.19 = (f32[6,1,64]{2,1,0:T(1,128)S(1)}, f32[6,1,64]{2,1,0:T(1,128)S(1)}, u32[]{:S(2)}, u32[]{:S(2)}) collective-permute-start(f32[6,1,64]{2,1,0:T(1,128)S(1)} %get-tuple-element.61), channel_id=1, source_target_pairs={{2,0},{4,2},{6,4},{3,1},{5,3},{7,5},{10,8},{12,10},{14,12},{11,9},... | collective-permute-start | bytes 4616 | tf_op jit(solution)/shard_map/ppermute | solution.py:21
  131.9 16.5 %collective-permute-start.25 = (f32[1,8,32]{2,1,0:T(8,128)S(1)}, f32[1,8,32]{2,1,0:T(8,128)S(1)}, u32[]{:S(2)}, u32[]{:S(2)}) collective-permute-start(f32[1,8,32]{2,1,0:T(8,128)S(1)} %get-tuple-element.93), channel_id=1, source_target_pairs={{8,0},{16,8},{24,16},{32,24},{40,32},{48,40},{56,48},{64,56},{72,6... | collective-permute-start | bytes 3080 | tf_op jit(solution)/shard_map/ppermute | solution.py:21
  133.8 14.6 %collective-permute-start.24 = (f32[1,8,32]{2,1,0:T(8,128)S(1)}, f32[1,8,32]{2,1,0:T(8,128)S(1)}, u32[]{:S(2)}, u32[]{:S(2)}) collective-permute-start(f32[1,8,32]{2,1,0:T(8,128)S(1)} %get-tuple-element.94), channel_id=1, source_target_pairs={{0,8},{8,16},{16,24},{24,32},{32,40},{40,48},{48,56},{56,64},{64,7... | collective-permute-start | bytes 3080 | tf_op jit(solution)/shard_map/ppermute | solution.py:20
  142.6 12.4 %collective-permute-start.20 = (f32[1,16,64]{2,1,0:T(8,128)S(1)}, f32[1,16,64]{2,1,0:T(8,128)S(1)}, u32[]{:S(2)}, u32[]{:S(2)}) collective-permute-start(f32[1,16,64]{2,1,0:T(8,128)S(1)} %get-tuple-element.68), channel_id=1, source_target_pairs={{0,8},{8,16},{16,24},{24,32},{32,40},{40,48},{48,56},{56,64},{64,7... | collective-permute-start | bytes 12296 | tf_op jit(solution)/shard_map/ppermute | solution.py:20
  144.5 10.5 %collective-permute-start.21 = (f32[1,16,64]{2,1,0:T(8,128)S(1)}, f32[1,16,64]{2,1,0:T(8,128)S(1)}, u32[]{:S(2)}, u32[]{:S(2)}) collective-permute-start(f32[1,16,64]{2,1,0:T(8,128)S(1)} %get-tuple-element.69), channel_id=1, source_target_pairs={{8,0},{16,8},{24,16},{32,24},{40,32},{48,40},{56,48},{64,56},{72,6... | collective-permute-start | bytes 12296 | tf_op jit(solution)/shard_map/ppermute | solution.py:21
  148.5 11.8 %collective-permute-start.27 = (f32[4,1,32]{2,1,0:T(1,128)S(1)}, f32[4,1,32]{2,1,0:T(1,128)S(1)}, u32[]{:S(2)}, u32[]{:S(2)}) collective-permute-start(f32[4,1,32]{2,1,0:T(1,128)S(1)} %get-tuple-element.82), channel_id=1, source_target_pairs={{2,0},{4,2},{6,4},{3,1},{5,3},{7,5},{10,8},{12,10},{14,12},{11,9},... | collective-permute-start | bytes 1544 | tf_op jit(solution)/shard_map/ppermute | solution.py:21
  149.8 10.5 %collective-permute-start.26 = (f32[4,1,32]{2,1,0:T(1,128)S(1)}, f32[4,1,32]{2,1,0:T(1,128)S(1)}, u32[]{:S(2)}, u32[]{:S(2)}) collective-permute-start(f32[4,1,32]{2,1,0:T(1,128)S(1)} %get-tuple-element.83), channel_id=1, source_target_pairs={{0,2},{2,4},{4,6},{1,3},{3,5},{5,7},{8,10},{10,12},{12,14},{9,11},... | collective-permute-start | bytes 1544 | tf_op jit(solution)/shard_map/ppermute | solution.py:20
  180.0 12.4 %collective-permute-start.30 = (f32[4,1,32]{2,1,0:T(1,128)S(1)}, f32[4,1,32]{2,1,0:T(1,128)S(1)}, u32[]{:S(2)}, u32[]{:S(2)}) collective-permute-start(f32[4,1,32]{2,1,0:T(1,128)S(1)} %get-tuple-element.80), channel_id=1, source_target_pairs={{0,2},{2,4},{4,6},{1,3},{3,5},{5,7},{8,10},{10,12},{12,14},{9,11},... | collective-permute-start | bytes 1544 | tf_op jit(solution)/shard_map/ppermute | solution.py:20
  181.9 10.5 %collective-permute-start.31 = (f32[4,1,32]{2,1,0:T(1,128)S(1)}, f32[4,1,32]{2,1,0:T(1,128)S(1)}, u32[]{:S(2)}, u32[]{:S(2)}) collective-permute-start(f32[4,1,32]{2,1,0:T(1,128)S(1)} %get-tuple-element.81), channel_id=1, source_target_pairs={{2,0},{4,2},{6,4},{3,1},{5,3},{7,5},{10,8},{12,10},{14,12},{11,9},... | collective-permute-start | bytes 1544 | tf_op jit(solution)/shard_map/ppermute | solution.py:21
  183.3 15.2 %collective-permute-start.37 = (f32[1,4,16]{2,1,0:T(4,128)S(1)}, f32[1,4,16]{2,1,0:T(4,128)S(1)}, u32[]{:S(2)}, u32[]{:S(2)}) collective-permute-start(f32[1,4,16]{2,1,0:T(4,128)S(1)} %multiply_bitcast_fusion), channel_id=1, source_target_pairs={{8,0},{16,8},{24,16},{32,24},{40,32},{48,40},{56,48},{64,56},{72,6... | collective-permute-start | bytes 776 | tf_op jit(solution)/shard_map/ppermute | solution.py:21
  185.2 13.3 %collective-permute-start.36 = (f32[1,4,16]{2,1,0:T(4,128)S(1)}, f32[1,4,16]{2,1,0:T(4,128)S(1)}, u32[]{:S(2)}, u32[]{:S(2)}) collective-permute-start(f32[1,4,16]{2,1,0:T(4,128)S(1)} %multiply_bitcast_fusion), channel_id=1, source_target_pairs={{0,8},{8,16},{16,24},{24,32},{32,40},{40,48},{48,56},{56,64},{64,7... | collective-permute-start | bytes 776 | tf_op jit(solution)/shard_map/ppermute | solution.py:20
  192.6 12.4 %collective-permute-start.32 = (f32[1,8,32]{2,1,0:T(8,128)S(1)}, f32[1,8,32]{2,1,0:T(8,128)S(1)}, u32[]{:S(2)}, u32[]{:S(2)}) collective-permute-start(f32[1,8,32]{2,1,0:T(8,128)S(1)} %get-tuple-element.89), channel_id=1, source_target_pairs={{0,8},{8,16},{16,24},{24,32},{32,40},{40,48},{48,56},{56,64},{64,7... | collective-permute-start | bytes 3080 | tf_op jit(solution)/shard_map/ppermute | solution.py:20
  198.5 11.8 %collective-permute-start.39 = (f32[3,1,16]{2,1,0:T(1,128)S(1)}, f32[3,1,16]{2,1,0:T(1,128)S(1)}, u32[]{:S(2)}, u32[]{:S(2)}) collective-permute-start(f32[3,1,16]{2,1,0:T(1,128)S(1)} %get-tuple-element.109), channel_id=1, source_target_pairs={{2,0},{4,2},{6,4},{3,1},{5,3},{7,5},{10,8},{12,10},{14,12},{11,9},... | collective-permute-start | bytes 584 | tf_op jit(solution)/shard_map/ppermute | solution.py:21
  (76 other events, 552.3 us)
where the time goes:
time: 494 us; the launch traced here: 491 us
  starting transfers between devices  281 us (57%)
  waiting for transfers between devices  139 us (28%)
  local copies, waits for them, and re-layouts  48.5 us (10%)
  other arithmetic  19.7 us (4%)
    ppermute x48, starting transfers between devices, padded_2(): before = lax.ppermute(last, axis, up)  184 us
    ppermute x48, waiting for transfers between devices, padded_2(): after = lax.ppermute(initial, axis, down)  130 us
    ppermute x48, starting transfers between devices, padded_2(): after = lax.ppermute(initial, axis, down)  97.3 us
    reshape x5, local copies, waits for them, and re-layouts, restrict(): field.reshape(length_x // 2, 2, length_y // 2, 2, length_z // 2, 2)  32.3 us
    reduce_sum x12, other arithmetic, restrict(): field.reshape(length_x // 2, 2, length_y // 2, 2, length_z // 2, 2)  13.2 us
  transfers between devices with their start and end apart: 96, of which 35 were waited for; matrix products, arithmetic and copies ran while one was open for 7% of the time, Pallas kernels for 0%

commit v1 on v0

v1 whole, which is shorter than its diff:
```python
import jax
import jax.numpy as jnp
from jax import lax
from jax.experimental import pallas as pl
from jax.experimental.pallas import tpu as pltpu
from jax.sharding import PartitionSpec as P

OMEGA = 0.7
COARSE = 8
F32 = jnp.float32


def lanes(like):
    return lax.broadcasted_iota(jnp.int32, like.shape, 1)


def rows(like):
    return lax.broadcasted_iota(jnp.int32, like.shape, 0)


def roll(v, shift, axis):
    return pltpu.roll(v, shift % v.shape[axis], axis)


def bit(v, b):
    return (lanes(v) & b) == 0


def split(p, b):
    low = bit(p, b)
    return jnp.where(low, p, roll(p, b, 1)), jnp.where(low, roll(p, -b, 1), p)


def pack2(a, b):
    return jnp.where(bit(a, 1), a, b)


def unpack2(p):
    return split(p, 1)


def pack4(a, b, c, d):
    return jnp.where(bit(a, 2), pack2(a, b), pack2(c, d))


def unpack4(p):
    even, odd = split(p, 1)
    a, c = split(even, 2)
    b, d = split(odd, 2)
    return a, b, c, d


def pack8(v):
    return jnp.where(bit(v[0], 4), pack4(*v[:4]), pack4(*v[4:]))


def unpack8(p):
    a, b, c, d = unpack4_pairs(p)
    return a[0], b[0], c[0], d[0], a[1], b[1], c[1], d[1]


def unpack4_pairs(p):
    return tuple(split(q, 4) for q in unpack4(p))


def harmonic(a, b, level):
    return 2.0**level * 2.0 * a * b / jnp.maximum(a + b, 0.01)


class Level:
    def __init__(self, level, whole_y, tx, ty, tz, store, gain):
        self.level, self.whole_y = level, whole_y
        self.tx, self.ty, self.tz, self.store, self.gain = tx, ty, tz, store, gain
        self.w = 2**level

    def build(self, perm, first, last, origin=None, extent=None):
        for p in range(first, last + 2):
            face = harmonic(perm[p], perm[p - 1], self.level)
            if origin is not None:
                at = origin + p
                face = face * jnp.where((at == 0) | (at == extent), 0.0, 1.0)
            self.tx[p] = face
        for p in range(first, last + 1):
            k = perm[p]
            ty = harmonic(k, roll(k, 1, 0), self.level)
            if self.whole_y:
                ty = jnp.where(rows(k) < 1, 0.0, ty)
            tz = jnp.where(lanes(k) < self.w, 0.0, harmonic(k, roll(k, self.w, 1), self.level))
            self.ty[p] = ty
            self.tz[p] = tz
            d = (
                self.store[p] + self.tx[p] + self.tx[p + 1] + ty + roll(ty, -1, 0)
                + tz + roll(tz, -self.w, 1)
            )
            self.gain[p] = OMEGA / jnp.maximum(d, 0.01)

    def apply(self, v, first, last, use):
        low = self.tx[first] * (v[first] - v[first - 1])
        for p in range(first, last + 1):
            here = v[p]
            high = self.tx[p + 1] * (v[p + 1] - here)
            fy = self.ty[p] * (here - roll(here, 1, 0))
            fz = self.tz[p] * (here - roll(here, self.w, 1))
            out = (
                self.store[p] * here + (low - high) + (fy - roll(fy, -1, 0))
                + (fz - roll(fz, -self.w, 1))
            )
            use(p, here, out)
            low = high

    def sweep(self, v, source, first, last):
        def use(p, here, out):
            v[p] = here + self.gain[p] * (source[p] - out)

        self.apply(v, first, last, use)

    def first_sweep(self, v, source, first, last):
        for p in range(first, last + 1):
            v[p] = self.gain[p] * source[p]

    def defect(self, r, v, source, first, last):
        def use(p, here, out):
            r[p] = source[p] - out

        self.apply(v, first, last, use)


def restrict(ref, p, count, level):
    half = count // 2
    t = ref[p, pl.ds(0, half, stride=2), :] + ref[p, pl.ds(1, half, stride=2), :]
    t = t + (ref[p + 1, pl.ds(0, half, stride=2), :] + ref[p + 1, pl.ds(1, half, stride=2), :])
    w = 2**level
    return t + jnp.where(bit(t, w), roll(t, -w, 1), roll(t, w, 1))


def doubled(ref, p, e):
    half = e.shape[0]
    ref[p, pl.ds(0, half, stride=2), :] = e
    ref[p, pl.ds(1, half, stride=2), :] = e


def rows_kernel(k, f, s, xl, xr, up, down):
    zero = jnp.zeros((8, 128), F32)
    sub = rows(zero)

    def planes(p):
        if p < 3:
            kp = lambda sl: xl[p, sl, :]
            fp = (lambda sl: xl[3 + p - 1, sl, :]) if p >= 1 else None
            sp = (lambda sl: xl[5 + p - 1, sl, :]) if p >= 1 else None
        elif p < 11:
            kp = lambda sl: k[p - 3, sl, :]
            fp = lambda sl: f[p - 3, sl, :]
            sp = lambda sl: s[p - 3, sl, :]
        else:
            kp = lambda sl: xr[p - 11, sl, :]
            fp = (lambda sl: xr[3 + p - 11, sl, :]) if p < 13 else None
            sp = (lambda sl: xr[5 + p - 11, sl, :]) if p < 13 else None
        return kp, fp, sp

    last, initial = pl.ds(24, 8), pl.ds(0, 8)
    for p in range(14):
        kp, fp, sp = planes(p)
        fl, sl = (zero, zero) if fp is None else (fp(last), sp(last))
        up[p] = jnp.where(sub >= 5, kp(last), jnp.where(sub >= 3, roll(fl, -3, 0), roll(sl, -5, 0)))
        fi, si = (zero, zero) if fp is None else (fp(initial), sp(initial))
        down[p] = jnp.where(sub < 3, kp(initial), jnp.where(sub < 5, roll(fi, 3, 0), roll(si, 5, 0)))


def fine_kernel(
    k, f, s, xl, xr, above, below, r0, v0, tx, ty, tz, st, gain, msg, ke, fe, ve, re
):
    zero = jnp.zeros((8, 128), F32)
    sub = rows(zero)
    own, edge = pl.ds(0, 32), pl.ds(32, 8)
    for p in range(14):
        a, b = above[p], below[p]
        ke[p, edge, :] = jnp.where(sub < 3, a, jnp.where(sub >= 5, b, 0.0))
        fe[p, edge, :] = jnp.where(
            sub < 2, roll(a, -3, 0), jnp.where(sub >= 6, roll(b, 3, 0), 0.0)
        )
        st[p, edge, :] = jnp.where(
            sub < 2, roll(a, -5, 0), jnp.where(sub >= 6, roll(b, 5, 0), 0.0)
        )
        if p < 3:
            ke[p, own, :] = xl[p]
            if p >= 1:
                fe[p, own, :] = xl[2 + p]
                st[p, own, :] = xl[4 + p]
        elif p < 11:
            ke[p, own, :] = k[p - 3]
            fe[p, own, :] = f[p - 3]
            st[p, own, :] = s[p - 3]
        else:
            ke[p, own, :] = xr[p - 11]
            if p < 13:
                fe[p, own, :] = xr[p - 8]
                st[p, own, :] = xr[p - 6]
    op = Level(0, False, tx, ty, tz, st, gain)
    op.build(ke, 1, 12)
    op.first_sweep(ve, fe, 1, 12)
    op.sweep(ve, fe, 2, 11)
    op.defect(re, ve, fe, 3, 10)
    for p in range(8):
        r0[p] = re[p + 3, own, :]
        v0[p] = ve[p + 3, own, :]
    source = [restrict(re, 3 + 2 * p, 32, 0) for p in range(4)]
    perm = [restrict(ke, 3 + 2 * p, 32, 0) * 0.125 for p in range(4)]
    store = [restrict(st, 3 + 2 * p, 32, 0) for p in range(4)]
    packed = [
        pack2(source[0], source[1]), pack2(source[2], source[3]),
        pack2(perm[0], perm[1]), pack2(perm[2], perm[3]),
        pack2(store[0], store[1]), pack2(store[2], store[3]),
    ]
    tiles = []
    for p in range(8):
        t = jnp.where(sub < 2, re[p + 3, pl.ds(0, 8), :], roll(re[p + 3, pl.ds(24, 8), :], -4, 0))
        tiles.append(t)
    edges = [jnp.where(sub < 4, tiles[p], roll(tiles[p + 4], 4, 0)) for p in range(4)]
    for peer in range(4):
        for i in range(6):
            msg[peer, i] = packed[i]
        for i in range(4):
            msg[peer, 6 + i // 2, pl.ds(8 * (i % 2), 8), :] = edges[i]


def middle_kernel(
    gc, gl, gr, r0, to_left, to_right, r0h, tx, ty, tz, st, gain, v1, r1, ke, fe, de
):
    for block, ref in enumerate((gl, gc, gr)):
        for j in range(4):
            sl = pl.ds(16 * j, 16)
            for half in range(2):
                for target, at in ((fe, 0), (ke, 2), (st, 4)):
                    a, b = unpack2(ref[j, at + half])
                    target[4 * block + 2 * half, sl, :] = a
                    target[4 * block + 2 * half + 1, sl, :] = b
    op = Level(1, True, tx, ty, tz, st, gain)
    op.build(ke, 1, 10)
    op.first_sweep(v1, fe, 1, 10)
    op.sweep(v1, fe, 2, 9)
    op.defect(r1, v1, fe, 3, 8)
    source = [restrict(r1, 4 + 2 * p, 64, 1) for p in range(2)]
    store = [restrict(st, 4 + 2 * p, 64, 1) for p in range(2)]
    perm = [restrict(ke, 2 + 2 * p, 64, 1) * 0.125 for p in range(4)]
    faces = [harmonic(perm[p], perm[p + 1], 2) for p in range(3)]
    for p in range(2):
        k = perm[p + 1]
        fy = jnp.where(rows(k) < 1, 0.0, harmonic(k, roll(k, 1, 0), 2))
        fz = jnp.where(lanes(k) < 4, 0.0, harmonic(k, roll(k, 4, 1), 2))
        de[p] = store[p] + faces[p] + faces[p + 1] + fy + roll(fy, -1, 0) + fz + roll(fz, -4, 1)
    block = (
        pack4(source[0], source[1], perm[1], perm[2]),
        pack4(store[0], store[1], de[0], de[1]),
    )
    edge = pack2(r1[5], r1[6])
    j = lax.axis_index("gy")
    jn, jp = jnp.minimum(j + 1, 3), jnp.maximum(j - 1, 0)
    sub = rows(jnp.zeros((8, 128), F32))
    for p in range(8):
        i = p % 4
        at = (6 + i // 2, pl.ds(8 * (i % 2), 8), slice(None))
        a, b = gc[(jn,) + at], gc[(jp,) + at]
        if p >= 4:
            a, b = roll(a, -4, 0), roll(b, -4, 0)
        r0h[p] = jnp.where(sub < 4, a, roll(b, 4, 0))
    for ref, planes in ((to_left, (0, 1)), (to_right, (6, 7))):
        ref[pl.ds(0, 32), :] = block[0]
        ref[pl.ds(32, 32), :] = block[1]
        ref[pl.ds(64, 64), :] = edge
        for n, p in enumerate(planes):
            ref[pl.ds(128 + 40 * n, 32), :] = r0[p]
            ref[pl.ds(160 + 40 * n, 8), :] = r0h[p]


def coarse_kernel(own, left, right, msg, tx, ty, tz, st, gain, v2, r2, ke, fe, de):
    n = 0
    for ref in (left, own, right):
        for b in range(3):
            a = unpack4(ref[pl.ds(64 * b, 32), :])
            c = unpack4(ref[pl.ds(64 * b + 32, 32), :])
            for half in range(2):
                fe[n + half] = a[half]
                ke[n + half] = a[2 + half]
                st[n + half] = c[half]
                de[n + half] = c[2 + half]
            n += 2
    op = Level(2, True, tx, ty, tz, st, gain)
    i = lax.axis_index("gx")
    op.build(ke, 1, 16, 2 * i - 8, 2 * lax.axis_size("gx"))
    for p in (0, 17):
        gain[p] = OMEGA / jnp.maximum(de[p], 0.01)
    op.first_sweep(v2, fe, 0, 17)
    op.sweep(v2, fe, 1, 16)
    op.defect(r2, v2, fe, 2, 15)
    zero = jnp.zeros((16, 128), F32)
    source = [restrict(r2, 2 + 2 * p, 32, 2) for p in range(7)] + [zero]
    perm = [restrict(ke, 2 + 2 * p, 32, 2) * 0.125 for p in range(7)] + [zero]
    store = [restrict(st, 2 + 2 * p, 32, 2) for p in range(7)] + [zero]
    for i, v in enumerate((source, perm, store)):
        msg[pl.ds(16 * i, 16), :] = pack8(v)


def up_kernel(
    own3, left3, right3,
    t2x, t2y, t2z, s2, g2, v2, r2,
    t1x, t1y, t1z, s1, g1, v1, r1,
    t0x, t0y, t0z, s0, g0, v0, r0, r0h,
    from_left, from_right,
    pressure, residual,
    k3, f3, s3, t3x, t3y, t3z, g3, v3, c2, c1, e1, q1, c0, q0,
):
    n = 0
    for ref in (left3, own3, right3):
        parts = [unpack8(ref[pl.ds(16 * i, 16), :]) for i in range(3)]
        for b in range(7):
            f3[n], k3[n], s3[n] = parts[0][b], parts[1][b], parts[2][b]
            n += 1
    op = Level(3, True, t3x, t3y, t3z, s3, g3)
    op.build(k3, 1, 19, lax.axis_index("gx") - 10, lax.axis_size("gx"))
    op.first_sweep(v3, f3, 1, 19)
    for m in range(1, COARSE):
        op.sweep(v3, f3, 1 + m, 19 - m)
    op = Level(2, True, t2x, t2y, t2z, s2, g2)
    for p in range(5):
        e = v3[8 + p]
        doubled(c2, 4 + 2 * p, e)
        doubled(c2, 5 + 2 * p, e)
    op.sweep(c2, r2, 5, 12)
    op.sweep(c2, r2, 6, 11)
    for p in range(6):
        e = v2[6 + p] + c2[6 + p]
        doubled(c1, 2 * p, e)
        doubled(c1, 2 * p + 1, e)
    for p in range(3, 9):
        q1[p] = r1[p]
    q1[1], q1[2] = unpack2(from_left[pl.ds(64, 64), :])
    q1[9], q1[10] = unpack2(from_right[pl.ds(64, 64), :])
    op = Level(1, True, t1x, t1y, t1z, s1, g1)
    op.sweep(c1, q1, 1, 10)
    op.sweep(c1, q1, 2, 9)
    zero = jnp.zeros((8, 128), F32)
    sub = rows(zero)
    j = lax.axis_index("gy")
    for p in range(8):
        e1[p, pl.ds(0, 8), :] = zero
        e1[p, pl.ds(8, 64), :] = v1[2 + p] + c1[2 + p]
        e1[p, pl.ds(72, 8), :] = zero
    for p in range(8):
        e = e1[p, pl.ds(pl.multiple_of(16 * j, 8), 32), :]
        for q in (2 * p - 1, 2 * p):
            if 0 <= q < 14:
                q0[0, pl.ds(0, 32, stride=2), :] = e
                q0[0, pl.ds(1, 32, stride=2), :] = e
                c0[q, pl.ds(0, 32), :] = q0[0, pl.ds(16, 32), :]
                c0[q, pl.ds(32, 8), :] = jnp.where(
                    sub < 4, q0[0, pl.ds(48, 8), :], q0[0, pl.ds(8, 8), :]
                )
    for p in range(8):
        q0[p + 4, pl.ds(0, 32), :] = r0[p]
        q0[p + 4, pl.ds(32, 8), :] = r0h[p]
    for p in range(2):
        q0[p + 2, pl.ds(0, 40), :] = from_left[pl.ds(128 + 40 * p, 40), :]
        q0[p + 12, pl.ds(0, 40), :] = from_right[pl.ds(128 + 40 * p, 40), :]

    class Source:
        def __getitem__(self, p):
            return q0[p + 1, pl.ds(0, 40), :]

    op = Level(0, False, t0x, t0y, t0z, s0, g0)
    op.sweep(c0, Source(), 1, 12)
    op.sweep(c0, Source(), 2, 11)

    def use(p, here, out):
        pressure[p - 3] = v0[p - 3] + here[:32]
        residual[p - 3] = r0[p - 3] - out[:32]

    op.apply(c0, 3, 10, use)


def call(kernel, outs, scratch, args):
    return pl.pallas_call(
        kernel,
        out_shape=[jax.ShapeDtypeStruct(s, F32) for s in outs],
        scratch_shapes=[pltpu.VMEM(s, F32) for s in scratch],
        compiler_params=pltpu.CompilerParams(vmem_limit_bytes=32 * 1024 * 1024),
    )(*args)


def shifted(x, axis, k):
    n = lax.axis_size(axis)
    return lax.ppermute(x, axis, [(i, i + k) for i in range(n) if 0 <= i + k < n])


def turned(x, axis, k):
    n = lax.axis_size(axis)
    return lax.ppermute(x, axis, [(i, (i + k) % n) for i in range(n)])


def body(permeability, storage, source_term):
    k, s, f = permeability, storage, source_term
    xl = shifted(jnp.concatenate([k[5:], f[6:], s[6:]]), "gx", 1)
    xr = shifted(jnp.concatenate([k[:3], f[:2], s[:2]]), "gx", -1)
    up, down = call(rows_kernel, [(14, 8, 128)] * 2, [], (k, f, s, xl, xr))
    below = shifted(up, "gy", 1)
    above = shifted(down, "gy", -1)
    fine = (14, 40, 128)
    r0, v0, t0x, t0y, t0z, s0, g0, msg = call(
        fine_kernel,
        [(8, 32, 128)] * 2 + [fine] * 5 + [(4, 8, 16, 128)],
        [fine] * 4,
        (k, f, s, xl, xr, above, below),
    )
    gc = lax.all_to_all(msg, "gy", 0, 0)
    gl, gr = shifted(gc, "gx", 1), shifted(gc, "gx", -1)
    mid = (12, 64, 128)
    to_left, to_right, r0h, t1x, t1y, t1z, s1, g1, v1, r1 = call(
        middle_kernel,
        [(208, 128)] * 2 + [(8, 8, 128)] + [mid] * 7,
        [mid] * 2 + [(2, 32, 128)],
        (gc, gl, gr, r0),
    )
    from_left, from_right = turned(to_right, "gx", 1), turned(to_left, "gx", -1)
    blocks = jnp.concatenate([from_left[:64], to_left[:64], from_right[:64]])
    bl, br = turned(blocks, "gx", 3), turned(blocks, "gx", -3)
    low = (18, 32, 128)
    msg3, t2x, t2y, t2z, s2, g2, v2, r2 = call(
        coarse_kernel, [(48, 128)] + [low] * 7, [low] * 3, (blocks, bl, br)
    )
    cl, cr = turned(msg3, "gx", 7), turned(msg3, "gx", -7)
    base = (21, 16, 128)
    pressure, residual = call(
        up_kernel,
        [(8, 32, 128)] * 2,
        [base] * 8 + [low, mid, (8, 80, 128), mid, fine, (15, 64, 128)],
        (
            msg3, cl, cr,
            t2x, t2y, t2z, s2, g2, v2, r2,
            t1x, t1y, t1z, s1, g1, v1, r1,
            t0x, t0y, t0z, s0, g0, v0, r0, r0h,
            from_left, from_right,
        ),
    )
    return pressure, residual


def solution(mesh):
    spec = P(("ma", "gx"), "gy", None)
    return jax.shard_map(
        body, mesh=mesh, in_specs=(spec,) * 3, out_specs=(spec,) * 2, check_vma=False
    )
```

time: 494 us -> 111 us (0.22)
  the two profiles are of different devices: /device:TPU:102 before, /device:TPU:8 now
where the time goes in v1:
time: 111 us; the launch traced here: 110 us
  starting transfers between devices  50.9 us (46%)
  waiting for transfers between devices  35 us (32%)
  Pallas kernels  13.6 us (12%)
  blocking collectives  8.37 us (8%)
  local copies, waits for them, and re-layouts  1.75 us (2%)
    ppermute x6, starting transfers between devices, turned(): return lax.ppermute(x, axis, [(i, (i + k) % n) for i in range(n)])  32.7 us
    ppermute x6, waiting for transfers between devices, turned(): return lax.ppermute(x, axis, [(i, (i + k) % n) for i in range(n)])  21.3 us
    ppermute x6, starting transfers between devices, shifted(): lax.ppermute(x, axis, [(i, i + k) for i in range(n) if 0 <= i + k < n])  18.2 us
    ppermute x6, waiting for transfers between devices, shifted(): lax.ppermute(x, axis, [(i, i + k) for i in range(n) if 0 <= i + k < n])  13.6 us
    pallas_call x5, Pallas kernels, call(): pl.pallas_call(kernel, out_shape=[jax.ShapeDtypeStruct(s, F32) for s in o...  13.6 us
    all_to_all x1, blocking collectives, body(): gc = lax.all_to_all(msg, 'gy', 0, 0)  8.37 us
  transfers between devices with their start and end apart: 12, of which 10 were waited for; matrix products, arithmetic and copies ran while one was open for 0% of the time, Pallas kernels for 0%

profile of v1, /device:TPU:8, one launch (start us, length us, event | category | flops | bytes accessed | tf_op | source)
XLA Modules:
  0.0 110.5 jit_solution(14826447700828617912)
XLA Ops:
  2.4 3.5 %collective-permute-start = (f32[7,32,128]{2,1,0:T(8,128)S(1)}, f32[7,32,128]{2,1,0:T(8,128)S(1)}, u32[]{:S(2)}, u32[]{:S(2)}) collective-permute-start(f32[7,32,128]{2,1,0:T(8,128)S(1)} %pad_maximum_fusion), channel_id=1, source_target_pairs={{0,8},{8,16},{16,24},{24,32},{32,40},{40,48},{48,56},{56,64},{64,7... | collective-permute-start | bytes 344072 | tf_op jit(solution)/shard_map/ppermute | solution.py:392
  6.0 1.3 %collective-permute-start.1 = (f32[7,32,128]{2,1,0:T(8,128)S(1)}, f32[7,32,128]{2,1,0:T(8,128)S(1)}, u32[]{:S(2)}, u32[]{:S(2)}) collective-permute-start(f32[7,32,128]{2,1,0:T(8,128)S(1)} %pad_maximum_fusion.1), channel_id=1, source_target_pairs={{8,0},{16,8},{24,16},{32,24},{40,32},{48,40},{56,48},{64,56},{72,6... | collective-permute-start | bytes 344072 | tf_op jit(solution)/shard_map/ppermute | solution.py:392
  7.3 1.1 collective-permute-done.xl
  8.3 4.3 %collective-permute-done.1.xr = f32[7,32,128]{2,1,0:T(8,128)S(1)} collective-permute-done((f32[7,32,128]{2,1,0:T(8,128)S(1)}, f32[7,32,128]{2,1,0:T(8,128)S(1)}, u32[]{:S(2)}, u32[]{:S(2)}) %collective-permute-start.1) | collective-permute-done | bytes 114720 | tf_op jit(solution)/shard_map/ppermute | solution.py:392
  12.7 5.6 %collective-permute-start.2 = (f32[14,8,128]{2,1,0:T(8,128)S(1)}, f32[14,8,128]{2,1,0:T(8,128)S(1)}, u32[]{:S(2)}, u32[]{:S(2)}) collective-permute-start(f32[14,8,128]{2,1,0:T(8,128)S(1)} %get-tuple-element.30), channel_id=1, source_target_pairs={{2,0},{4,2},{6,4},{3,1},{5,3},{7,5},{10,8},{12,10},{14,12},{11,9},... | collective-permute-start | bytes 172040 | tf_op jit(solution)/shard_map/ppermute | solution.py:392
  18.3 1.9 %collective-permute-start.3 = (f32[14,8,128]{2,1,0:T(8,128)S(1)}, f32[14,8,128]{2,1,0:T(8,128)S(1)}, u32[]{:S(2)}, u32[]{:S(2)}) collective-permute-start(f32[14,8,128]{2,1,0:T(8,128)S(1)} %get-tuple-element.31), channel_id=1, source_target_pairs={{0,2},{2,4},{4,6},{1,3},{3,5},{5,7},{8,10},{10,12},{12,14},{9,11},... | collective-permute-start | bytes 172040 | tf_op jit(solution)/shard_map/ppermute | solution.py:392
  20.3 4.1 %collective-permute-done.3.below = f32[14,8,128]{2,1,0:T(8,128)S(1)} collective-permute-done((f32[14,8,128]{2,1,0:T(8,128)S(1)}, f32[14,8,128]{2,1,0:T(8,128)S(1)}, u32[]{:S(2)}, u32[]{:S(2)}) %collective-permute-start.3) | collective-permute-done | bytes 57376 | tf_op jit(solution)/shard_map/ppermute | solution.py:392
  25.3 8.4 %all_to_all.5.gc = f32[4,8,16,128]{3,2,1,0:T(8,128)S(1)} all-to-all(f32[4,8,16,128]{3,2,1,0:T(8,128)S(1)} %get-tuple-element.32), channel_id=1, replica_groups=mesh['gx'=64,'gy'=4,'ma'=2] {'gy'}, dimensions={0} | all-to-all | bytes 524288 | tf_op jit(solution)/shard_map/all_to_all | solution.py:414
  33.7 1.3 %collective-permute-start.5 = (f32[4,8,16,128]{3,2,1,0:T(8,128)S(1)}, f32[4,8,16,128]{3,2,1,0:T(8,128)S(1)}, u32[]{:S(2)}, u32[]{:S(2)}) collective-permute-start(f32[4,8,16,128]{3,2,1,0:T(8,128)S(1)} %all_to_all.5.gc), channel_id=1, source_target_pairs={{8,0},{16,8},{24,16},{32,24},{40,32},{48,40},{56,48},{64,56},{72,6... | collective-permute-start | bytes 786440 | tf_op jit(solution)/shard_map/ppermute | solution.py:392
  35.0 4.6 %collective-permute-start.4 = (f32[4,8,16,128]{3,2,1,0:T(8,128)S(1)}, f32[4,8,16,128]{3,2,1,0:T(8,128)S(1)}, u32[]{:S(2)}, u32[]{:S(2)}) collective-permute-start(f32[4,8,16,128]{3,2,1,0:T(8,128)S(1)} %all_to_all.5.gc), channel_id=1, source_target_pairs={{0,8},{8,16},{16,24},{24,32},{32,40},{40,48},{48,56},{56,64},{64,7... | collective-permute-start | bytes 786440 | tf_op jit(solution)/shard_map/ppermute | solution.py:392
  39.5 2.4 %collective-permute-done.5.gr = f32[4,8,16,128]{3,2,1,0:T(8,128)S(1)} collective-permute-done((f32[4,8,16,128]{3,2,1,0:T(8,128)S(1)}, f32[4,8,16,128]{3,2,1,0:T(8,128)S(1)}, u32[]{:S(2)}, u32[]{:S(2)}) %collective-permute-start.5) | collective-permute-done | bytes 262176 | tf_op jit(solution)/shard_map/ppermute | solution.py:392
  41.9 1.7 %collective-permute-done.4.gl = f32[4,8,16,128]{3,2,1,0:T(8,128)S(1)} collective-permute-done((f32[4,8,16,128]{3,2,1,0:T(8,128)S(1)}, f32[4,8,16,128]{3,2,1,0:T(8,128)S(1)}, u32[]{:S(2)}, u32[]{:S(2)}) %collective-permute-start.4) | collective-permute-done | bytes 262176 | tf_op jit(solution)/shard_map/ppermute | solution.py:392
  43.7 2.5 %shard_map.52 = (f32[208,128]{1,0:T(8,128)S(1)}, f32[208,128]{1,0:T(8,128)S(1)}, f32[8,8,128]{2,1,0:T(8,128)S(1)}, f32[12,64,128]{2,1,0:T(8,128)S(1)}, f32[12,64...) custom-call(f32[4,8,16,128]{3,2,1,0:T(8,128)S(1)} %all_to_all.5.gc, ...), custom_call_target="tpu_custom_call" | custom-call | tf_op jit(solution)/shard_map/pallas_call | solution.py:382
  46.1 4.4 %collective-permute-start.6 = (f32[208,128]{1,0:T(8,128)S(1)}, f32[208,128]{1,0:T(8,128)S(1)}, u32[]{:S(2)}, u32[]{:S(2)}) collective-permute-start(f32[208,128]{1,0:T(8,128)S(1)} %get-tuple-element.34), channel_id=1, source_target_pairs={{0,8},{8,16},{16,24},{24,32},{32,40},{40,48},{48,56},{56,64},{64,7... | collective-permute-start | bytes 319496 | tf_op jit(solution)/shard_map/ppermute | solution.py:397
  50.5 10.3 %collective-permute-start.7 = (f32[208,128]{1,0:T(8,128)S(1)}, f32[208,128]{1,0:T(8,128)S(1)}, u32[]{:S(2)}, u32[]{:S(2)}) collective-permute-start(f32[208,128]{1,0:T(8,128)S(1)} %get-tuple-element.35), channel_id=1, source_target_pairs={{0,504},{8,0},{16,8},{24,16},{32,24},{40,32},{48,40},{56,48},{64,5... | collective-permute-start | bytes 319496 | tf_op jit(solution)/shard_map/ppermute | solution.py:397
  61.6 1.5 %collective-permute-done.7.from_right = f32[208,128]{1,0:T(8,128)S(1)} collective-permute-done((f32[208,128]{1,0:T(8,128)S(1)}, f32[208,128]{1,0:T(8,128)S(1)}, u32[]{:S(2)}, u32[]{:S(2)}) %collective-permute-start.7) | collective-permute-done | bytes 106528 | tf_op jit(solution)/shard_map/ppermute | solution.py:397
  63.1 7.5 %collective-permute-start.9 = (f32[192,128]{1,0:T(8,128)S(1)}, f32[192,128]{1,0:T(8,128)S(1)}, u32[]{:S(2)}, u32[]{:S(2)}) collective-permute-start(f32[192,128]{1,0:T(8,128)S(1)} %pad_maximum_fusion.2.own), channel_id=1, source_target_pairs={{0,488},{8,496},{16,504},{24,0},{32,8},{40,16},{48,24},{56,32},{64... | collective-permute-start | bytes 294920 | tf_op jit(solution)/shard_map/ppermute | solution.py:397
  70.6 1.9 %collective-permute-start.8 = (f32[192,128]{1,0:T(8,128)S(1)}, f32[192,128]{1,0:T(8,128)S(1)}, u32[]{:S(2)}, u32[]{:S(2)}) collective-permute-start(f32[192,128]{1,0:T(8,128)S(1)} %pad_maximum_fusion.2.own), channel_id=1, source_target_pairs={{0,24},{8,32},{16,40},{24,48},{32,56},{40,64},{48,72},{56,80},{64,... | collective-permute-start | bytes 294920 | tf_op jit(solution)/shard_map/ppermute | solution.py:397
  72.8 6.4 %collective-permute-done.8.left = f32[192,128]{1,0:T(8,128)S(1)} collective-permute-done((f32[192,128]{1,0:T(8,128)S(1)}, f32[192,128]{1,0:T(8,128)S(1)}, u32[]{:S(2)}, u32[]{:S(2)}) %collective-permute-start.8) | collective-permute-done | bytes 98336 | tf_op jit(solution)/shard_map/ppermute | solution.py:397
  79.2 5.0 %shard_map.53 = (f32[48,128]{1,0:T(8,128)S(1)}, f32[18,32,128]{2,1,0:T(8,128)S(1)}, f32[18,32,128]{2,1,0:T(8,128)S(1)}, f32[18,32,128]{2,1,0:T(8,128)S(1)}, f32[...) custom-call(f32[192,128]{1,0:T(8,128)S(1)} %pad_maximum_fusion.2.own, ...), custom_call_target="tpu_custom_call" | custom-call | tf_op jit(solution)/shard_map/pallas_call | solution.py:382
  84.2 6.7 %collective-permute-start.11 = (f32[48,128]{1,0:T(8,128)S(1)}, f32[48,128]{1,0:T(8,128)S(1)}, u32[]{:S(2)}, u32[]{:S(2)}) collective-permute-start(f32[48,128]{1,0:T(8,128)S(1)} %get-tuple-element.36.own3), channel_id=1, source_target_pairs={{0,456},{8,464},{16,472},{24,480},{32,488},{40,496},{48,504},{56,0... | collective-permute-start | bytes 73736 | tf_op jit(solution)/shard_map/ppermute | solution.py:397
  90.9 1.9 %collective-permute-start.10 = (f32[48,128]{1,0:T(8,128)S(1)}, f32[48,128]{1,0:T(8,128)S(1)}, u32[]{:S(2)}, u32[]{:S(2)}) collective-permute-start(f32[48,128]{1,0:T(8,128)S(1)} %get-tuple-element.36.own3), channel_id=1, source_target_pairs={{0,56},{8,64},{16,72},{24,80},{32,88},{40,96},{48,104},{56,112},{6... | collective-permute-start | bytes 73736 | tf_op jit(solution)/shard_map/ppermute | solution.py:397
  92.8 12.4 %collective-permute-done.10.left3 = f32[48,128]{1,0:T(8,128)S(1)} collective-permute-done((f32[48,128]{1,0:T(8,128)S(1)}, f32[48,128]{1,0:T(8,128)S(1)}, u32[]{:S(2)}, u32[]{:S(2)}) %collective-permute-start.10) | collective-permute-done | bytes 24608 | tf_op jit(solution)/shard_map/ppermute | solution.py:397
  105.2 5.2 %shard_map.54 = (f32[8,32,128]{2,1,0:T(8,128)}, f32[8,32,128]{2,1,0:T(8,128)}) custom-call(f32[48,128]{1,0:T(8,128)S(1)} %get-tuple-element.36.own3, f32[48,128]{1,0:T(8,128)S(1)} %collective-permute-done.10.left3, f32[48,128]{1,0:T(8,128)S(1)} %collective-permute-done.11.right3, f32[18,32,128]{2,1,0:T(8,128)S(1)} %get-tuple-element.37.t2x, ...), custom_call_target="tpu_custom_call" | custom-call | tf_op jit(solution)/shard_map/pallas_call | solution.py:382
  (20 shorter events, 3.7 us)
Async XLA Ops:
  0.6 1.0 copy-start.1
  2.4 10.3 %copy-start.2 = (f32[8,32,128]{2,1,0:T(8,128)S(1)}, f32[8,32,128]{2,1,0:T(8,128)}, u32[]{:S(2)}) copy-start(f32[8,32,128]{2,1,0:T(8,128)} %s.3) | copy-start | bytes 393220
  2.4 10.3 %copy-start = (f32[8,32,128]{2,1,0:T(8,128)S(1)}, f32[8,32,128]{2,1,0:T(8,128)}, u32[]{:S(2)}) copy-start(f32[8,32,128]{2,1,0:T(8,128)} %k.3) | copy-start | bytes 393220
  2.4 5.9 %collective-permute-start = (f32[7,32,128]{2,1,0:T(8,128)S(1)}, f32[7,32,128]{2,1,0:T(8,128)S(1)}, u32[]{:S(2)}, u32[]{:S(2)}) collective-permute-start(f32[7,32,128]{2,1,0:T(8,128)S(1)} %pad_maximum_fusion), channel_id=1, source_target_pairs={{0,8},{8,16},{16,24},{24,32},{32,40},{40,48},{48,56},{56,64},{64,7... | collective-permute-start | bytes 344072 | tf_op jit(solution)/shard_map/ppermute | solution.py:392
  6.0 6.7 %collective-permute-start.1 = (f32[7,32,128]{2,1,0:T(8,128)S(1)}, f32[7,32,128]{2,1,0:T(8,128)S(1)}, u32[]{:S(2)}, u32[]{:S(2)}) collective-permute-start(f32[7,32,128]{2,1,0:T(8,128)S(1)} %pad_maximum_fusion.1), channel_id=1, source_target_pairs={{8,0},{16,8},{24,16},{32,24},{40,32},{48,40},{56,48},{64,56},{72,6... | collective-permute-start | bytes 344072 | tf_op jit(solution)/shard_map/ppermute | solution.py:392
  12.7 7.6 %collective-permute-start.2 = (f32[14,8,128]{2,1,0:T(8,128)S(1)}, f32[14,8,128]{2,1,0:T(8,128)S(1)}, u32[]{:S(2)}, u32[]{:S(2)}) collective-permute-start(f32[14,8,128]{2,1,0:T(8,128)S(1)} %get-tuple-element.30), channel_id=1, source_target_pairs={{2,0},{4,2},{6,4},{3,1},{5,3},{7,5},{10,8},{12,10},{14,12},{11,9},... | collective-permute-start | bytes 172040 | tf_op jit(solution)/shard_map/ppermute | solution.py:392
  18.3 6.1 %collective-permute-start.3 = (f32[14,8,128]{2,1,0:T(8,128)S(1)}, f32[14,8,128]{2,1,0:T(8,128)S(1)}, u32[]{:S(2)}, u32[]{:S(2)}) collective-permute-start(f32[14,8,128]{2,1,0:T(8,128)S(1)} %get-tuple-element.31), channel_id=1, source_target_pairs={{0,2},{2,4},{4,6},{1,3},{3,5},{5,7},{8,10},{10,12},{12,14},{9,11},... | collective-permute-start | bytes 172040 | tf_op jit(solution)/shard_map/ppermute | solution.py:392
  33.7 8.3 %collective-permute-start.5 = (f32[4,8,16,128]{3,2,1,0:T(8,128)S(1)}, f32[4,8,16,128]{3,2,1,0:T(8,128)S(1)}, u32[]{:S(2)}, u32[]{:S(2)}) collective-permute-start(f32[4,8,16,128]{3,2,1,0:T(8,128)S(1)} %all_to_all.5.gc), channel_id=1, source_target_pairs={{8,0},{16,8},{24,16},{32,24},{40,32},{48,40},{56,48},{64,56},{72,6... | collective-permute-start | bytes 786440 | tf_op jit(solution)/shard_map/ppermute | solution.py:392
  35.0 8.7 %collective-permute-start.4 = (f32[4,8,16,128]{3,2,1,0:T(8,128)S(1)}, f32[4,8,16,128]{3,2,1,0:T(8,128)S(1)}, u32[]{:S(2)}, u32[]{:S(2)}) collective-permute-start(f32[4,8,16,128]{3,2,1,0:T(8,128)S(1)} %all_to_all.5.gc), channel_id=1, source_target_pairs={{0,8},{8,16},{16,24},{24,32},{32,40},{40,48},{48,56},{56,64},{64,7... | collective-permute-start | bytes 786440 | tf_op jit(solution)/shard_map/ppermute | solution.py:392
  46.1 15.4 %collective-permute-start.6 = (f32[208,128]{1,0:T(8,128)S(1)}, f32[208,128]{1,0:T(8,128)S(1)}, u32[]{:S(2)}, u32[]{:S(2)}) collective-permute-start(f32[208,128]{1,0:T(8,128)S(1)} %get-tuple-element.34), channel_id=1, source_target_pairs={{0,8},{8,16},{16,24},{24,32},{32,40},{40,48},{48,56},{56,64},{64,7... | collective-permute-start | bytes 319496 | tf_op jit(solution)/shard_map/ppermute | solution.py:397
  50.5 12.5 %collective-permute-start.7 = (f32[208,128]{1,0:T(8,128)S(1)}, f32[208,128]{1,0:T(8,128)S(1)}, u32[]{:S(2)}, u32[]{:S(2)}) collective-permute-start(f32[208,128]{1,0:T(8,128)S(1)} %get-tuple-element.35), channel_id=1, source_target_pairs={{0,504},{8,0},{16,8},{24,16},{32,24},{40,32},{48,40},{56,48},{64,5... | collective-permute-start | bytes 319496 | tf_op jit(solution)/shard_map/ppermute | solution.py:397
  63.1 9.7 %collective-permute-start.9 = (f32[192,128]{1,0:T(8,128)S(1)}, f32[192,128]{1,0:T(8,128)S(1)}, u32[]{:S(2)}, u32[]{:S(2)}) collective-permute-start(f32[192,128]{1,0:T(8,128)S(1)} %pad_maximum_fusion.2.own), channel_id=1, source_target_pairs={{0,488},{8,496},{16,504},{24,0},{32,8},{40,16},{48,24},{56,32},{64... | collective-permute-start | bytes 294920 | tf_op jit(solution)/shard_map/ppermute | solution.py:397
  70.6 8.6 %collective-permute-start.8 = (f32[192,128]{1,0:T(8,128)S(1)}, f32[192,128]{1,0:T(8,128)S(1)}, u32[]{:S(2)}, u32[]{:S(2)}) collective-permute-start(f32[192,128]{1,0:T(8,128)S(1)} %pad_maximum_fusion.2.own), channel_id=1, source_target_pairs={{0,24},{8,32},{16,40},{24,48},{32,56},{40,64},{48,72},{56,80},{64,... | collective-permute-start | bytes 294920 | tf_op jit(solution)/shard_map/ppermute | solution.py:397
  84.2 8.7 %collective-permute-start.11 = (f32[48,128]{1,0:T(8,128)S(1)}, f32[48,128]{1,0:T(8,128)S(1)}, u32[]{:S(2)}, u32[]{:S(2)}) collective-permute-start(f32[48,128]{1,0:T(8,128)S(1)} %get-tuple-element.36.own3), channel_id=1, source_target_pairs={{0,456},{8,464},{16,472},{24,480},{32,488},{40,496},{48,504},{56,0... | collective-permute-start | bytes 73736 | tf_op jit(solution)/shard_map/ppermute | solution.py:397
  90.9 14.3 %collective-permute-start.10 = (f32[48,128]{1,0:T(8,128)S(1)}, f32[48,128]{1,0:T(8,128)S(1)}, u32[]{:S(2)}, u32[]{:S(2)}) collective-permute-start(f32[48,128]{1,0:T(8,128)S(1)} %get-tuple-element.36.own3), channel_id=1, source_target_pairs={{0,56},{8,64},{16,72},{24,80},{32,88},{40,96},{48,104},{56,112},{6... | collective-permute-start | bytes 73736 | tf_op jit(solution)/shard_map/ppermute | solution.py:397

commit v2 on v0

v2 whole, which is shorter than its diff:
```python
import jax
import jax.numpy as jnp
from jax import lax
from jax.experimental import pallas as pl
from jax.experimental.pallas import tpu as pltpu
from jax.sharding import PartitionSpec as P

OMEGA = 0.7
COARSE = 8
F32 = jnp.float32


def lanes(like):
    return lax.broadcasted_iota(jnp.int32, like.shape, 1)


def rows(like):
    return lax.broadcasted_iota(jnp.int32, like.shape, 0)


def roll(v, shift, axis):
    return pltpu.roll(v, shift % v.shape[axis], axis)


def bit(v, b):
    return (lanes(v) & b) == 0


def swap(v, b, axis=1):
    at = rows(v) if axis == 0 else lanes(v)
    return jnp.where((at & b) == 0, roll(v, -b, axis), roll(v, b, axis))


def split(p, b, axis=1):
    at = rows(p) if axis == 0 else lanes(p)
    low = (at & b) == 0
    return jnp.where(low, p, roll(p, b, axis)), jnp.where(low, roll(p, -b, axis), p)


def pack2(a, b):
    return jnp.where(bit(a, 1), a, b)


def pack4(a, b, c, d):
    return jnp.where(bit(a, 2), pack2(a, b), pack2(c, d))


def exchange(a, b, w):
    low = bit(a, w)
    return jnp.where(low, a, roll(b, w, 1)), jnp.where(low, roll(a, -w, 1), b)


def pack_coarse(a, b, c, d):
    even = (rows(a) & 1) == 0
    return jnp.where(bit(a, 4), jnp.where(even, a, b), jnp.where(even, c, d))


def unpack_coarse(p):
    left, right = split(p, 4)
    return split(left, 1, 0) + split(right, 1, 0)


def harmonic(a, b, level):
    return 2.0**level * 2.0 * a * b / jnp.maximum(a + b, 0.01)


class Level:
    def __init__(self, level, tx, ty, tz, store, gain):
        self.level = level
        self.tx, self.ty, self.tz, self.store, self.gain = tx, ty, tz, store, gain
        self.w = 2**level

    def y_low(self, v):
        if self.level < 2:
            return roll(v, 1, 0)
        n = self.level - 1
        t = roll(v, n, 0)
        return jnp.where(rows(v) < n, roll(t, 1, 1), t)

    def y_high(self, v):
        if self.level < 2:
            return roll(v, -1, 0)
        n = self.level - 1
        t = roll(v, -n, 0)
        return jnp.where(rows(v) >= 8 - n, roll(t, -1, 1), t)

    def build(self, perm, first, last, origin=None, extent=None):
        for p in range(first, last + 2):
            face = harmonic(perm[p], perm[p - 1], self.level)
            if origin is not None:
                at = origin + p
                face = face * jnp.where((at == 0) | (at == extent), 0.0, 1.0)
            self.tx[p] = face
        for p in range(first, last + 1):
            k = perm[p]
            ty = harmonic(k, self.y_low(k), self.level)
            if self.level >= 2:
                outer = (rows(k) < self.level - 1) & ((lanes(k) & 3) == 0)
                ty = jnp.where(outer, 0.0, ty)
            tz = jnp.where(lanes(k) < self.w, 0.0, harmonic(k, roll(k, self.w, 1), self.level))
            self.ty[p] = ty
            self.tz[p] = tz
            d = (
                self.store[p] + self.tx[p] + self.tx[p + 1] + ty + self.y_high(ty)
                + tz + roll(tz, -self.w, 1)
            )
            self.gain[p] = OMEGA / jnp.maximum(d, 0.01)

    def apply(self, v, first, last, use):
        low = self.tx[first] * (v[first] - v[first - 1])
        for p in range(first, last + 1):
            here = v[p]
            high = self.tx[p + 1] * (v[p + 1] - here)
            fy = self.ty[p] * (here - self.y_low(here))
            fz = self.tz[p] * (here - roll(here, self.w, 1))
            out = (
                self.store[p] * here + (low - high) + (fy - self.y_high(fy))
                + (fz - roll(fz, -self.w, 1))
            )
            use(p, here, out)
            low = high

    def sweep(self, v, source, first, last):
        def use(p, here, out):
            v[p] = here + self.gain[p] * (source[p] - out)

        self.apply(v, first, last, use)

    def first_sweep(self, v, source, first, last):
        for p in range(first, last + 1):
            v[p] = self.gain[p] * source[p]

    def defect(self, r, v, source, first, last):
        def use(p, here, out):
            r[p] = source[p] - out

        self.apply(v, first, last, use)


def restrict(ref, p, count, level):
    half = count // 2
    t = ref[p, pl.ds(0, half, stride=2), :] + ref[p, pl.ds(1, half, stride=2), :]
    t = t + (ref[p + 1, pl.ds(0, half, stride=2), :] + ref[p + 1, pl.ds(1, half, stride=2), :])
    return t + swap(t, 2**level)


def restrict_packed(ref, p):
    t = ref[p] + ref[p + 1]
    t = t + swap(t, 1, 0)
    return t + swap(t, 4)


def doubled(ref, p, e):
    half = e.shape[0]
    ref[p, pl.ds(0, half, stride=2), :] = e
    ref[p, pl.ds(1, half, stride=2), :] = e


def planes_kernel(k, f, s, to_left, to_right):
    for p in range(8):
        to_left[p] = k[p]
        to_right[p] = k[p]
    for p in range(6):
        to_left[8 + p] = f[p]
        to_left[14 + p] = s[p]
        to_right[8 + p] = f[2 + p]
        to_right[14 + p] = s[2 + p]


def window(own, left, right, at, edge):
    for p in range(edge):
        yield 8 - edge + p, left, at + p
    for p in range(8):
        yield 8 + p, own, p
    for p in range(edge):
        yield 16 + p, right, at + p


def halo_planes(k, f, s, xl, xr):
    return (
        tuple(window(k, xl, xr, 0, 8)),
        tuple(window(f, xl, xr, 8, 6)),
        tuple(window(s, xl, xr, 14, 6)),
    )


def rows_kernel(k, f, s, xl, xr, up, down):
    n = 0
    for planes in halo_planes(k, f, s, xl, xr):
        for _, ref, p in planes:
            up[n] = ref[p, pl.ds(24, 8), :]
            down[n] = ref[p, pl.ds(0, 8), :]
            n += 1


def fine_kernel(
    k, f, s, xl, xr, above, below,
    slot, ve, re, tx, ty, tz, st, gain, t1x, t1y, t1z, s1, g1,
    ke, fe, k1, f1, v1, r1,
):
    n = 0
    for target, planes in zip((ke, fe, st), halo_planes(k, f, s, xl, xr)):
        for at, ref, p in planes:
            target[at, pl.ds(0, 32), :] = ref[p]
            target[at, pl.ds(32, 8), :] = above[n]
            target[at, pl.ds(40, 8), :] = below[n]
            n += 1
    op = Level(0, tx, ty, tz, st, gain)
    op.build(ke, 2, 21)
    op.first_sweep(ve, fe, 2, 21)
    op.sweep(ve, fe, 3, 20)
    op.defect(re, ve, fe, 4, 19)
    for q in range(12):
        k1[q] = restrict(ke, 2 * q, 48, 0) * 0.125
        if 1 <= q < 11:
            s1[q] = restrict(st, 2 * q, 48, 0)
        if 2 <= q < 10:
            f1[q] = restrict(re, 2 * q, 48, 0)
    op = Level(1, t1x, t1y, t1z, s1, g1)
    op.build(k1, 1, 10)
    op.first_sweep(v1, f1, 2, 9)
    op.sweep(v1, f1, 3, 8)
    op.defect(r1, v1, f1, 4, 7)
    source = [restrict(r1, 4 + 2 * p, 16, 1) for p in range(2)]
    perm = [restrict(k1, 4 + 2 * p, 16, 1) * 0.125 for p in range(2)]
    store = [restrict(s1, 4 + 2 * p, 16, 1) for p in range(2)]
    tiles = [pack4(*source, *perm), pack4(*store, *store)]
    for ref in (r1, v1):
        for p in (4, 6):
            t = pack2(ref[p, pl.ds(0, 16), :], ref[p + 1, pl.ds(0, 16), :])
            tiles += [t[:8], t[8:]]
    for peer in range(16):
        for i, t in enumerate(tiles):
            slot[peer, i] = t


def ring_kernel(g, to_next, to_prev):
    for x in range(4):
        t = [g[4 * x + j, 0] for j in range(4)]
        e0, o0 = exchange(t[0], t[1], 1)
        e1, o1 = exchange(t[2], t[3], 1)
        f0, k0 = exchange(e0, e1, 2)
        f1, k1 = exchange(o0, o1, 2)
        t = [g[4 * x + j, 1] for j in range(4)]
        e0, o0 = exchange(t[0], t[1], 1)
        e1, o1 = exchange(t[2], t[3], 1)
        s0 = jnp.where(bit(e0, 2), e0, e1)
        s1 = jnp.where(bit(o0, 2), o0, o1)
        for out in (to_next, to_prev):
            for at, v in ((0, f0), (1, f1), (8, k0), (9, k1), (16, s0), (17, s1)):
                out[at + 2 * x] = v
    j = lax.axis_index("gy")
    for out, x, v in ((to_next, 3, 8), (to_prev, 0, 6)):
        for i, t in enumerate(edge_tiles(v)):
            out[24 + i] = g[4 * x + peer_of(j, t[0]), t[1]]


def peer_of(j, step):
    return jnp.clip(j + step, 0, 3)


def edge_tiles(v):
    out = []
    for t in (2, 4, v):
        out += [(0, t), (0, t + 1), (1, t), (-1, t + 1)]
    return out


def coarse_kernel(prev, own, nxt, msg, tx, ty, tz, st, gain, v2, r2, ke, fe):
    for b, ref in enumerate((prev, own, nxt)):
        for p in range(8):
            fe[8 * b + p] = ref[p]
            ke[8 * b + p] = ref[8 + p]
            st[8 * b + p] = ref[16 + p]
    op = Level(2, tx, ty, tz, st, gain)
    z = lax.axis_index("gx") // 4
    op.build(ke, 1, 22, 8 * z - 8, 2 * lax.axis_size("gx"))
    op.first_sweep(v2, fe, 1, 22)
    op.sweep(v2, fe, 2, 21)
    op.defect(r2, v2, fe, 3, 20)
    for i, (ref, scale) in enumerate(((r2, None), (ke, 0.125), (st, None))):
        cells = [restrict_packed(ref, 4 + 2 * c) for c in range(8)]
        if scale is not None:
            cells = [c * scale for c in cells]
        msg[2 * i] = pack_coarse(*cells[:4])
        msg[2 * i + 1] = pack_coarse(*cells[4:])


def up_kernel(
    own3, left3, right3,
    t2x, t2y, t2z, s2, g2, v2, r2,
    t1x, t1y, t1z, s1, g1,
    t0x, t0y, t0z, s0, g0, v0, r0,
    slots, prev, nxt,
    pressure, residual,
    k3, f3, s3, t3x, t3y, t3z, g3, v3, c2, e2, c1, q1, w1, dup, c0,
):
    n = 0
    for ref in (left3, own3, right3):
        for half in range(2):
            for i, target in enumerate((f3, k3, s3)):
                for c, v in enumerate(unpack_coarse(ref[2 * i + half])):
                    target[n + c] = v
            n += 4
    i = lax.axis_index("gx")
    j = lax.axis_index("gy")
    z, x = i // 4, i % 4
    op = Level(3, t3x, t3y, t3z, s3, g3)
    op.build(k3, 1, 22, 4 * z - 10, lax.axis_size("gx"))
    op.first_sweep(v3, f3, 1, 22)
    for m in range(1, COARSE):
        op.sweep(v3, f3, 1 + m, 22 - m)
    for n in range(8, 16):
        e = v3[n]
        c2[2 * n - 12] = e
        c2[2 * n - 11] = e
    op = Level(2, t2x, t2y, t2z, s2, g2)
    op.sweep(c2, r2, 5, 18)
    op.sweep(c2, r2, 6, 17)
    for p in range(6, 18):
        e2[p] = v2[p] + c2[p]
    sub = rows(jnp.zeros((8, 128), F32))
    for p in range(6):
        e = e2[6 + 2 * x + p]
        part = []
        for step in (0, 1, -1):
            t = jnp.where((lanes(e) & 3) == j + step, e, 0.0)
            t = t + swap(t, 1)
            part.append(t + swap(t, 2))
        for n, t in enumerate(part):
            doubled(dup, n, t)
        halo = jnp.where(sub < 4, dup[1, pl.ds(0, 8), :], dup[2, pl.ds(8, 8), :])
        for q in (2 * p, 2 * p + 1):
            c1[q, pl.ds(0, 16), :] = dup[0]
            c1[q, pl.ds(16, 8), :] = halo

    def pairs(get, count):
        out = []
        for n in range(count):
            a, b, c, d = (get(4 * n + m) for m in range(4))
            out.append(split(jnp.concatenate([a, b, jnp.where(sub < 4, c, d)], axis=0), 1))
        return out

    def beside(step, v, outer):
        at = 4 * jnp.clip(x + step, 0, 3)
        tiles = edge_tiles(v)
        inside = (x + step >= 0) & (x + step < 4)

        def get(n):
            y, t = tiles[n]
            return jnp.where(inside, slots[at + peer_of(j, y), t], outer[24 + n])

        return pairs(get, 3)

    def own(n):
        y, t = (edge_tiles(6) + edge_tiles(8)[8:])[n]
        return slots[4 * x + peer_of(j, y), t]

    (_, a), (b, c), (d, e) = beside(-1, 8, prev)
    q1[1], q1[2], q1[3], w1[2], w1[3] = a, b, c, d, e
    (a, b), (c, _), (d, e) = beside(1, 6, nxt)
    q1[8], q1[9], q1[10], w1[8], w1[9] = a, b, c, d, e
    (a, b), (c, d), (e, f), (g, h) = pairs(own, 4)
    q1[4], q1[5], q1[6], q1[7] = a, b, c, d
    w1[4], w1[5], w1[6], w1[7] = e, f, g, h
    op = Level(1, t1x, t1y, t1z, s1, g1)
    op.sweep(c1, q1, 1, 10)
    op.sweep(c1, q1, 2, 9)
    for q in range(2, 10):
        e = w1[q] + c1[q]
        doubled(c0, 2 * q, e)
        doubled(c0, 2 * q + 1, e)
    op = Level(0, t0x, t0y, t0z, s0, g0)
    op.sweep(c0, r0, 6, 17)
    op.sweep(c0, r0, 7, 16)

    def use(p, here, out):
        pressure[p - 8] = v0[p, pl.ds(0, 32), :] + here[:32]
        residual[p - 8] = r0[p, pl.ds(0, 32), :] - out[:32]

    op.apply(c0, 8, 15, use)


def call(kernel, outs, scratch, args):
    return pl.pallas_call(
        kernel,
        out_shape=[jax.ShapeDtypeStruct(s, F32) for s in outs],
        scratch_shapes=[pltpu.VMEM(s, F32) for s in scratch],
        compiler_params=pltpu.CompilerParams(vmem_limit_bytes=32 * 1024 * 1024),
    )(*args)


def shifted(x, axis, k):
    n = lax.axis_size(axis)
    return lax.ppermute(x, axis, [(i, i + k) for i in range(n) if 0 <= i + k < n])


def turned(x, axis, k):
    n = lax.axis_size(axis)
    return lax.ppermute(x, axis, [(i, (i + k) % n) for i in range(n)])


def body(permeability, storage, source_term):
    k, s, f = permeability, storage, source_term
    to_left, to_right = call(planes_kernel, [(20, 32, 128)] * 2, [], (k, f, s))
    xl = shifted(to_right, "gx", 1)
    xr = shifted(to_left, "gx", -1)
    up, down = call(rows_kernel, [(64, 8, 128)] * 2, [], (k, f, s, xl, xr))
    below = shifted(up, "gy", 1)
    above = shifted(down, "gy", -1)
    fine, mid = (24, 48, 128), (12, 24, 128)
    slot, v0, r0, t0x, t0y, t0z, s0, g0, t1x, t1y, t1z, s1, g1 = call(
        fine_kernel,
        [(16, 10, 8, 128)] + [fine] * 7 + [mid] * 5,
        [fine] * 2 + [mid] * 4,
        (k, f, s, xl, xr, above, below),
    )
    n = lax.axis_size("gx") * lax.axis_size("gy")
    groups = [[16 * a + b for b in range(16)] for a in range(n // 16)]
    slots = lax.all_to_all(slot, ("gx", "gy"), 0, 0, axis_index_groups=groups)
    to_next, to_prev = call(ring_kernel, [(36, 8, 128)] * 2, [], (slots,))
    prev, nxt = turned(to_next, "gx", 4), turned(to_prev, "gx", -4)
    low = (24, 8, 128)
    msg3, t2x, t2y, t2z, s2, g2, v2, r2 = call(
        coarse_kernel, [(6, 8, 128)] + [low] * 7, [low] * 2, (prev, to_next, nxt)
    )
    left3, right3 = turned(msg3, "gx", 8), turned(msg3, "gx", -8)
    return tuple(call(
        up_kernel,
        [(8, 32, 128)] * 2,
        [low] * 10 + [mid] * 3 + [(3, 16, 128), fine],
        (
            msg3, left3, right3,
            t2x, t2y, t2z, s2, g2, v2, r2,
            t1x, t1y, t1z, s1, g1,
            t0x, t0y, t0z, s0, g0, v0, r0,
            slots, prev, nxt,
        ),
    ))


def solution(mesh):
    spec = P(("ma", "gx"), "gy", None)
    return jax.shard_map(
        body, mesh=mesh, in_specs=(spec,) * 3, out_specs=(spec,) * 2, check_vma=False
    )
```

time: 494 us -> 88.8 us (0.18)
  the two profiles are of different devices: /device:TPU:102 before, /device:TPU:2 now
where the time goes in v2:
time: 88.8 us; the launch traced here: 88.4 us
  starting transfers between devices  32.6 us (37%)
  waiting for transfers between devices  21.5 us (24%)
  blocking collectives  19.7 us (22%)
  Pallas kernels  11.3 us (13%)
  local copies, waits for them, and re-layouts  2.7 us (3%)
    all_to_all x1, blocking collectives, body(): slots = lax.all_to_all(slot, ('gx', 'gy'), 0, 0, axis_index_groups=groups)  19.7 us
    ppermute x4, starting transfers between devices, turned(): return lax.ppermute(x, axis, [(i, (i + k) % n) for i in range(n)])  17.6 us
    ppermute x4, starting transfers between devices, shifted(): lax.ppermute(x, axis, [(i, i + k) for i in range(n) if 0 <= i + k < n])  15 us
    ppermute x4, waiting for transfers between devices, turned(): return lax.ppermute(x, axis, [(i, (i + k) % n) for i in range(n)])  12.1 us
    pallas_call x6, Pallas kernels, call(): pl.pallas_call(kernel, out_shape=[jax.ShapeDtypeStruct(s, F32) for s in o...  11.3 us
    ppermute x4, waiting for transfers between devices, shifted(): lax.ppermute(x, axis, [(i, i + k) for i in range(n) if 0 <= i + k < n])  9.39 us
    unnamed x6, local copies, waits for them, and re-layouts  2.7 us
  transfers between devices with their start and end apart: 8, of which 7 were waited for; matrix products, arithmetic and copies ran while one was open for 0% of the time, Pallas kernels for 0%

profile of v2, /device:TPU:2, one launch (start us, length us, event | category | flops | bytes accessed | tf_op | source)
XLA Modules:
  0.0 88.4 jit_solution(5011323030824408625)
XLA Ops:
  0.6 0.9 %copy-done = f32[8,32,128]{2,1,0:T(8,128)S(1)} copy-done((f32[8,32,128]{2,1,0:T(8,128)S(1)}, f32[8,32,128]{2,1,0:T(8,128)}, u32[]{:S(2)}) %copy-start) | copy-done | bytes 131096
  1.5 0.9 %copy-done.1 = f32[8,32,128]{2,1,0:T(8,128)S(1)} copy-done((f32[8,32,128]{2,1,0:T(8,128)S(1)}, f32[8,32,128]{2,1,0:T(8,128)}, u32[]{:S(2)}) %copy-start.1) | copy-done | bytes 131096
  2.4 0.9 %copy-done.2 = f32[8,32,128]{2,1,0:T(8,128)S(1)} copy-done((f32[8,32,128]{2,1,0:T(8,128)S(1)}, f32[8,32,128]{2,1,0:T(8,128)}, u32[]{:S(2)}) %copy-start.2) | copy-done | bytes 131096
  3.4 3.4 %collective-permute-start = (f32[20,32,128]{2,1,0:T(8,128)S(1)}, f32[20,32,128]{2,1,0:T(8,128)S(1)}, u32[]{:S(2)}, u32[]{:S(2)}) collective-permute-start(f32[20,32,128]{2,1,0:T(8,128)S(1)} %get-tuple-element.29), channel_id=1, source_target_pairs={{0,8},{8,16},{16,24},{24,32},{32,40},{40,48},{48,56},{56,64},{64,7... | collective-permute-start | bytes 983048 | tf_op jit(solution)/shard_map/ppermute | solution.py:395
  6.8 5.7 %collective-permute-start.1 = (f32[20,32,128]{2,1,0:T(8,128)S(1)}, f32[20,32,128]{2,1,0:T(8,128)S(1)}, u32[]{:S(2)}, u32[]{:S(2)}) collective-permute-start(f32[20,32,128]{2,1,0:T(8,128)S(1)} %get-tuple-element.30), channel_id=1, source_target_pairs={{8,0},{16,8},{24,16},{32,24},{40,32},{48,40},{56,48},{64,56},{72,6... | collective-permute-start | bytes 983048 | tf_op jit(solution)/shard_map/ppermute | solution.py:395
  12.5 3.1 %collective-permute-done.xl = f32[20,32,128]{2,1,0:T(8,128)S(1)} collective-permute-done((f32[20,32,128]{2,1,0:T(8,128)S(1)}, f32[20,32,128]{2,1,0:T(8,128)S(1)}, u32[]{:S(2)}, u32[]{:S(2)}) %collective-permute-start) | collective-permute-done | bytes 327712 | tf_op jit(solution)/shard_map/ppermute | solution.py:395
  15.6 2.2 %collective-permute-done.1.xr = f32[20,32,128]{2,1,0:T(8,128)S(1)} collective-permute-done((f32[20,32,128]{2,1,0:T(8,128)S(1)}, f32[20,32,128]{2,1,0:T(8,128)S(1)}, u32[]{:S(2)}, u32[]{:S(2)}) %collective-permute-start.1) | collective-permute-done | bytes 327712 | tf_op jit(solution)/shard_map/ppermute | solution.py:395
  17.9 1.3 %collective-permute-start.2 = (f32[64,8,128]{2,1,0:T(8,128)S(1)}, f32[64,8,128]{2,1,0:T(8,128)S(1)}, u32[]{:S(2)}, u32[]{:S(2)}) collective-permute-start(f32[64,8,128]{2,1,0:T(8,128)S(1)} %get-tuple-element.31), channel_id=1, source_target_pairs={{2,0},{4,2},{6,4},{3,1},{5,3},{7,5},{10,8},{12,10},{14,12},{11,9},... | collective-permute-start | bytes 786440 | tf_op jit(solution)/shard_map/ppermute | solution.py:395
  19.2 4.6 %collective-permute-start.3 = (f32[64,8,128]{2,1,0:T(8,128)S(1)}, f32[64,8,128]{2,1,0:T(8,128)S(1)}, u32[]{:S(2)}, u32[]{:S(2)}) collective-permute-start(f32[64,8,128]{2,1,0:T(8,128)S(1)} %get-tuple-element.32), channel_id=1, source_target_pairs={{0,2},{2,4},{4,6},{1,3},{3,5},{5,7},{8,10},{10,12},{12,14},{9,11},... | collective-permute-start | bytes 786440 | tf_op jit(solution)/shard_map/ppermute | solution.py:395
  23.8 2.9 %collective-permute-done.2.above = f32[64,8,128]{2,1,0:T(8,128)S(1)} collective-permute-done((f32[64,8,128]{2,1,0:T(8,128)S(1)}, f32[64,8,128]{2,1,0:T(8,128)S(1)}, u32[]{:S(2)}, u32[]{:S(2)}) %collective-permute-start.2) | collective-permute-done | bytes 262176 | tf_op jit(solution)/shard_map/ppermute | solution.py:395
  26.7 1.2 %collective-permute-done.3.below = f32[64,8,128]{2,1,0:T(8,128)S(1)} collective-permute-done((f32[64,8,128]{2,1,0:T(8,128)S(1)}, f32[64,8,128]{2,1,0:T(8,128)S(1)}, u32[]{:S(2)}, u32[]{:S(2)}) %collective-permute-start.3) | collective-permute-done | bytes 262176 | tf_op jit(solution)/shard_map/ppermute | solution.py:395
  27.8 4.5 %shard_map.52 = (f32[16,10,8,128]{3,2,1,0:T(8,128)S(1)}, f32[24,48,128]{2,1,0:T(8,128)S(1)}, f32[24,48,128]{2,1,0:T(8,128)S(1)}, f32[24,48,128]{2,1,0:T(8,128)S(...) custom-call(f32[8,32,128]{2,1,0:T(8,128)S(1)} %copy-done, ...), custom_call_target="tpu_custom_call" | custom-call | tf_op jit(solution)/shard_map/pallas_call | solution.py:385
  32.3 19.7 %all_to_all.5.g.slots = f32[16,10,8,128]{3,2,1,0:T(8,128)S(1)} all-to-all(f32[16,10,8,128]{3,2,1,0:T(8,128)S(1)} %get-tuple-element.33), channel_id=1, replica_groups={{0,2,4,6,8,10,12,14,16,18,20,22,24,26,28,30},{32,34,36,38,40,42,44,46,4..., dimensions={0} | all-to-all | bytes 1310720 | tf_op jit(solution)/shard_map/all_to_all | solution.py:420
  52.0 0.2 shard_map.53
  52.1 8.9 %collective-permute-start.5 = (f32[36,8,128]{2,1,0:T(8,128)S(1)}, f32[36,8,128]{2,1,0:T(8,128)S(1)}, u32[]{:S(2)}, u32[]{:S(2)}) collective-permute-start(f32[36,8,128]{2,1,0:T(8,128)S(1)} %get-tuple-element.35), channel_id=1, source_target_pairs={{0,480},{8,488},{16,496},{24,504},{32,0},{40,8},{48,16},{56,24},{6... | collective-permute-start | bytes 442376 | tf_op jit(solution)/shard_map/ppermute | solution.py:400
  61.1 1.9 %collective-permute-start.4 = (f32[36,8,128]{2,1,0:T(8,128)S(1)}, f32[36,8,128]{2,1,0:T(8,128)S(1)}, u32[]{:S(2)}, u32[]{:S(2)}) collective-permute-start(f32[36,8,128]{2,1,0:T(8,128)S(1)} %get-tuple-element.34.own), channel_id=1, source_target_pairs={{0,32},{8,40},{16,48},{24,56},{32,64},{40,72},{48,80},{56,88},{64,... | collective-permute-start | bytes 442376 | tf_op jit(solution)/shard_map/ppermute | solution.py:400
  63.0 0.7 collective-permute-done.5.nxt
  63.7 5.6 %collective-permute-done.4.prev = f32[36,8,128]{2,1,0:T(8,128)S(1)} collective-permute-done((f32[36,8,128]{2,1,0:T(8,128)S(1)}, f32[36,8,128]{2,1,0:T(8,128)S(1)}, u32[]{:S(2)}, u32[]{:S(2)}) %collective-permute-start.4) | collective-permute-done | bytes 147488 | tf_op jit(solution)/shard_map/ppermute | solution.py:400
  69.3 0.8 shard_map.54
  70.2 3.7 %collective-permute-start.7 = (f32[6,8,128]{2,1,0:T(8,128)S(1)}, f32[6,8,128]{2,1,0:T(8,128)S(1)}, u32[]{:S(2)}, u32[]{:S(2)}) collective-permute-start(f32[6,8,128]{2,1,0:T(8,128)S(1)} %get-tuple-element.36.own3), channel_id=1, source_target_pairs={{0,448},{8,456},{16,464},{24,472},{32,480},{40,488},{48,496},{56,5... | collective-permute-start | bytes 73736 | tf_op jit(solution)/shard_map/ppermute | solution.py:400
  73.9 3.0 %collective-permute-start.6 = (f32[6,8,128]{2,1,0:T(8,128)S(1)}, f32[6,8,128]{2,1,0:T(8,128)S(1)}, u32[]{:S(2)}, u32[]{:S(2)}) collective-permute-start(f32[6,8,128]{2,1,0:T(8,128)S(1)} %get-tuple-element.36.own3), channel_id=1, source_target_pairs={{0,64},{8,72},{16,80},{24,88},{32,96},{40,104},{48,112},{56,120},{... | collective-permute-start | bytes 73736 | tf_op jit(solution)/shard_map/ppermute | solution.py:400
  76.9 0.0 collective-permute-done.7.right3
  76.9 5.8 %collective-permute-done.6.left3 = f32[6,8,128]{2,1,0:T(8,128)S(1)} collective-permute-done((f32[6,8,128]{2,1,0:T(8,128)S(1)}, f32[6,8,128]{2,1,0:T(8,128)S(1)}, u32[]{:S(2)}, u32[]{:S(2)}) %collective-permute-start.6) | collective-permute-done | bytes 24608 | tf_op jit(solution)/shard_map/ppermute | solution.py:400
  82.7 5.7 %shard_map.55 = (f32[8,32,128]{2,1,0:T(8,128)}, f32[8,32,128]{2,1,0:T(8,128)}) custom-call(f32[6,8,128]{2,1,0:T(8,128)S(1)} %get-tuple-element.36.own3, f32[6,8,128]{2,1,0:T(8,128)S(1)} %collective-permute-done.6.left3, f32[6,8,128]{2,1,0:T(8,128)S(1)} %collective-permute-done.7.right3, f32[24,8,128]{2,1,0:T(8,128)S(1)} %get-tuple-element.37.t2x, ...), custom_call_target="tpu_custom_call" | custom-call | tf_op jit(solution)/shard_map/pallas_call | solution.py:385
  (5 shorter events, 0.1 us)
Async XLA Ops:
  0.6 0.9 %copy-start = (f32[8,32,128]{2,1,0:T(8,128)S(1)}, f32[8,32,128]{2,1,0:T(8,128)}, u32[]{:S(2)}) copy-start(f32[8,32,128]{2,1,0:T(8,128)} %k.5) | copy-start | bytes 393220
  1.5 0.9 %copy-start.1 = (f32[8,32,128]{2,1,0:T(8,128)S(1)}, f32[8,32,128]{2,1,0:T(8,128)}, u32[]{:S(2)}) copy-start(f32[8,32,128]{2,1,0:T(8,128)} %f.5) | copy-start | bytes 393220
  2.4 0.9 %copy-start.2 = (f32[8,32,128]{2,1,0:T(8,128)S(1)}, f32[8,32,128]{2,1,0:T(8,128)}, u32[]{:S(2)}) copy-start(f32[8,32,128]{2,1,0:T(8,128)} %s.5) | copy-start | bytes 393220
  3.4 12.2 %collective-permute-start = (f32[20,32,128]{2,1,0:T(8,128)S(1)}, f32[20,32,128]{2,1,0:T(8,128)S(1)}, u32[]{:S(2)}, u32[]{:S(2)}) collective-permute-start(f32[20,32,128]{2,1,0:T(8,128)S(1)} %get-tuple-element.29), channel_id=1, source_target_pairs={{0,8},{8,16},{16,24},{24,32},{32,40},{40,48},{48,56},{56,64},{64,7... | collective-permute-start | bytes 983048 | tf_op jit(solution)/shard_map/ppermute | solution.py:395
  6.8 11.1 %collective-permute-start.1 = (f32[20,32,128]{2,1,0:T(8,128)S(1)}, f32[20,32,128]{2,1,0:T(8,128)S(1)}, u32[]{:S(2)}, u32[]{:S(2)}) collective-permute-start(f32[20,32,128]{2,1,0:T(8,128)S(1)} %get-tuple-element.30), channel_id=1, source_target_pairs={{8,0},{16,8},{24,16},{32,24},{40,32},{48,40},{56,48},{64,56},{72,6... | collective-permute-start | bytes 983048 | tf_op jit(solution)/shard_map/ppermute | solution.py:395
  17.9 8.7 %collective-permute-start.2 = (f32[64,8,128]{2,1,0:T(8,128)S(1)}, f32[64,8,128]{2,1,0:T(8,128)S(1)}, u32[]{:S(2)}, u32[]{:S(2)}) collective-permute-start(f32[64,8,128]{2,1,0:T(8,128)S(1)} %get-tuple-element.31), channel_id=1, source_target_pairs={{2,0},{4,2},{6,4},{3,1},{5,3},{7,5},{10,8},{12,10},{14,12},{11,9},... | collective-permute-start | bytes 786440 | tf_op jit(solution)/shard_map/ppermute | solution.py:395
  19.2 8.6 %collective-permute-start.3 = (f32[64,8,128]{2,1,0:T(8,128)S(1)}, f32[64,8,128]{2,1,0:T(8,128)S(1)}, u32[]{:S(2)}, u32[]{:S(2)}) collective-permute-start(f32[64,8,128]{2,1,0:T(8,128)S(1)} %get-tuple-element.32), channel_id=1, source_target_pairs={{0,2},{2,4},{4,6},{1,3},{3,5},{5,7},{8,10},{10,12},{12,14},{9,11},... | collective-permute-start | bytes 786440 | tf_op jit(solution)/shard_map/ppermute | solution.py:395
  52.1 11.6 %collective-permute-start.5 = (f32[36,8,128]{2,1,0:T(8,128)S(1)}, f32[36,8,128]{2,1,0:T(8,128)S(1)}, u32[]{:S(2)}, u32[]{:S(2)}) collective-permute-start(f32[36,8,128]{2,1,0:T(8,128)S(1)} %get-tuple-element.35), channel_id=1, source_target_pairs={{0,480},{8,488},{16,496},{24,504},{32,0},{40,8},{48,16},{56,24},{6... | collective-permute-start | bytes 442376 | tf_op jit(solution)/shard_map/ppermute | solution.py:400
  61.1 8.2 %collective-permute-start.4 = (f32[36,8,128]{2,1,0:T(8,128)S(1)}, f32[36,8,128]{2,1,0:T(8,128)S(1)}, u32[]{:S(2)}, u32[]{:S(2)}) collective-permute-start(f32[36,8,128]{2,1,0:T(8,128)S(1)} %get-tuple-element.34.own), channel_id=1, source_target_pairs={{0,32},{8,40},{16,48},{24,56},{32,64},{40,72},{48,80},{56,88},{64,... | collective-permute-start | bytes 442376 | tf_op jit(solution)/shard_map/ppermute | solution.py:400
  70.2 6.8 %collective-permute-start.7 = (f32[6,8,128]{2,1,0:T(8,128)S(1)}, f32[6,8,128]{2,1,0:T(8,128)S(1)}, u32[]{:S(2)}, u32[]{:S(2)}) collective-permute-start(f32[6,8,128]{2,1,0:T(8,128)S(1)} %get-tuple-element.36.own3), channel_id=1, source_target_pairs={{0,448},{8,456},{16,464},{24,472},{32,480},{40,488},{48,496},{56,5... | collective-permute-start | bytes 73736 | tf_op jit(solution)/shard_map/ppermute | solution.py:400
  73.9 8.8 %collective-permute-start.6 = (f32[6,8,128]{2,1,0:T(8,128)S(1)}, f32[6,8,128]{2,1,0:T(8,128)S(1)}, u32[]{:S(2)}, u32[]{:S(2)}) collective-permute-start(f32[6,8,128]{2,1,0:T(8,128)S(1)} %get-tuple-element.36.own3), channel_id=1, source_target_pairs={{0,64},{8,72},{16,80},{24,88},{32,96},{40,104},{48,112},{56,120},{... | collective-permute-start | bytes 73736 | tf_op jit(solution)/shard_map/ppermute | solution.py:400

commit v3 on v2

--- a/solution.py
+++ b/solution.py
@@ -65,9 +65,10 @@
 
 
 class Level:
-    def __init__(self, level, tx, ty, tz, store, gain):
+    def __init__(self, level, tx, ty, tz, tzh, store, gain, tyh=None):
         self.level = level
-        self.tx, self.ty, self.tz, self.store, self.gain = tx, ty, tz, store, gain
+        self.tx, self.ty, self.tz, self.tzh = tx, ty, tz, tzh
+        self.store, self.gain, self.tyh = store, gain, tyh
         self.w = 2**level
 
     def y_low(self, v):
@@ -85,25 +86,27 @@
         return jnp.where(rows(v) >= 8 - n, roll(t, -1, 1), t)
 
     def build(self, perm, first, last, origin=None, extent=None):
+        level, w, n = self.level, self.w, self.level - 1
         for p in range(first, last + 2):
-            face = harmonic(perm[p], perm[p - 1], self.level)
+            face = harmonic(perm[p], perm[p - 1], level)
             if origin is not None:
                 at = origin + p
                 face = face * jnp.where((at == 0) | (at == extent), 0.0, 1.0)
             self.tx[p] = face
         for p in range(first, last + 1):
             k = perm[p]
-            ty = harmonic(k, self.y_low(k), self.level)
-            if self.level >= 2:
-                outer = (rows(k) < self.level - 1) & ((lanes(k) & 3) == 0)
-                ty = jnp.where(outer, 0.0, ty)
-            tz = jnp.where(lanes(k) < self.w, 0.0, harmonic(k, roll(k, self.w, 1), self.level))
-            self.ty[p] = ty
-            self.tz[p] = tz
-            d = (
-                self.store[p] + self.tx[p] + self.tx[p + 1] + ty + self.y_high(ty)
-                + tz + roll(tz, -self.w, 1)
-            )
+            ty = harmonic(k, self.y_low(k), level)
+            if level < 2:
+                tyh = roll(ty, -1, 0)
+            else:
+                tyh = harmonic(k, self.y_high(k), level)
+                ty = jnp.where((rows(k) < n) & ((lanes(k) & 3) == 0), 0.0, ty)
+                tyh = jnp.where((rows(k) >= 8 - n) & ((lanes(k) & 3) == 3), 0.0, tyh)
+                self.tyh[p] = tyh
+            tz = jnp.where(lanes(k) < w, 0.0, harmonic(k, roll(k, w, 1), level))
+            tzh = jnp.where(lanes(k) >= 128 - w, 0.0, harmonic(k, roll(k, -w, 1), level))
+            self.ty[p], self.tz[p], self.tzh[p] = ty, tz, tzh
+            d = self.store[p] + self.tx[p] + self.tx[p + 1] + ty + tyh + tz + tzh
             self.gain[p] = OMEGA / jnp.maximum(d, 0.01)
 
     def apply(self, v, first, last, use):
@@ -112,12 +115,13 @@
             here = v[p]
             high = self.tx[p + 1] * (v[p + 1] - here)
             fy = self.ty[p] * (here - self.y_low(here))
-            fz = self.tz[p] * (here - roll(here, self.w, 1))
-            out = (
-                self.store[p] * here + (low - high) + (fy - self.y_high(fy))
-                + (fz - roll(fz, -self.w, 1))
-            )
-            use(p, here, out)
+            if self.level < 2:
+                y = fy - self.y_high(fy)
+            else:
+                y = fy + self.tyh[p] * (here - self.y_high(here))
+            z = self.tz[p] * (here - roll(here, self.w, 1))
+            z = z + self.tzh[p] * (here - roll(here, -self.w, 1))
+            use(p, here, self.store[p] * here + (low - high) + y + z)
             low = high
 
     def sweep(self, v, source, first, last):
@@ -156,15 +160,24 @@
     ref[p, pl.ds(1, half, stride=2), :] = e
 
 
-def planes_kernel(k, f, s, to_left, to_right):
+def planes_kernel(k, f, s, to_left, to_right, kv, fv, sv, sems):
+    copies = [
+        pltpu.make_async_copy(src.at[pl.ds(4 * h, 4)], dst.at[pl.ds(4 * h, 4)], sems.at[2 * i + h])
+        for i, (src, dst) in enumerate(((k, kv), (f, fv), (s, sv)))
+        for h in range(2)
+    ]
+    for c in copies:
+        c.start()
+    for c in copies:
+        c.wait()
     for p in range(8):
-        to_left[p] = k[p]
-        to_right[p] = k[p]
+        to_left[p] = kv[p]
+        to_right[p] = kv[p]
     for p in range(6):
-        to_left[8 + p] = f[p]
-        to_left[14 + p] = s[p]
-        to_right[8 + p] = f[2 + p]
-        to_right[14 + p] = s[2 + p]
+        to_left[8 + p] = fv[p]
+        to_left[14 + p] = sv[p]
+        to_right[8 + p] = fv[2 + p]
+        to_right[14 + p] = sv[2 + p]
 
 
 def window(own, left, right, at, edge):
@@ -195,7 +208,7 @@
 
 def fine_kernel(
     k, f, s, xl, xr, above, below,
-    slot, ve, re, tx, ty, tz, st, gain, t1x, t1y, t1z, s1, g1,
+    slot, ve, re, tx, ty, tz, tzh, st, gain, t1x, t1y, t1z, t1h, s1, g1,
     ke, fe, k1, f1, v1, r1,
 ):
     n = 0
@@ -205,7 +218,7 @@
             target[at, pl.ds(32, 8), :] = above[n]
             target[at, pl.ds(40, 8), :] = below[n]
             n += 1
-    op = Level(0, tx, ty, tz, st, gain)
+    op = Level(0, tx, ty, tz, tzh, st, gain)
     op.build(ke, 2, 21)
     op.first_sweep(ve, fe, 2, 21)
     op.sweep(ve, fe, 3, 20)
@@ -216,7 +229,7 @@
             s1[q] = restrict(st, 2 * q, 48, 0)
         if 2 <= q < 10:
             f1[q] = restrict(re, 2 * q, 48, 0)
-    op = Level(1, t1x, t1y, t1z, s1, g1)
+    op = Level(1, t1x, t1y, t1z, t1h, s1, g1)
     op.build(k1, 1, 10)
     op.first_sweep(v1, f1, 2, 9)
     op.sweep(v1, f1, 3, 8)
@@ -266,13 +279,15 @@
     return out
 
 
-def coarse_kernel(prev, own, nxt, msg, tx, ty, tz, st, gain, v2, r2, ke, fe):
+def coarse_kernel(
+    prev, own, nxt, msg, tx, ty, tyh, tz, tzh, st, gain, v2, r2, ke, fe
+):
     for b, ref in enumerate((prev, own, nxt)):
         for p in range(8):
             fe[8 * b + p] = ref[p]
             ke[8 * b + p] = ref[8 + p]
             st[8 * b + p] = ref[16 + p]
-    op = Level(2, tx, ty, tz, st, gain)
+    op = Level(2, tx, ty, tz, tzh, st, gain, tyh)
     z = lax.axis_index("gx") // 4
     op.build(ke, 1, 22, 8 * z - 8, 2 * lax.axis_size("gx"))
     op.first_sweep(v2, fe, 1, 22)
@@ -288,12 +303,12 @@
 
 def up_kernel(
     own3, left3, right3,
-    t2x, t2y, t2z, s2, g2, v2, r2,
-    t1x, t1y, t1z, s1, g1,
-    t0x, t0y, t0z, s0, g0, v0, r0,
+    t2x, t2y, t2yh, t2z, t2h, s2, g2, v2, r2,
+    t1x, t1y, t1z, t1h, s1, g1,
+    t0x, t0y, t0z, t0h, s0, g0, v0, r0,
     slots, prev, nxt,
     pressure, residual,
-    k3, f3, s3, t3x, t3y, t3z, g3, v3, c2, e2, c1, q1, w1, dup, c0,
+    k3, f3, s3, t3x, t3y, t3yh, t3z, t3h, g3, v3, c2, e2, c1, q1, w1, dup, c0,
 ):
     n = 0
     for ref in (left3, own3, right3):
@@ -305,7 +320,7 @@
     i = lax.axis_index("gx")
     j = lax.axis_index("gy")
     z, x = i // 4, i % 4
-    op = Level(3, t3x, t3y, t3z, s3, g3)
+    op = Level(3, t3x, t3y, t3z, t3h, s3, g3, t3yh)
     op.build(k3, 1, 22, 4 * z - 10, lax.axis_size("gx"))
     op.first_sweep(v3, f3, 1, 22)
     for m in range(1, COARSE):
@@ -314,7 +329,7 @@
         e = v3[n]
         c2[2 * n - 12] = e
         c2[2 * n - 11] = e
-    op = Level(2, t2x, t2y, t2z, s2, g2)
+    op = Level(2, t2x, t2y, t2z, t2h, s2, g2, t2yh)
     op.sweep(c2, r2, 5, 18)
     op.sweep(c2, r2, 6, 17)
     for p in range(6, 18):
@@ -363,14 +378,14 @@
     (a, b), (c, d), (e, f), (g, h) = pairs(own, 4)
     q1[4], q1[5], q1[6], q1[7] = a, b, c, d
     w1[4], w1[5], w1[6], w1[7] = e, f, g, h
-    op = Level(1, t1x, t1y, t1z, s1, g1)
+    op = Level(1, t1x, t1y, t1z, t1h, s1, g1)
     op.sweep(c1, q1, 1, 10)
     op.sweep(c1, q1, 2, 9)
     for q in range(2, 10):
         e = w1[q] + c1[q]
         doubled(c0, 2 * q, e)
         doubled(c0, 2 * q + 1, e)
-    op = Level(0, t0x, t0y, t0z, s0, g0)
+    op = Level(0, t0x, t0y, t0z, t0h, s0, g0)
     op.sweep(c0, r0, 6, 17)
     op.sweep(c0, r0, 7, 16)
 
@@ -402,16 +417,23 @@
 
 def body(permeability, storage, source_term):
     k, s, f = permeability, storage, source_term
-    to_left, to_right = call(planes_kernel, [(20, 32, 128)] * 2, [], (k, f, s))
+    to_left, to_right, k, f, s = pl.pallas_call(
+        planes_kernel,
+        out_shape=[
+            jax.ShapeDtypeStruct((n, 32, 128), F32) for n in (20, 20, 8, 8, 8)
+        ],
+        in_specs=[pl.BlockSpec(memory_space=pl.ANY)] * 3,
+        scratch_shapes=[pltpu.SemaphoreType.DMA((6,))],
+    )(k, f, s)
     xl = shifted(to_right, "gx", 1)
     xr = shifted(to_left, "gx", -1)
     up, down = call(rows_kernel, [(64, 8, 128)] * 2, [], (k, f, s, xl, xr))
     below = shifted(up, "gy", 1)
     above = shifted(down, "gy", -1)
     fine, mid = (24, 48, 128), (12, 24, 128)
-    slot, v0, r0, t0x, t0y, t0z, s0, g0, t1x, t1y, t1z, s1, g1 = call(
+    slot, v0, r0, t0x, t0y, t0z, t0h, s0, g0, t1x, t1y, t1z, t1h, s1, g1 = call(
         fine_kernel,
-        [(16, 10, 8, 128)] + [fine] * 7 + [mid] * 5,
+        [(16, 10, 8, 128)] + [fine] * 8 + [mid] * 6,
         [fine] * 2 + [mid] * 4,
         (k, f, s, xl, xr, above, below),
     )
@@ -421,19 +443,19 @@
     to_next, to_prev = call(ring_kernel, [(36, 8, 128)] * 2, [], (slots,))
     prev, nxt = turned(to_next, "gx", 4), turned(to_prev, "gx", -4)
     low = (24, 8, 128)
-    msg3, t2x, t2y, t2z, s2, g2, v2, r2 = call(
-        coarse_kernel, [(6, 8, 128)] + [low] * 7, [low] * 2, (prev, to_next, nxt)
+    msg3, t2x, t2y, t2yh, t2z, t2h, s2, g2, v2, r2 = call(
+        coarse_kernel, [(6, 8, 128)] + [low] * 9, [low] * 2, (prev, to_next, nxt)
     )
     left3, right3 = turned(msg3, "gx", 8), turned(msg3, "gx", -8)
     return tuple(call(
         up_kernel,
         [(8, 32, 128)] * 2,
-        [low] * 10 + [mid] * 3 + [(3, 16, 128), fine],
+        [low] * 12 + [mid] * 3 + [(3, 16, 128), fine],
         (
             msg3, left3, right3,
-            t2x, t2y, t2z, s2, g2, v2, r2,
-            t1x, t1y, t1z, s1, g1,
-            t0x, t0y, t0z, s0, g0, v0, r0,
+            t2x, t2y, t2yh, t2z, t2h, s2, g2, v2, r2,
+            t1x, t1y, t1z, t1h, s1, g1,
+            t0x, t0y, t0z, t0h, s0, g0, v0, r0,
             slots, prev, nxt,
         ),
     ))

time: 88.8 us -> 85.1 us (0.958)
  the two profiles are of different devices: /device:TPU:2 before, /device:TPU:8 now
where the time goes in v3:
time: 85.1 us; the launch traced here: 84.6 us
  starting transfers between devices  28.1 us (33%)
  waiting for transfers between devices  28 us (33%)
  blocking collectives  17.7 us (21%)
  Pallas kernels  7.32 us (9%)
  local copies, waits for them, and re-layouts  2.71 us (3%)
    all_to_all x1, blocking collectives, body(): slots = lax.all_to_all(slot, ('gx', 'gy'), 0, 0, axis_index_groups=groups)  17.7 us
    ppermute x4, starting transfers between devices, turned(): return lax.ppermute(x, axis, [(i, (i + k) % n) for i in range(n)])  17.6 us
    ppermute x4, waiting for transfers between devices, shifted(): lax.ppermute(x, axis, [(i, i + k) for i in range(n) if 0 <= i + k < n])  15.9 us
    ppermute x4, waiting for transfers between devices, turned(): return lax.ppermute(x, axis, [(i, (i + k) % n) for i in range(n)])  12.1 us
    ppermute x4, starting transfers between devices, shifted(): lax.ppermute(x, axis, [(i, i + k) for i in range(n) if 0 <= i + k < n])  10.5 us
    pallas_call x5, Pallas kernels, call(): pl.pallas_call(kernel, out_shape=[jax.ShapeDtypeStruct(s, F32) for s in o...  5.31 us
    unnamed x6, local copies, waits for them, and re-layouts  2.71 us
    pallas_call x1, Pallas kernels, body(): pl.pallas_call(planes_kernel, out_shape=[jax.ShapeDtypeStruct((n, 32, 128...  2.01 us
  transfers between devices with their start and end apart: 8, of which 7 were waited for; matrix products, arithmetic and copies ran while one was open for 0% of the time, Pallas kernels for 0%

profile of v3, /device:TPU:8, one launch (start us, length us, event | category | flops | bytes accessed | tf_op | source)
XLA Modules:
  0.0 84.6 jit_solution(5788961524098937916)
XLA Ops:
  0.6 2.0 %shard_map.50 = (f32[20,32,128]{2,1,0:T(8,128)}, f32[20,32,128]{2,1,0:T(8,128)}, f32[8,32,128]{2,1,0:T(8,128)}, f32[8,32,128]{2,1,0:T(8,128)}, f32[8,32,128]{2,1,0:T(8,128)}) custom-call(f32[8,32,128]{2,1,0:T(8,128)} %k.1, f32[8,32,128]{2,1,0:T(8,128)} %f.1, f32[8,32,128]{2,1,0:T(8,128)} %s.1), custom_call_target="tpu_custom_call" | custom-call | tf_op jit(solution)/shard_map/pallas_call | solution.py:420
  2.6 3.4 %collective-permute-start = (f32[20,32,128]{2,1,0:T(8,128)}, f32[20,32,128]{2,1,0:T(8,128)S(1)}, u32[]{:S(2)}, u32[]{:S(2)}) collective-permute-start(f32[20,32,128]{2,1,0:T(8,128)} %get-tuple-element.39), channel_id=1, source_target_pairs={{0,8},{8,16},{16,24},{24,32},{32,40},{40,48},{48,56},{56,64},{64,7... | collective-permute-start | bytes 983048 | tf_op jit(solution)/shard_map/ppermute | solution.py:410
  6.1 1.3 %collective-permute-start.1 = (f32[20,32,128]{2,1,0:T(8,128)}, f32[20,32,128]{2,1,0:T(8,128)S(1)}, u32[]{:S(2)}, u32[]{:S(2)}) collective-permute-start(f32[20,32,128]{2,1,0:T(8,128)} %get-tuple-element.40), channel_id=1, source_target_pairs={{8,0},{16,8},{24,16},{32,24},{40,32},{48,40},{56,48},{64,56},{72,6... | collective-permute-start | bytes 983048 | tf_op jit(solution)/shard_map/ppermute | solution.py:410
  7.4 5.9 %collective-permute-done.xl = f32[20,32,128]{2,1,0:T(8,128)S(1)} collective-permute-done((f32[20,32,128]{2,1,0:T(8,128)}, f32[20,32,128]{2,1,0:T(8,128)S(1)}, u32[]{:S(2)}, u32[]{:S(2)}) %collective-permute-start) | collective-permute-done | bytes 327712 | tf_op jit(solution)/shard_map/ppermute | solution.py:410
  13.3 4.0 %collective-permute-done.1.xr = f32[20,32,128]{2,1,0:T(8,128)S(1)} collective-permute-done((f32[20,32,128]{2,1,0:T(8,128)}, f32[20,32,128]{2,1,0:T(8,128)S(1)}, u32[]{:S(2)}, u32[]{:S(2)}) %collective-permute-start.1) | collective-permute-done | bytes 327712 | tf_op jit(solution)/shard_map/ppermute | solution.py:410
  17.3 0.9 %copy-done = f32[8,32,128]{2,1,0:T(8,128)S(1)} copy-done((f32[8,32,128]{2,1,0:T(8,128)S(1)}, f32[8,32,128]{2,1,0:T(8,128)}, u32[]{:S(2)}) %copy-start) | copy-done | bytes 131096
  18.2 0.9 %copy-done.1 = f32[8,32,128]{2,1,0:T(8,128)S(1)} copy-done((f32[8,32,128]{2,1,0:T(8,128)S(1)}, f32[8,32,128]{2,1,0:T(8,128)}, u32[]{:S(2)}) %copy-start.1) | copy-done | bytes 131096
  19.2 0.9 %copy-done.2 = f32[8,32,128]{2,1,0:T(8,128)S(1)} copy-done((f32[8,32,128]{2,1,0:T(8,128)S(1)}, f32[8,32,128]{2,1,0:T(8,128)}, u32[]{:S(2)}) %copy-start.2) | copy-done | bytes 131096
  20.1 3.5 %collective-permute-start.2 = (f32[64,8,128]{2,1,0:T(8,128)S(1)}, f32[64,8,128]{2,1,0:T(8,128)S(1)}, u32[]{:S(2)}, u32[]{:S(2)}) collective-permute-start(f32[64,8,128]{2,1,0:T(8,128)S(1)} %get-tuple-element.41), channel_id=1, source_target_pairs={{2,0},{4,2},{6,4},{3,1},{5,3},{7,5},{10,8},{12,10},{14,12},{11,9},... | collective-permute-start | bytes 786440 | tf_op jit(solution)/shard_map/ppermute | solution.py:410
  23.6 2.3 %collective-permute-start.3 = (f32[64,8,128]{2,1,0:T(8,128)S(1)}, f32[64,8,128]{2,1,0:T(8,128)S(1)}, u32[]{:S(2)}, u32[]{:S(2)}) collective-permute-start(f32[64,8,128]{2,1,0:T(8,128)S(1)} %get-tuple-element.42), channel_id=1, source_target_pairs={{0,2},{2,4},{4,6},{1,3},{3,5},{5,7},{8,10},{10,12},{12,14},{9,11},... | collective-permute-start | bytes 786440 | tf_op jit(solution)/shard_map/ppermute | solution.py:410
  26.0 2.9 %collective-permute-done.2.above = f32[64,8,128]{2,1,0:T(8,128)S(1)} collective-permute-done((f32[64,8,128]{2,1,0:T(8,128)S(1)}, f32[64,8,128]{2,1,0:T(8,128)S(1)}, u32[]{:S(2)}, u32[]{:S(2)}) %collective-permute-start.2) | collective-permute-done | bytes 262176 | tf_op jit(solution)/shard_map/ppermute | solution.py:410
  28.8 3.1 %collective-permute-done.3.below = f32[64,8,128]{2,1,0:T(8,128)S(1)} collective-permute-done((f32[64,8,128]{2,1,0:T(8,128)S(1)}, f32[64,8,128]{2,1,0:T(8,128)S(1)}, u32[]{:S(2)}, u32[]{:S(2)}) %collective-permute-start.3) | collective-permute-done | bytes 262176 | tf_op jit(solution)/shard_map/ppermute | solution.py:410
  31.9 1.9 %shard_map.52 = (f32[16,10,8,128]{3,2,1,0:T(8,128)S(1)}, f32[24,48,128]{2,1,0:T(8,128)S(1)}, f32[24,48,128]{2,1,0:T(8,128)S(1)}, f32[24,48,128]{2,1,0:T(8,128)S(...) custom-call(f32[8,32,128]{2,1,0:T(8,128)S(1)} %copy-done, ...), custom_call_target="tpu_custom_call" | custom-call | tf_op jit(solution)/shard_map/pallas_call | solution.py:400
  33.8 17.7 %all_to_all.5.g.slots = f32[16,10,8,128]{3,2,1,0:T(8,128)S(1)} all-to-all(f32[16,10,8,128]{3,2,1,0:T(8,128)S(1)} %get-tuple-element.43), channel_id=1, replica_groups={{0,2,4,6,8,10,12,14,16,18,20,22,24,26,28,30},{32,34,36,38,40,42,44,46,4..., dimensions={0} | all-to-all | bytes 1310720 | tf_op jit(solution)/shard_map/all_to_all | solution.py:442
  51.5 0.2 shard_map.53
  51.7 8.9 %collective-permute-start.5 = (f32[36,8,128]{2,1,0:T(8,128)S(1)}, f32[36,8,128]{2,1,0:T(8,128)S(1)}, u32[]{:S(2)}, u32[]{:S(2)}) collective-permute-start(f32[36,8,128]{2,1,0:T(8,128)S(1)} %get-tuple-element.45), channel_id=1, source_target_pairs={{0,480},{8,488},{16,496},{24,504},{32,0},{40,8},{48,16},{56,24},{6... | collective-permute-start | bytes 442376 | tf_op jit(solution)/shard_map/ppermute | solution.py:415
  60.6 1.9 %collective-permute-start.4 = (f32[36,8,128]{2,1,0:T(8,128)S(1)}, f32[36,8,128]{2,1,0:T(8,128)S(1)}, u32[]{:S(2)}, u32[]{:S(2)}) collective-permute-start(f32[36,8,128]{2,1,0:T(8,128)S(1)} %get-tuple-element.44.own), channel_id=1, source_target_pairs={{0,32},{8,40},{16,48},{24,56},{32,64},{40,72},{48,80},{56,88},{64,... | collective-permute-start | bytes 442376 | tf_op jit(solution)/shard_map/ppermute | solution.py:415
  62.5 0.7 collective-permute-done.5.nxt
  63.2 5.6 %collective-permute-done.4.prev = f32[36,8,128]{2,1,0:T(8,128)S(1)} collective-permute-done((f32[36,8,128]{2,1,0:T(8,128)S(1)}, f32[36,8,128]{2,1,0:T(8,128)S(1)}, u32[]{:S(2)}, u32[]{:S(2)}) %collective-permute-start.4) | collective-permute-done | bytes 147488 | tf_op jit(solution)/shard_map/ppermute | solution.py:415
  68.8 0.5 shard_map.54
  69.3 3.7 %collective-permute-start.7 = (f32[6,8,128]{2,1,0:T(8,128)S(1)}, f32[6,8,128]{2,1,0:T(8,128)S(1)}, u32[]{:S(2)}, u32[]{:S(2)}) collective-permute-start(f32[6,8,128]{2,1,0:T(8,128)S(1)} %get-tuple-element.46.own3), channel_id=1, source_target_pairs={{0,448},{8,456},{16,464},{24,472},{32,480},{40,488},{48,496},{56,5... | collective-permute-start | bytes 73736 | tf_op jit(solution)/shard_map/ppermute | solution.py:415
  73.1 3.0 %collective-permute-start.6 = (f32[6,8,128]{2,1,0:T(8,128)S(1)}, f32[6,8,128]{2,1,0:T(8,128)S(1)}, u32[]{:S(2)}, u32[]{:S(2)}) collective-permute-start(f32[6,8,128]{2,1,0:T(8,128)S(1)} %get-tuple-element.46.own3), channel_id=1, source_target_pairs={{0,64},{8,72},{16,80},{24,88},{32,96},{40,104},{48,112},{56,120},{... | collective-permute-start | bytes 73736 | tf_op jit(solution)/shard_map/ppermute | solution.py:415
  76.1 5.8 %collective-permute-done.6.left3 = f32[6,8,128]{2,1,0:T(8,128)S(1)} collective-permute-done((f32[6,8,128]{2,1,0:T(8,128)S(1)}, f32[6,8,128]{2,1,0:T(8,128)S(1)}, u32[]{:S(2)}, u32[]{:S(2)}) %collective-permute-start.6) | collective-permute-done | bytes 24608 | tf_op jit(solution)/shard_map/ppermute | solution.py:415
  81.9 2.8 %shard_map.55 = (f32[8,32,128]{2,1,0:T(8,128)}, f32[8,32,128]{2,1,0:T(8,128)}) custom-call(f32[6,8,128]{2,1,0:T(8,128)S(1)} %get-tuple-element.46.own3, f32[6,8,128]{2,1,0:T(8,128)S(1)} %collective-permute-done.6.left3, f32[6,8,128]{2,1,0:T(8,128)S(1)} %collective-permute-done.7.right3, f32[24,8,128]{2,1,0:T(8,128)S(1)} %get-tuple-element.47.t2x, ...), custom_call_target="tpu_custom_call" | custom-call | tf_op jit(solution)/shard_map/pallas_call | solution.py:400
  (5 shorter events, 0.0 us)
Async XLA Ops:
  2.6 10.7 %collective-permute-start = (f32[20,32,128]{2,1,0:T(8,128)}, f32[20,32,128]{2,1,0:T(8,128)S(1)}, u32[]{:S(2)}, u32[]{:S(2)}) collective-permute-start(f32[20,32,128]{2,1,0:T(8,128)} %get-tuple-element.39), channel_id=1, source_target_pairs={{0,8},{8,16},{16,24},{24,32},{32,40},{40,48},{48,56},{56,64},{64,7... | collective-permute-start | bytes 983048 | tf_op jit(solution)/shard_map/ppermute | solution.py:410
  6.1 11.3 %collective-permute-start.1 = (f32[20,32,128]{2,1,0:T(8,128)}, f32[20,32,128]{2,1,0:T(8,128)S(1)}, u32[]{:S(2)}, u32[]{:S(2)}) collective-permute-start(f32[20,32,128]{2,1,0:T(8,128)} %get-tuple-element.40), channel_id=1, source_target_pairs={{8,0},{16,8},{24,16},{32,24},{40,32},{48,40},{56,48},{64,56},{72,6... | collective-permute-start | bytes 983048 | tf_op jit(solution)/shard_map/ppermute | solution.py:410
  17.3 0.9 %copy-start = (f32[8,32,128]{2,1,0:T(8,128)S(1)}, f32[8,32,128]{2,1,0:T(8,128)}, u32[]{:S(2)}) copy-start(f32[8,32,128]{2,1,0:T(8,128)} %get-tuple-element.36.k) | copy-start | bytes 393220
  18.2 0.9 %copy-start.1 = (f32[8,32,128]{2,1,0:T(8,128)S(1)}, f32[8,32,128]{2,1,0:T(8,128)}, u32[]{:S(2)}) copy-start(f32[8,32,128]{2,1,0:T(8,128)} %get-tuple-element.37.f) | copy-start | bytes 393220
  19.2 0.9 %copy-start.2 = (f32[8,32,128]{2,1,0:T(8,128)S(1)}, f32[8,32,128]{2,1,0:T(8,128)}, u32[]{:S(2)}) copy-start(f32[8,32,128]{2,1,0:T(8,128)} %get-tuple-element.38.s) | copy-start | bytes 393220
  20.1 8.7 %collective-permute-start.2 = (f32[64,8,128]{2,1,0:T(8,128)S(1)}, f32[64,8,128]{2,1,0:T(8,128)S(1)}, u32[]{:S(2)}, u32[]{:S(2)}) collective-permute-start(f32[64,8,128]{2,1,0:T(8,128)S(1)} %get-tuple-element.41), channel_id=1, source_target_pairs={{2,0},{4,2},{6,4},{3,1},{5,3},{7,5},{10,8},{12,10},{14,12},{11,9},... | collective-permute-start | bytes 786440 | tf_op jit(solution)/shard_map/ppermute | solution.py:410
  23.6 8.3 %collective-permute-start.3 = (f32[64,8,128]{2,1,0:T(8,128)S(1)}, f32[64,8,128]{2,1,0:T(8,128)S(1)}, u32[]{:S(2)}, u32[]{:S(2)}) collective-permute-start(f32[64,8,128]{2,1,0:T(8,128)S(1)} %get-tuple-element.42), channel_id=1, source_target_pairs={{0,2},{2,4},{4,6},{1,3},{3,5},{5,7},{8,10},{10,12},{12,14},{9,11},... | collective-permute-start | bytes 786440 | tf_op jit(solution)/shard_map/ppermute | solution.py:410
  51.7 11.6 %collective-permute-start.5 = (f32[36,8,128]{2,1,0:T(8,128)S(1)}, f32[36,8,128]{2,1,0:T(8,128)S(1)}, u32[]{:S(2)}, u32[]{:S(2)}) collective-permute-start(f32[36,8,128]{2,1,0:T(8,128)S(1)} %get-tuple-element.45), channel_id=1, source_target_pairs={{0,480},{8,488},{16,496},{24,504},{32,0},{40,8},{48,16},{56,24},{6... | collective-permute-start | bytes 442376 | tf_op jit(solution)/shard_map/ppermute | solution.py:415
  60.6 8.2 %collective-permute-start.4 = (f32[36,8,128]{2,1,0:T(8,128)S(1)}, f32[36,8,128]{2,1,0:T(8,128)S(1)}, u32[]{:S(2)}, u32[]{:S(2)}) collective-permute-start(f32[36,8,128]{2,1,0:T(8,128)S(1)} %get-tuple-element.44.own), channel_id=1, source_target_pairs={{0,32},{8,40},{16,48},{24,56},{32,64},{40,72},{48,80},{56,88},{64,... | collective-permute-start | bytes 442376 | tf_op jit(solution)/shard_map/ppermute | solution.py:415
  69.3 6.8 %collective-permute-start.7 = (f32[6,8,128]{2,1,0:T(8,128)S(1)}, f32[6,8,128]{2,1,0:T(8,128)S(1)}, u32[]{:S(2)}, u32[]{:S(2)}) collective-permute-start(f32[6,8,128]{2,1,0:T(8,128)S(1)} %get-tuple-element.46.own3), channel_id=1, source_target_pairs={{0,448},{8,456},{16,464},{24,472},{32,480},{40,488},{48,496},{56,5... | collective-permute-start | bytes 73736 | tf_op jit(solution)/shard_map/ppermute | solution.py:415
  73.1 8.8 %collective-permute-start.6 = (f32[6,8,128]{2,1,0:T(8,128)S(1)}, f32[6,8,128]{2,1,0:T(8,128)S(1)}, u32[]{:S(2)}, u32[]{:S(2)}) collective-permute-start(f32[6,8,128]{2,1,0:T(8,128)S(1)} %get-tuple-element.46.own3), channel_id=1, source_target_pairs={{0,64},{8,72},{16,80},{24,88},{32,96},{40,104},{48,112},{56,120},{... | collective-permute-start | bytes 73736 | tf_op jit(solution)/shard_map/ppermute | solution.py:415

commit v4 on v3

--- a/solution.py
+++ b/solution.py
@@ -8,6 +8,7 @@
 OMEGA = 0.7
 COARSE = 8
 F32 = jnp.float32
+PARAMS = pltpu.CompilerParams(vmem_limit_bytes=32 * 1024 * 1024)
 
 
 def lanes(like):
@@ -160,64 +161,47 @@
     ref[p, pl.ds(1, half, stride=2), :] = e
 
 
-def planes_kernel(k, f, s, to_left, to_right, kv, fv, sv, sems):
-    copies = [
-        pltpu.make_async_copy(src.at[pl.ds(4 * h, 4)], dst.at[pl.ds(4 * h, 4)], sems.at[2 * i + h])
-        for i, (src, dst) in enumerate(((k, kv), (f, fv), (s, sv)))
-        for h in range(2)
-    ]
-    for c in copies:
-        c.start()
-    for c in copies:
-        c.wait()
-    for p in range(8):
-        to_left[p] = kv[p]
-        to_right[p] = kv[p]
-    for p in range(6):
-        to_left[8 + p] = fv[p]
-        to_left[14 + p] = sv[p]
-        to_right[8 + p] = fv[2 + p]
-        to_right[14 + p] = sv[2 + p]
-
-
-def window(own, left, right, at, edge):
-    for p in range(edge):
-        yield 8 - edge + p, left, at + p
-    for p in range(8):
-        yield 8 + p, own, p
-    for p in range(edge):
-        yield 16 + p, right, at + p
-
-
-def halo_planes(k, f, s, xl, xr):
-    return (
-        tuple(window(k, xl, xr, 0, 8)),
-        tuple(window(f, xl, xr, 8, 6)),
-        tuple(window(s, xl, xr, 14, 6)),
-    )
-
-
-def rows_kernel(k, f, s, xl, xr, up, down):
+def fine_planes(to_left, to_right, xl, xr):
+    out = []
+    for at, edge, near in ((0, 8, 7), (8, 6, 6), (14, 6, 6)):
+        planes = []
+        for p in range(edge):
+            planes.append((8 - edge + p, xl, at + p, edge - p <= near))
+        for p in range(8):
+            if p < edge:
+                planes.append((8 + p, to_left, at + p, True))
+            else:
+                planes.append((8 + p, to_right, at + p - 8 + edge, True))
+        for p in range(edge):
+            planes.append((16 + p, xr, at + p, p < near))
+        out.append(planes)
+    return out
+
+
+def rows_kernel(to_left, to_right, xl, xr, up, down):
     n = 0
-    for planes in halo_planes(k, f, s, xl, xr):
-        for _, ref, p in planes:
-            up[n] = ref[p, pl.ds(24, 8), :]
-            down[n] = ref[p, pl.ds(0, 8), :]
-            n += 1
+    for planes in fine_planes(to_left, to_right, xl, xr):
+        for _, ref, p, near in planes:
+            if near:
+                up[n] = ref[p, pl.ds(24, 8), :]
+                down[n] = ref[p, pl.ds(0, 8), :]
+                n += 1
 
 
 def fine_kernel(
-    k, f, s, xl, xr, above, below,
-    slot, ve, re, tx, ty, tz, tzh, st, gain, t1x, t1y, t1z, t1h, s1, g1,
-    ke, fe, k1, f1, v1, r1,
+    to_left, to_right, xl, xr, above, below,
+    slot, ve, re, tx, ty, tz, tzh, st, gain, t1x, t1y, t1z, t1h, s1, g1, f1,
+    ke, fe, k1, v1, r1,
 ):
     n = 0
-    for target, planes in zip((ke, fe, st), halo_planes(k, f, s, xl, xr)):
-        for at, ref, p in planes:
+    zero = jnp.zeros((8, 128), F32)
+    sub = rows(zero)
+    for target, planes in zip((ke, fe, st), fine_planes(to_left, to_right, xl, xr)):
+        for at, ref, p, near in planes:
             target[at, pl.ds(0, 32), :] = ref[p]
-            target[at, pl.ds(32, 8), :] = above[n]
-            target[at, pl.ds(40, 8), :] = below[n]
-            n += 1
+            target[at, pl.ds(32, 8), :] = above[n] if near else zero
+            target[at, pl.ds(40, 8), :] = below[n] if near else zero
+            n += near
     op = Level(0, tx, ty, tz, tzh, st, gain)
     op.build(ke, 2, 21)
     op.first_sweep(ve, fe, 2, 21)
@@ -237,14 +221,29 @@
     source = [restrict(r1, 4 + 2 * p, 16, 1) for p in range(2)]
     perm = [restrict(k1, 4 + 2 * p, 16, 1) * 0.125 for p in range(2)]
     store = [restrict(s1, 4 + 2 * p, 16, 1) for p in range(2)]
-    tiles = [pack4(*source, *perm), pack4(*store, *store)]
-    for ref in (r1, v1):
-        for p in (4, 6):
-            t = pack2(ref[p, pl.ds(0, 16), :], ref[p + 1, pl.ds(0, 16), :])
-            tiles += [t[:8], t[8:]]
+    tiles = [pack4(*source, *perm), pack4(*store, *store), zero, zero, zero]
     for peer in range(16):
         for i, t in enumerate(tiles):
             slot[peer, i] = t
+    j = lax.axis_index("gy")
+    x = lax.axis_index("gx") % 4
+    after, before = (j + 1) % 4, (j + 3) % 4
+    first, last = pl.ds(0, 8), pl.ds(8, 8)
+    for step, p, q in ((1, 5, 6), (3, 6, 4)):
+        to = 4 * ((x + step) % 4)
+        slot[to + j, 2] = pack2(r1[5, first, :], r1[6, first, :])
+        slot[to + j, 3] = pack2(r1[5, last, :], r1[6, last, :])
+        slot[to + j, 4] = pack2(f1[p, first, :], f1[p, last, :])
+        slot[to + after, 2] = pack2(r1[q, last, :], r1[q + 1, last, :])
+        slot[to + before, 2] = pack2(r1[q, first, :], r1[q + 1, first, :])
+    for n in range(2):
+        p = 4 + 2 * n
+        r = pack2(r1[p, last, :], r1[p + 1, last, :])
+        f = pack2(f1[p, last, :], f1[p + 1, last, :])
+        slot[4 * x + after, 2 + n] = jnp.where(sub < 4, roll(f, -4, 0), r)
+        r = pack2(r1[p, first, :], r1[p + 1, first, :])
+        f = pack2(f1[p, first, :], f1[p + 1, first, :])
+        slot[4 * x + before, 2 + n] = jnp.where(sub < 4, r, roll(f, 4, 0))
 
 
 def ring_kernel(g, to_next, to_prev):
@@ -263,20 +262,13 @@
             for at, v in ((0, f0), (1, f1), (8, k0), (9, k1), (16, s0), (17, s1)):
                 out[at + 2 * x] = v
     j = lax.axis_index("gy")
-    for out, x, v in ((to_next, 3, 8), (to_prev, 0, 6)):
-        for i, t in enumerate(edge_tiles(v)):
-            out[24 + i] = g[4 * x + peer_of(j, t[0]), t[1]]
-
-
-def peer_of(j, step):
-    return jnp.clip(j + step, 0, 3)
-
-
-def edge_tiles(v):
-    out = []
-    for t in (2, 4, v):
-        out += [(0, t), (0, t + 1), (1, t), (-1, t + 1)]
-    return out
+    x = lax.axis_index("gx") % 4
+    for out, step in ((to_next, 3), (to_prev, 1)):
+        at = 4 * ((x + step) % 4)
+        for i in range(3):
+            out[24 + i] = g[at + j, 2 + i]
+        out[27] = g[at + (j + 1) % 4, 2]
+        out[28] = g[at + (j + 3) % 4, 2]
 
 
 def coarse_kernel(
@@ -301,14 +293,64 @@
         msg[2 * i + 1] = pack_coarse(*cells[4:])
 
 
+def halo_kernel(slots, prev, nxt, f1, tx, ty, tz, th, st, gain, v, q1, fe):
+    zero = jnp.zeros((8, 128), F32)
+    sub = rows(zero)
+    j = lax.axis_index("gy")
+    x = lax.axis_index("gx") % 4
+    after, before = (j + 1) % 4, (j + 3) % 4
+    first, last, halo = pl.ds(0, 8), pl.ds(8, 8), pl.ds(16, 8)
+
+    def beside(step, outer):
+        at = 4 * jnp.clip(x + step, 0, 3)
+        inside = (x + step >= 0) & (x + step < 4)
+        tiles = ((j, 2), (j, 3), (j, 4), (after, 2), (before, 2))
+        return [
+            split(jnp.where(inside, slots[at + y, t], outer[24 + n]), 1)
+            for n, (y, t) in enumerate(tiles)
+        ]
+
+    left, right = beside(-1, prev), beside(1, nxt)
+    ends = []
+    for n in range(2):
+        ends.append((split(slots[4 * x + after, 2 + n], 1), split(slots[4 * x + before, 2 + n], 1)))
+    for q in range(2, 10):
+        fe[q] = f1[q]
+    for q in range(4, 8):
+        a, b = (e[q % 2] for e in ends[(q - 4) // 2])
+        fe[q, halo, :] = jnp.where(
+            sub == 2, roll(a, -4, 0), jnp.where(sub == 5, roll(b, 4, 0), f1[q, halo, :])
+        )
+    for q, side in ((1, left), (10, right)):
+        fe[q, first, :], fe[q, last, :] = side[2]
+        fe[q, halo, :] = zero
+    op = Level(1, tx, ty, tz, th, st, gain)
+    op.first_sweep(v, fe, 1, 10)
+    op.sweep(v, fe, 2, 9)
+    op.defect(q1, v, fe, 3, 8)
+    for q in range(4, 8):
+        a, b = (e[q % 2] for e in ends[(q - 4) // 2])
+        near = (sub == 1) | (sub == 2)
+        q1[q, halo, :] = jnp.where(
+            near, a, jnp.where((sub == 5) | (sub == 6), b, q1[q, halo, :])
+        )
+    for side, q, edge, corner in ((left, 1, 1, 2), (right, 9, 10, 8)):
+        for n in range(2):
+            q1[q + n, first, :] = side[0][n]
+            q1[q + n, last, :] = side[1][n]
+        for n in range(2):
+            q1[corner + n, halo, :] = jnp.where(sub < 4, side[3][n], side[4][n])
+        q1[edge, halo, :] = zero
+
+
 def up_kernel(
     own3, left3, right3,
     t2x, t2y, t2yh, t2z, t2h, s2, g2, v2, r2,
     t1x, t1y, t1z, t1h, s1, g1,
     t0x, t0y, t0z, t0h, s0, g0, v0, r0,
-    slots, prev, nxt,
+    w1, q1,
     pressure, residual,
-    k3, f3, s3, t3x, t3y, t3yh, t3z, t3h, g3, v3, c2, e2, c1, q1, w1, dup, c0,
+    k3, f3, s3, t3x, t3y, t3yh, t3z, t3h, g3, v3, c2, e2, c1, dup, c0, pv, rv, sems,
 ):
     n = 0
     for ref in (left3, own3, right3):
@@ -349,35 +391,6 @@
             c1[q, pl.ds(0, 16), :] = dup[0]
             c1[q, pl.ds(16, 8), :] = halo
 
-    def pairs(get, count):
-        out = []
-        for n in range(count):
-            a, b, c, d = (get(4 * n + m) for m in range(4))
-            out.append(split(jnp.concatenate([a, b, jnp.where(sub < 4, c, d)], axis=0), 1))
-        return out
-
-    def beside(step, v, outer):
-        at = 4 * jnp.clip(x + step, 0, 3)
-        tiles = edge_tiles(v)
-        inside = (x + step >= 0) & (x + step < 4)
-
-        def get(n):
-            y, t = tiles[n]
-            return jnp.where(inside, slots[at + peer_of(j, y), t], outer[24 + n])
-
-        return pairs(get, 3)
-
-    def own(n):
-        y, t = (edge_tiles(6) + edge_tiles(8)[8:])[n]
-        return slots[4 * x + peer_of(j, y), t]
-
-    (_, a), (b, c), (d, e) = beside(-1, 8, prev)
-    q1[1], q1[2], q1[3], w1[2], w1[3] = a, b, c, d, e
-    (a, b), (c, _), (d, e) = beside(1, 6, nxt)
-    q1[8], q1[9], q1[10], w1[8], w1[9] = a, b, c, d, e
-    (a, b), (c, d), (e, f), (g, h) = pairs(own, 4)
-    q1[4], q1[5], q1[6], q1[7] = a, b, c, d
-    w1[4], w1[5], w1[6], w1[7] = e, f, g, h
     op = Level(1, t1x, t1y, t1z, t1h, s1, g1)
     op.sweep(c1, q1, 1, 10)
     op.sweep(c1, q1, 2, 9)
@@ -389,11 +402,22 @@
     op.sweep(c0, r0, 6, 17)
     op.sweep(c0, r0, 7, 16)
 
+    copies = []
+
     def use(p, here, out):
-        pressure[p - 8] = v0[p, pl.ds(0, 32), :] + here[:32]
-        residual[p - 8] = r0[p, pl.ds(0, 32), :] - out[:32]
+        n = p - 8
+        pv[n] = v0[p, pl.ds(0, 32), :] + here[:32]
+        rv[n] = r0[p, pl.ds(0, 32), :] - out[:32]
+        if n % 2 == 1:
+            two = pl.ds(n - 1, 2)
+            for m, (src, dst) in enumerate(((pv, pressure), (rv, residual))):
+                c = pltpu.make_async_copy(src.at[two], dst.at[two], sems.at[n - m])
+                c.start()
+                copies.append(c)
 
     op.apply(c0, 8, 15, use)
+    for c in copies:
+        c.wait()
 
 
 def call(kernel, outs, scratch, args):
@@ -401,7 +425,7 @@
         kernel,
         out_shape=[jax.ShapeDtypeStruct(s, F32) for s in outs],
         scratch_shapes=[pltpu.VMEM(s, F32) for s in scratch],
-        compiler_params=pltpu.CompilerParams(vmem_limit_bytes=32 * 1024 * 1024),
+        compiler_params=PARAMS,
     )(*args)
 
 
@@ -417,48 +441,50 @@
 
 def body(permeability, storage, source_term):
     k, s, f = permeability, storage, source_term
-    to_left, to_right, k, f, s = pl.pallas_call(
-        planes_kernel,
-        out_shape=[
-            jax.ShapeDtypeStruct((n, 32, 128), F32) for n in (20, 20, 8, 8, 8)
-        ],
-        in_specs=[pl.BlockSpec(memory_space=pl.ANY)] * 3,
-        scratch_shapes=[pltpu.SemaphoreType.DMA((6,))],
-    )(k, f, s)
+    to_left = jnp.concatenate([k, f[:6], s[:6]])
+    to_right = jnp.concatenate([k, f[2:], s[2:]])
     xl = shifted(to_right, "gx", 1)
     xr = shifted(to_left, "gx", -1)
-    up, down = call(rows_kernel, [(64, 8, 128)] * 2, [], (k, f, s, xl, xr))
+    planes = (to_left, to_right, xl, xr)
+    up, down = call(rows_kernel, [(62, 8, 128)] * 2, [], planes)
     below = shifted(up, "gy", 1)
     above = shifted(down, "gy", -1)
     fine, mid = (24, 48, 128), (12, 24, 128)
-    slot, v0, r0, t0x, t0y, t0z, t0h, s0, g0, t1x, t1y, t1z, t1h, s1, g1 = call(
+    slot, v0, r0, t0x, t0y, t0z, t0h, s0, g0, t1x, t1y, t1z, t1h, s1, g1, f1 = call(
         fine_kernel,
-        [(16, 10, 8, 128)] + [fine] * 8 + [mid] * 6,
-        [fine] * 2 + [mid] * 4,
-        (k, f, s, xl, xr, above, below),
+        [(16, 5, 8, 128)] + [fine] * 8 + [mid] * 7,
+        [fine] * 2 + [mid] * 3,
+        planes + (above, below),
     )
     n = lax.axis_size("gx") * lax.axis_size("gy")
     groups = [[16 * a + b for b in range(16)] for a in range(n // 16)]
     slots = lax.all_to_all(slot, ("gx", "gy"), 0, 0, axis_index_groups=groups)
-    to_next, to_prev = call(ring_kernel, [(36, 8, 128)] * 2, [], (slots,))
+    to_next, to_prev = call(ring_kernel, [(29, 8, 128)] * 2, [], (slots,))
     prev, nxt = turned(to_next, "gx", 4), turned(to_prev, "gx", -4)
     low = (24, 8, 128)
     msg3, t2x, t2y, t2yh, t2z, t2h, s2, g2, v2, r2 = call(
         coarse_kernel, [(6, 8, 128)] + [low] * 9, [low] * 2, (prev, to_next, nxt)
     )
+    w1, q1 = call(
+        halo_kernel, [mid] * 2, [mid], (slots, prev, nxt, f1, t1x, t1y, t1z, t1h, s1, g1)
+    )
     left3, right3 = turned(msg3, "gx", 8), turned(msg3, "gx", -8)
-    return tuple(call(
+    own = (8, 32, 128)
+    scratch = [low] * 12 + [mid, (3, 16, 128), fine, own, own]
+    args = (
+        msg3, left3, right3,
+        t2x, t2y, t2yh, t2z, t2h, s2, g2, v2, r2,
+        t1x, t1y, t1z, t1h, s1, g1,
+        t0x, t0y, t0z, t0h, s0, g0, v0, r0,
+        w1, q1,
+    )
+    return tuple(pl.pallas_call(
         up_kernel,
-        [(8, 32, 128)] * 2,
-        [low] * 12 + [mid] * 3 + [(3, 16, 128), fine],
-        (
-            msg3, left3, right3,
-            t2x, t2y, t2yh, t2z, t2h, s2, g2, v2, r2,
-            t1x, t1y, t1z, t1h, s1, g1,
-            t0x, t0y, t0z, t0h, s0, g0, v0, r0,
-            slots, prev, nxt,
-        ),
-    ))
+        out_shape=[jax.ShapeDtypeStruct(own, F32)] * 2,
+        out_specs=[pl.BlockSpec(memory_space=pl.ANY)] * 2,
+        scratch_shapes=[pltpu.VMEM(n, F32) for n in scratch] + [pltpu.SemaphoreType.DMA((8,))],
+        compiler_params=PARAMS,
+    )(*args))
 
 
 def solution(mesh):

time: 85.1 us -> 78.9 us (0.927)
  blocking collectives: 17.7 us -> 15.7 us
  Pallas kernels: 7.32 us -> 5.63 us
  local copies, waits for them, and re-layouts: 2.71 us -> 1.1 us
  waiting for transfers between devices: 28 us -> 27.1 us
    unnamed x6 -> x2, local copies, waits for them, and re-layouts: 2.71 us -> 0.01 us
    pallas_call x5, Pallas kernels: 5.31 us -> 2.81 us  [call(): pl.pallas_call(kernel, out_shape=[jax.ShapeDtypeStruct(s, F32) for s in o...]
    all_to_all x1, blocking collectives: 17.7 us -> 15.7 us  [body(): slots = lax.all_to_all(slot, ('gx', 'gy'), 0, 0, axis_index_groups=groups)]
    slice x0 -> x1, local copies, waits for them, and re-layouts: none -> 1.1 us  [body(): to_right = jnp.concatenate([k, f[2:], s[2:]])]
where the time goes in v4:
time: 78.9 us; the launch traced here: 78.5 us
  starting transfers between devices  28.1 us (36%)
  waiting for transfers between devices  27.1 us (34%)
  blocking collectives  15.7 us (20%)
  Pallas kernels  5.63 us (7%)
  local copies, waits for them, and re-layouts  1.1 us (1%)
    ppermute x4, starting transfers between devices, turned(): return lax.ppermute(x, axis, [(i, (i + k) % n) for i in range(n)])  17.6 us
    all_to_all x1, blocking collectives, body(): slots = lax.all_to_all(slot, ('gx', 'gy'), 0, 0, axis_index_groups=groups)  15.7 us
    ppermute x4, waiting for transfers between devices, shifted(): lax.ppermute(x, axis, [(i, i + k) for i in range(n) if 0 <= i + k < n])  15.6 us
    ppermute x4, waiting for transfers between devices, turned(): return lax.ppermute(x, axis, [(i, (i + k) % n) for i in range(n)])  11.5 us
    ppermute x4, starting transfers between devices, shifted(): lax.ppermute(x, axis, [(i, i + k) for i in range(n) if 0 <= i + k < n])  10.6 us
    pallas_call x1, Pallas kernels, body(): pl.pallas_call(up_kernel, out_shape=[jax.ShapeDtypeStruct(own, F32)] * 2,...  2.82 us
    pallas_call x5, Pallas kernels, call(): pl.pallas_call(kernel, out_shape=[jax.ShapeDtypeStruct(s, F32) for s in o...  2.81 us
  transfers between devices with their start and end apart: 8, of which 7 were waited for; matrix products, arithmetic and copies ran while one was open for 0% of the time, Pallas kernels for 0%

profile of v4, /device:TPU:8, one launch (start us, length us, event | category | flops | bytes accessed | tf_op | source)
XLA Modules:
  0.0 78.5 jit_solution(16971867389860601842)
XLA Ops:
  0.6 1.1 %fusion.2 = (f32[6,32,128]{2,1,0:T(8,128)S(1)}, f32[6,32,128]{2,1,0:T(8,128)S(1)}, f32[6,32,128]{2,1,0:T(8,128)S(1)}, f32[6,32,128]{2,1,0:T(8,128)S(1)}) fusion(f32[8,32,128]{2,1,0:T(8,128)} %param.5, f32[8,32,128]{2,1,0:T(8,128)} %param.4), kind=kLoop, calls=%fused_computation.4 | loop fusion | bytes 786432 | tf_op jit(solution)/shard_map/slice | solution.py:445
  1.8 0.1 fusion.1
  1.8 3.4 %collective-permute-start = (f32[20,32,128]{2,1,0:T(8,128)S(1)}, f32[20,32,128]{2,1,0:T(8,128)S(1)}, u32[]{:S(2)}, u32[]{:S(2)}) collective-permute-start(f32[20,32,128]{2,1,0:T(8,128)S(1)} %get-tuple-element.66.to_right), channel_id=1, source_target_pairs={{0,8},{8,16},{16,24},{24,32},{32,40},{40,48},{48,56},{56,64},{64,7... | collective-permute-start | bytes 983048 | tf_op jit(solution)/shard_map/ppermute | solution.py:434
  5.2 1.3 %collective-permute-start.1 = (f32[20,32,128]{2,1,0:T(8,128)S(1)}, f32[20,32,128]{2,1,0:T(8,128)S(1)}, u32[]{:S(2)}, u32[]{:S(2)}) collective-permute-start(f32[20,32,128]{2,1,0:T(8,128)S(1)} %get-tuple-element.67.to_left), channel_id=1, source_target_pairs={{8,0},{16,8},{24,16},{32,24},{40,32},{48,40},{56,48},{64,56},{72,6... | collective-permute-start | bytes 983048 | tf_op jit(solution)/shard_map/ppermute | solution.py:434
  6.5 5.6 %collective-permute-done.xl = f32[20,32,128]{2,1,0:T(8,128)S(1)} collective-permute-done((f32[20,32,128]{2,1,0:T(8,128)S(1)}, f32[20,32,128]{2,1,0:T(8,128)S(1)}, u32[]{:S(2)}, u32[]{:S(2)}) %collective-permute-start) | collective-permute-done | bytes 327712 | tf_op jit(solution)/shard_map/ppermute | solution.py:434
  12.2 4.1 %collective-permute-done.1.xr = f32[20,32,128]{2,1,0:T(8,128)S(1)} collective-permute-done((f32[20,32,128]{2,1,0:T(8,128)S(1)}, f32[20,32,128]{2,1,0:T(8,128)S(1)}, u32[]{:S(2)}, u32[]{:S(2)}) %collective-permute-start.1) | collective-permute-done | bytes 327712 | tf_op jit(solution)/shard_map/ppermute | solution.py:434
  16.4 3.5 %collective-permute-start.2 = (f32[62,8,128]{2,1,0:T(8,128)S(1)}, f32[62,8,128]{2,1,0:T(8,128)S(1)}, u32[]{:S(2)}, u32[]{:S(2)}) collective-permute-start(f32[62,8,128]{2,1,0:T(8,128)S(1)} %get-tuple-element.34), channel_id=1, source_target_pairs={{2,0},{4,2},{6,4},{3,1},{5,3},{7,5},{10,8},{12,10},{14,12},{11,9},... | collective-permute-start | bytes 761864 | tf_op jit(solution)/shard_map/ppermute | solution.py:434
  19.9 2.3 %collective-permute-start.3 = (f32[62,8,128]{2,1,0:T(8,128)S(1)}, f32[62,8,128]{2,1,0:T(8,128)S(1)}, u32[]{:S(2)}, u32[]{:S(2)}) collective-permute-start(f32[62,8,128]{2,1,0:T(8,128)S(1)} %get-tuple-element.35), channel_id=1, source_target_pairs={{0,2},{2,4},{4,6},{1,3},{3,5},{5,7},{8,10},{10,12},{12,14},{9,11},... | collective-permute-start | bytes 761864 | tf_op jit(solution)/shard_map/ppermute | solution.py:434
  22.2 2.7 %collective-permute-done.2.above = f32[62,8,128]{2,1,0:T(8,128)S(1)} collective-permute-done((f32[62,8,128]{2,1,0:T(8,128)S(1)}, f32[62,8,128]{2,1,0:T(8,128)S(1)}, u32[]{:S(2)}, u32[]{:S(2)}) %collective-permute-start.2) | collective-permute-done | bytes 253984 | tf_op jit(solution)/shard_map/ppermute | solution.py:434
  24.9 3.1 %collective-permute-done.3.below = f32[62,8,128]{2,1,0:T(8,128)S(1)} collective-permute-done((f32[62,8,128]{2,1,0:T(8,128)S(1)}, f32[62,8,128]{2,1,0:T(8,128)S(1)}, u32[]{:S(2)}, u32[]{:S(2)}) %collective-permute-start.3) | collective-permute-done | bytes 253984 | tf_op jit(solution)/shard_map/ppermute | solution.py:434
  28.1 1.9 %shard_map.51 = (f32[16,5,8,128]{3,2,1,0:T(8,128)S(1)}, f32[24,48,128]{2,1,0:T(8,128)S(1)}, f32[24,48,128]{2,1,0:T(8,128)S(1)}, f32[24,48,128]{2,1,0:T(8,128)S(1...) custom-call(f32[20,32,128]{2,1,0:T(8,128)S(1)} %get-tuple-element.67, ...), custom_call_target="tpu_custom_call" | custom-call | tf_op jit(solution)/shard_map/pallas_call | solution.py:424
  30.0 15.7 %all_to_all.5.g.slots = f32[16,5,8,128]{3,2,1,0:T(8,128)S(1)} all-to-all(f32[16,5,8,128]{3,2,1,0:T(8,128)S(1)} %get-tuple-element.36), channel_id=1, replica_groups={{0,2,4,6,8,10,12,14,16,18,20,22,24,26,28,30},{32,34,36,38,40,42,44,46,4..., dimensions={0} | all-to-all | bytes 655360 | tf_op jit(solution)/shard_map/all_to_all | solution.py:461
  45.7 0.2 shard_map.52
  45.8 8.9 %collective-permute-start.5 = (f32[29,8,128]{2,1,0:T(8,128)S(1)}, f32[29,8,128]{2,1,0:T(8,128)S(1)}, u32[]{:S(2)}, u32[]{:S(2)}) collective-permute-start(f32[29,8,128]{2,1,0:T(8,128)S(1)} %get-tuple-element.38), channel_id=1, source_target_pairs={{0,480},{8,488},{16,496},{24,504},{32,0},{40,8},{48,16},{56,24},{6... | collective-permute-start | bytes 356360 | tf_op jit(solution)/shard_map/ppermute | solution.py:439
  54.8 1.9 %collective-permute-start.4 = (f32[29,8,128]{2,1,0:T(8,128)S(1)}, f32[29,8,128]{2,1,0:T(8,128)S(1)}, u32[]{:S(2)}, u32[]{:S(2)}) collective-permute-start(f32[29,8,128]{2,1,0:T(8,128)S(1)} %get-tuple-element.37.own), channel_id=1, source_target_pairs={{0,32},{8,40},{16,48},{24,56},{32,64},{40,72},{48,80},{56,88},{64,... | collective-permute-start | bytes 356360 | tf_op jit(solution)/shard_map/ppermute | solution.py:439
  56.7 0.5 collective-permute-done.5.nxt
  57.2 5.6 %collective-permute-done.4.prev = f32[29,8,128]{2,1,0:T(8,128)S(1)} collective-permute-done((f32[29,8,128]{2,1,0:T(8,128)S(1)}, f32[29,8,128]{2,1,0:T(8,128)S(1)}, u32[]{:S(2)}, u32[]{:S(2)}) %collective-permute-start.4) | collective-permute-done | bytes 118816 | tf_op jit(solution)/shard_map/ppermute | solution.py:439
  62.7 0.5 shard_map.53
  63.2 3.7 %collective-permute-start.7 = (f32[6,8,128]{2,1,0:T(8,128)S(1)}, f32[6,8,128]{2,1,0:T(8,128)S(1)}, u32[]{:S(2)}, u32[]{:S(2)}) collective-permute-start(f32[6,8,128]{2,1,0:T(8,128)S(1)} %get-tuple-element.39.own3), channel_id=1, source_target_pairs={{0,448},{8,456},{16,464},{24,472},{32,480},{40,488},{48,496},{56,5... | collective-permute-start | bytes 73736 | tf_op jit(solution)/shard_map/ppermute | solution.py:439
  66.9 3.0 %collective-permute-start.6 = (f32[6,8,128]{2,1,0:T(8,128)S(1)}, f32[6,8,128]{2,1,0:T(8,128)S(1)}, u32[]{:S(2)}, u32[]{:S(2)}) collective-permute-start(f32[6,8,128]{2,1,0:T(8,128)S(1)} %get-tuple-element.39.own3), channel_id=1, source_target_pairs={{0,64},{8,72},{16,80},{24,88},{32,96},{40,104},{48,112},{56,120},{... | collective-permute-start | bytes 73736 | tf_op jit(solution)/shard_map/ppermute | solution.py:439
  70.0 0.3 shard_map.54
  70.2 0.0 collective-permute-done.7.right3
  70.2 5.5 %collective-permute-done.6.left3 = f32[6,8,128]{2,1,0:T(8,128)S(1)} collective-permute-done((f32[6,8,128]{2,1,0:T(8,128)S(1)}, f32[6,8,128]{2,1,0:T(8,128)S(1)}, u32[]{:S(2)}, u32[]{:S(2)}) %collective-permute-start.6) | collective-permute-done | bytes 24608 | tf_op jit(solution)/shard_map/ppermute | solution.py:439
  75.7 2.8 %shard_map.55 = (f32[8,32,128]{2,1,0:T(8,128)}, f32[8,32,128]{2,1,0:T(8,128)}) custom-call(f32[6,8,128]{2,1,0:T(8,128)S(1)} %get-tuple-element.39.own3, f32[6,8,128]{2,1,0:T(8,128)S(1)} %collective-permute-done.6.left3, f32[6,8,128]{2,1,0:T(8,128)S(1)} %collective-permute-done.7.right3, f32[24,8,128]{2,1,0:T(8,128)S(1)} %get-tuple-element.40.t2x, ...), custom_call_target="tpu_custom_call" | custom-call | tf_op jit(solution)/shard_map/pallas_call | solution.py:481
  (3 shorter events, 0.0 us)
Async XLA Ops:
  0.6 1.1 %copy-start = (f32[8,32,128]{2,1,0:T(8,128)S(1)}, f32[8,32,128]{2,1,0:T(8,128)}, u32[]{:S(2)}) copy-start(f32[8,32,128]{2,1,0:T(8,128)} %param.3) | copy-start | bytes 393220
  1.8 10.4 %collective-permute-start = (f32[20,32,128]{2,1,0:T(8,128)S(1)}, f32[20,32,128]{2,1,0:T(8,128)S(1)}, u32[]{:S(2)}, u32[]{:S(2)}) collective-permute-start(f32[20,32,128]{2,1,0:T(8,128)S(1)} %get-tuple-element.66.to_right), channel_id=1, source_target_pairs={{0,8},{8,16},{16,24},{24,32},{32,40},{40,48},{48,56},{56,64},{64,7... | collective-permute-start | bytes 983048 | tf_op jit(solution)/shard_map/ppermute | solution.py:434
  5.2 11.1 %collective-permute-start.1 = (f32[20,32,128]{2,1,0:T(8,128)S(1)}, f32[20,32,128]{2,1,0:T(8,128)S(1)}, u32[]{:S(2)}, u32[]{:S(2)}) collective-permute-start(f32[20,32,128]{2,1,0:T(8,128)S(1)} %get-tuple-element.67.to_left), channel_id=1, source_target_pairs={{8,0},{16,8},{24,16},{32,24},{40,32},{48,40},{56,48},{64,56},{72,6... | collective-permute-start | bytes 983048 | tf_op jit(solution)/shard_map/ppermute | solution.py:434
  16.4 8.6 %collective-permute-start.2 = (f32[62,8,128]{2,1,0:T(8,128)S(1)}, f32[62,8,128]{2,1,0:T(8,128)S(1)}, u32[]{:S(2)}, u32[]{:S(2)}) collective-permute-start(f32[62,8,128]{2,1,0:T(8,128)S(1)} %get-tuple-element.34), channel_id=1, source_target_pairs={{2,0},{4,2},{6,4},{3,1},{5,3},{7,5},{10,8},{12,10},{14,12},{11,9},... | collective-permute-start | bytes 761864 | tf_op jit(solution)/shard_map/ppermute | solution.py:434
  19.9 8.2 %collective-permute-start.3 = (f32[62,8,128]{2,1,0:T(8,128)S(1)}, f32[62,8,128]{2,1,0:T(8,128)S(1)}, u32[]{:S(2)}, u32[]{:S(2)}) collective-permute-start(f32[62,8,128]{2,1,0:T(8,128)S(1)} %get-tuple-element.35), channel_id=1, source_target_pairs={{0,2},{2,4},{4,6},{1,3},{3,5},{5,7},{8,10},{10,12},{12,14},{9,11},... | collective-permute-start | bytes 761864 | tf_op jit(solution)/shard_map/ppermute | solution.py:434
  45.8 11.3 %collective-permute-start.5 = (f32[29,8,128]{2,1,0:T(8,128)S(1)}, f32[29,8,128]{2,1,0:T(8,128)S(1)}, u32[]{:S(2)}, u32[]{:S(2)}) collective-permute-start(f32[29,8,128]{2,1,0:T(8,128)S(1)} %get-tuple-element.38), channel_id=1, source_target_pairs={{0,480},{8,488},{16,496},{24,504},{32,0},{40,8},{48,16},{56,24},{6... | collective-permute-start | bytes 356360 | tf_op jit(solution)/shard_map/ppermute | solution.py:439
  54.8 7.9 %collective-permute-start.4 = (f32[29,8,128]{2,1,0:T(8,128)S(1)}, f32[29,8,128]{2,1,0:T(8,128)S(1)}, u32[]{:S(2)}, u32[]{:S(2)}) collective-permute-start(f32[29,8,128]{2,1,0:T(8,128)S(1)} %get-tuple-element.37.own), channel_id=1, source_target_pairs={{0,32},{8,40},{16,48},{24,56},{32,64},{40,72},{48,80},{56,88},{64,... | collective-permute-start | bytes 356360 | tf_op jit(solution)/shard_map/ppermute | solution.py:439
  63.2 7.0 %collective-permute-start.7 = (f32[6,8,128]{2,1,0:T(8,128)S(1)}, f32[6,8,128]{2,1,0:T(8,128)S(1)}, u32[]{:S(2)}, u32[]{:S(2)}) collective-permute-start(f32[6,8,128]{2,1,0:T(8,128)S(1)} %get-tuple-element.39.own3), channel_id=1, source_target_pairs={{0,448},{8,456},{16,464},{24,472},{32,480},{40,488},{48,496},{56,5... | collective-permute-start | bytes 73736 | tf_op jit(solution)/shard_map/ppermute | solution.py:439
  66.9 8.8 %collective-permute-start.6 = (f32[6,8,128]{2,1,0:T(8,128)S(1)}, f32[6,8,128]{2,1,0:T(8,128)S(1)}, u32[]{:S(2)}, u32[]{:S(2)}) collective-permute-start(f32[6,8,128]{2,1,0:T(8,128)S(1)} %get-tuple-element.39.own3), channel_id=1, source_target_pairs={{0,64},{8,72},{16,80},{24,88},{32,96},{40,104},{48,112},{56,120},{... | collective-permute-start | bytes 73736 | tf_op jit(solution)/shard_map/ppermute | solution.py:439

commit v5 on v4

--- a/solution.py
+++ b/solution.py
@@ -149,6 +149,12 @@
     return t + swap(t, 2**level)
 
 
+def restrict_plane(ref, p, level):
+    half = ref.shape[1] // 2
+    t = ref[p, pl.ds(0, half, stride=2), :] + ref[p, pl.ds(1, half, stride=2), :]
+    return t + swap(t, 2**level)
+
+
 def restrict_packed(ref, p):
     t = ref[p] + ref[p + 1]
     t = t + swap(t, 1, 0)
@@ -161,58 +167,94 @@
     ref[p, pl.ds(1, half, stride=2), :] = e
 
 
-def fine_planes(to_left, to_right, xl, xr):
-    out = []
-    for at, edge, near in ((0, 8, 7), (8, 6, 6), (14, 6, 6)):
-        planes = []
-        for p in range(edge):
-            planes.append((8 - edge + p, xl, at + p, edge - p <= near))
-        for p in range(8):
-            if p < edge:
-                planes.append((8 + p, to_left, at + p, True))
-            else:
-                planes.append((8 + p, to_right, at + p - 8 + edge, True))
-        for p in range(edge):
-            planes.append((16 + p, xr, at + p, p < near))
-        out.append(planes)
-    return out
-
-
-def rows_kernel(to_left, to_right, xl, xr, up, down):
-    n = 0
-    for planes in fine_planes(to_left, to_right, xl, xr):
-        for _, ref, p, near in planes:
-            if near:
-                up[n] = ref[p, pl.ds(24, 8), :]
-                down[n] = ref[p, pl.ds(0, 8), :]
-                n += 1
+FINE_ROWS = 10 * 48
+MESSAGE_ROWS = FINE_ROWS + 3 * 24
+
+
+def with_rows(target, refs, above, below, at, first):
+    for p in range(8):
+        target[first + p, pl.ds(0, 32), :] = refs[p]
+        target[first + p, pl.ds(32, 8), :] = above[at + p]
+        target[first + p, pl.ds(40, 8), :] = below[at + p]
+
+
+def own_kernel(
+    k, f, s, above, below, to_left, to_right,
+    ke, fe, st, ve, re, tx, ty, tz, tzh, gain,
+):
+    for i, (target, ref) in enumerate(((ke, k), (fe, f), (st, s))):
+        with_rows(target, ref, above, below, 8 * i, 0)
+    op = Level(0, tx, ty, tz, tzh, st, gain)
+    op.build(ke, 1, 6)
+    op.first_sweep(ve, fe, 1, 6)
+    sides = ((to_left, (0, 1, 2, 3)), (to_right, (7, 6, 5, 4)))
+
+    def put(ref, n, v):
+        ref[pl.ds(48 * n, 48), :] = v
+
+    for ref, at in sides:
+        for n in range(3):
+            put(ref, n, ke[at[n]])
+        for n in range(2):
+            put(ref, 3 + n, fe[at[n]])
+            put(ref, 5 + n, st[at[n]])
+        put(ref, 7, ve[at[2]])
+    op.sweep(ve, fe, 2, 5)
+    for ref, at in sides:
+        put(ref, 8, ve[at[2]])
+        ve[at[1]] = jnp.zeros((48, 128), F32)
+    op.defect(re, ve, fe, 2, 5)
+    k1 = [restrict(ke, 2 * q, 48, 0) * 0.125 for q in range(4)]
+    s1 = [restrict(st, 2 * q, 48, 0) for q in (1, 2)]
+    for ref, at in sides:
+        put(ref, 9, re[at[2]])
+        far = k1[2:] if at[0] == 0 else k1[:2]
+        near, mid, last = (k1[1], s1[0], s1[1]) if at[0] == 0 else (k1[2], s1[1], s1[0])
+        share = restrict_plane(re, at[3], 0)
+        for n, v in enumerate((pack2(*far), pack2(near, mid), pack2(last, share))):
+            ref[pl.ds(FINE_ROWS + 24 * n, 24), :] = v
 
 
 def fine_kernel(
-    to_left, to_right, xl, xr, above, below,
+    k, f, s, above, below, xl, xr,
     slot, ve, re, tx, ty, tz, tzh, st, gain, t1x, t1y, t1z, t1h, s1, g1, f1,
     ke, fe, k1, v1, r1,
 ):
-    n = 0
     zero = jnp.zeros((8, 128), F32)
     sub = rows(zero)
-    for target, planes in zip((ke, fe, st), fine_planes(to_left, to_right, xl, xr)):
-        for at, ref, p, near in planes:
-            target[at, pl.ds(0, 32), :] = ref[p]
-            target[at, pl.ds(32, 8), :] = above[n] if near else zero
-            target[at, pl.ds(40, 8), :] = below[n] if near else zero
-            n += near
+    for i, (target, ref) in enumerate(((ke, k), (fe, f), (st, s))):
+        with_rows(target, ref, above, below, 8 * i, 8)
+    sides = ((xl, (7, 6, 5)), (xr, (16, 17, 18)))
+
+    def got(ref, n):
+        return ref[pl.ds(48 * n, 48), :]
+
+    for ref, at in sides:
+        for n in range(3):
+            ke[at[n]] = got(ref, n)
+        for n in range(2):
+            fe[at[n]] = got(ref, 3 + n)
+            st[at[n]] = got(ref, 5 + n)
+        ve[at[2]] = got(ref, 7)
     op = Level(0, tx, ty, tz, tzh, st, gain)
-    op.build(ke, 2, 21)
-    op.first_sweep(ve, fe, 2, 21)
-    op.sweep(ve, fe, 3, 20)
-    op.defect(re, ve, fe, 4, 19)
-    for q in range(12):
+    op.build(ke, 6, 17)
+    op.first_sweep(ve, fe, 6, 17)
+    op.sweep(ve, fe, 6, 17)
+    for ref, at in sides:
+        ve[at[2]] = got(ref, 8)
+    op.defect(re, ve, fe, 6, 17)
+    re[5] = got(xl, 9) + tx[6] * ve[6]
+    re[18] = got(xr, 9) + tx[18] * ve[17]
+    for q in range(3, 9):
         k1[q] = restrict(ke, 2 * q, 48, 0) * 0.125
-        if 1 <= q < 11:
-            s1[q] = restrict(st, 2 * q, 48, 0)
-        if 2 <= q < 10:
-            f1[q] = restrict(re, 2 * q, 48, 0)
+        s1[q] = restrict(st, 2 * q, 48, 0)
+        f1[q] = restrict(re, 2 * q, 48, 0)
+    for ref, lone, far, k2, s2 in ((xl, 5, (0, 1), 2, 1), (xr, 18, (10, 11), 9, 10)):
+        a, b, c = (split(ref[pl.ds(FINE_ROWS + 24 * n, 24), :], 1) for n in range(3))
+        k1[far[0]], k1[far[1]] = a
+        k1[k2], s1[k2] = b
+        s1[s2] = c[0]
+        f1[k2] = c[1] + restrict_plane(re, lone, 0)
     op = Level(1, t1x, t1y, t1z, t1h, s1, g1)
     op.build(k1, 1, 10)
     op.first_sweep(v1, f1, 2, 9)
@@ -441,20 +483,19 @@
 
 def body(permeability, storage, source_term):
     k, s, f = permeability, storage, source_term
-    to_left = jnp.concatenate([k, f[:6], s[:6]])
-    to_right = jnp.concatenate([k, f[2:], s[2:]])
-    xl = shifted(to_right, "gx", 1)
-    xr = shifted(to_left, "gx", -1)
-    planes = (to_left, to_right, xl, xr)
-    up, down = call(rows_kernel, [(62, 8, 128)] * 2, [], planes)
-    below = shifted(up, "gy", 1)
-    above = shifted(down, "gy", -1)
+    above = shifted(jnp.concatenate([k[:, :8], f[:, :8], s[:, :8]]), "gy", -1)
+    below = shifted(jnp.concatenate([k[:, 24:], f[:, 24:], s[:, 24:]]), "gy", 1)
+    own = (k, f, s, above, below)
+    to_left, to_right = call(
+        own_kernel, [(MESSAGE_ROWS, 128)] * 2, [(8, 48, 128)] * 10, own
+    )
+    xl, xr = shifted(to_right, "gx", 1), shifted(to_left, "gx", -1)
     fine, mid = (24, 48, 128), (12, 24, 128)
     slot, v0, r0, t0x, t0y, t0z, t0h, s0, g0, t1x, t1y, t1z, t1h, s1, g1, f1 = call(
         fine_kernel,
         [(16, 5, 8, 128)] + [fine] * 8 + [mid] * 7,
         [fine] * 2 + [mid] * 3,
-        planes + (above, below),
+        own + (xl, xr),
     )
     n = lax.axis_size("gx") * lax.axis_size("gy")
     groups = [[16 * a + b for b in range(16)] for a in range(n // 16)]

time: 78.9 us -> 75.4 us (0.956)
  waiting for transfers between devices: 27.1 us -> 23.3 us
  blocking collectives: 15.7 us -> 13.7 us
  starting transfers between devices: 28.1 us -> 30 us
    ppermute x4, waiting for transfers between devices: 15.6 us -> 11.8 us  [shifted(): lax.ppermute(x, axis, [(i, i + k) for i in range(n) if 0 <= i + k < n])]
    all_to_all x1, blocking collectives: 15.7 us -> 13.7 us  [body(): slots = lax.all_to_all(slot, ('gx', 'gy'), 0, 0, axis_index_groups=groups)]
    ppermute x4, starting transfers between devices: 10.6 us -> 12.4 us  [shifted(): lax.ppermute(x, axis, [(i, i + k) for i in range(n) if 0 <= i + k < n])]
    slice x1 -> x2, local copies, waits for them, and re-layouts: 1.1 us -> 1.6 us  [body(): below = shifted(jnp.concatenate([k[:, 24:], f[:, 24:], s[:, 24:]]), 'gy', 1)]
where the time goes in v5:
time: 75.4 us; the launch traced here: 75 us
  starting transfers between devices  30 us (40%)
  waiting for transfers between devices  23.3 us (31%)
  blocking collectives  13.7 us (18%)
  Pallas kernels  5.52 us (7%)
  local copies, waits for them, and re-layouts  1.72 us (2%)
  between operations  0.77 us (1%)
    ppermute x4, starting transfers between devices, turned(): return lax.ppermute(x, axis, [(i, (i + k) % n) for i in range(n)])  17.6 us
    all_to_all x1, blocking collectives, body(): slots = lax.all_to_all(slot, ('gx', 'gy'), 0, 0, axis_index_groups=groups)  13.7 us
    ppermute x4, starting transfers between devices, shifted(): lax.ppermute(x, axis, [(i, i + k) for i in range(n) if 0 <= i + k < n])  12.4 us
    ppermute x4, waiting for transfers between devices, shifted(): lax.ppermute(x, axis, [(i, i + k) for i in range(n) if 0 <= i + k < n])  11.8 us
    ppermute x4, waiting for transfers between devices, turned(): return lax.ppermute(x, axis, [(i, (i + k) % n) for i in range(n)])  11.5 us
    pallas_call x1, Pallas kernels, body(): pl.pallas_call(up_kernel, out_shape=[jax.ShapeDtypeStruct(own, F32)] * 2,...  2.82 us
    pallas_call x5, Pallas kernels, call(): pl.pallas_call(kernel, out_shape=[jax.ShapeDtypeStruct(s, F32) for s in o...  2.7 us
    slice x2, local copies, waits for them, and re-layouts, body(): below = shifted(jnp.concatenate([k[:, 24:], f[:, 24:], s[:, 24:]]), 'gy', 1)  1.6 us
  transfers between devices with their start and end apart: 8, of which 7 were waited for; matrix products, arithmetic and copies ran while one was open for 0% of the time, Pallas kernels for 0%

profile of v5, /device:TPU:8, one launch (start us, length us, event | category | flops | bytes accessed | tf_op | source)
XLA Modules:
  0.0 75.0 jit_solution(16622873491946145471)
XLA Ops:
  0.6 0.8 %fusion.2 = (f32[8,8,128]{2,1,0:T(8,128)S(1)}, f32[8,8,128]{2,1,0:T(8,128)S(1)}) fusion(f32[8,32,128]{2,1,0:T(8,128)} %s.3), kind=kLoop, calls=%fused_computation.4 | loop fusion | bytes 131072 | tf_op jit(solution)/shard_map/slice | solution.py:487
  1.6 0.8 %fusion = (f32[8,8,128]{2,1,0:T(8,128)S(1)}, f32[8,8,128]{2,1,0:T(8,128)S(1)}, f32[8,8,128]{2,1,0:T(8,128)S(1)}, f32[8,8,128]{2,1,0:T(8,128)S(1)}) fusion(f32[8,32,128]{2,1,0:T(8,128)S(1)} %copy-done.1, f32[8,32,128]{2,1,0:T(8,128)} %f.3), kind=kLoop, calls=%fused_computation.2 | loop fusion | bytes 262144 | tf_op jit(solution)/shard_map/slice | solution.py:487
  2.4 7.9 %collective-permute-start = (f32[24,8,128]{2,1,0:T(8,128)S(1)}, f32[24,8,128]{2,1,0:T(8,128)S(1)}, u32[]{:S(2)}, u32[]{:S(2)}) collective-permute-start(f32[24,8,128]{2,1,0:T(8,128)S(1)} %pad_maximum_fusion), channel_id=1, source_target_pairs={{2,0},{4,2},{6,4},{3,1},{5,3},{7,5},{10,8},{12,10},{14,12},{11,9},... | collective-permute-start | bytes 294920 | tf_op jit(solution)/shard_map/ppermute | solution.py:476
  10.3 1.9 %collective-permute-start.1 = (f32[24,8,128]{2,1,0:T(8,128)S(1)}, f32[24,8,128]{2,1,0:T(8,128)S(1)}, u32[]{:S(2)}, u32[]{:S(2)}) collective-permute-start(f32[24,8,128]{2,1,0:T(8,128)S(1)} %pad_maximum_fusion.1), channel_id=1, source_target_pairs={{0,2},{2,4},{4,6},{1,3},{3,5},{5,7},{8,10},{10,12},{12,14},{9,11},... | collective-permute-start | bytes 294920 | tf_op jit(solution)/shard_map/ppermute | solution.py:476
  12.2 0.2 collective-permute-done.above
  12.5 4.3 %collective-permute-done.1.below = f32[24,8,128]{2,1,0:T(8,128)S(1)} collective-permute-done((f32[24,8,128]{2,1,0:T(8,128)S(1)}, f32[24,8,128]{2,1,0:T(8,128)S(1)}, u32[]{:S(2)}, u32[]{:S(2)}) %collective-permute-start.1) | collective-permute-done | bytes 98336 | tf_op jit(solution)/shard_map/ppermute | solution.py:476
  16.8 0.4 shard_map.50
  17.2 1.3 %collective-permute-start.2 = (f32[552,128]{1,0:T(8,128)S(1)}, f32[552,128]{1,0:T(8,128)S(1)}, u32[]{:S(2)}, u32[]{:S(2)}) collective-permute-start(f32[552,128]{1,0:T(8,128)S(1)} %get-tuple-element.34), channel_id=1, source_target_pairs={{0,8},{8,16},{16,24},{24,32},{32,40},{40,48},{48,56},{56,64},{64,7... | collective-permute-start | bytes 847880 | tf_op jit(solution)/shard_map/ppermute | solution.py:476
  18.5 1.3 %collective-permute-start.3 = (f32[552,128]{1,0:T(8,128)S(1)}, f32[552,128]{1,0:T(8,128)S(1)}, u32[]{:S(2)}, u32[]{:S(2)}) collective-permute-start(f32[552,128]{1,0:T(8,128)S(1)} %get-tuple-element.35), channel_id=1, source_target_pairs={{8,0},{16,8},{24,16},{32,24},{40,32},{48,40},{56,48},{64,56},{72,6... | collective-permute-start | bytes 847880 | tf_op jit(solution)/shard_map/ppermute | solution.py:476
  19.8 2.8 %collective-permute-done.2.xl = f32[552,128]{1,0:T(8,128)S(1)} collective-permute-done((f32[552,128]{1,0:T(8,128)S(1)}, f32[552,128]{1,0:T(8,128)S(1)}, u32[]{:S(2)}, u32[]{:S(2)}) %collective-permute-start.2) | collective-permute-done | bytes 282656 | tf_op jit(solution)/shard_map/ppermute | solution.py:476
  22.6 4.4 %collective-permute-done.3.xr = f32[552,128]{1,0:T(8,128)S(1)} collective-permute-done((f32[552,128]{1,0:T(8,128)S(1)}, f32[552,128]{1,0:T(8,128)S(1)}, u32[]{:S(2)}, u32[]{:S(2)}) %collective-permute-start.3) | collective-permute-done | bytes 282656 | tf_op jit(solution)/shard_map/ppermute | solution.py:476
  27.0 1.4 %shard_map.51 = (f32[16,5,8,128]{3,2,1,0:T(8,128)S(1)}, f32[24,48,128]{2,1,0:T(8,128)S(1)}, f32[24,48,128]{2,1,0:T(8,128)S(1)}, f32[24,48,128]{2,1,0:T(8,128)S(1...) custom-call(f32[8,32,128]{2,1,0:T(8,128)S(1)} %copy-done.1, ...), custom_call_target="tpu_custom_call" | custom-call | tf_op jit(solution)/shard_map/pallas_call | solution.py:466
  28.4 13.7 %all_to_all.5.g.slots = f32[16,5,8,128]{3,2,1,0:T(8,128)S(1)} all-to-all(f32[16,5,8,128]{3,2,1,0:T(8,128)S(1)} %get-tuple-element.36), channel_id=1, replica_groups={{0,2,4,6,8,10,12,14,16,18,20,22,24,26,28,30},{32,34,36,38,40,42,44,46,4..., dimensions={0} | all-to-all | bytes 655360 | tf_op jit(solution)/shard_map/all_to_all | solution.py:502
  42.1 0.2 shard_map.52
  42.3 8.9 %collective-permute-start.5 = (f32[29,8,128]{2,1,0:T(8,128)S(1)}, f32[29,8,128]{2,1,0:T(8,128)S(1)}, u32[]{:S(2)}, u32[]{:S(2)}) collective-permute-start(f32[29,8,128]{2,1,0:T(8,128)S(1)} %get-tuple-element.38), channel_id=1, source_target_pairs={{0,480},{8,488},{16,496},{24,504},{32,0},{40,8},{48,16},{56,24},{6... | collective-permute-start | bytes 356360 | tf_op jit(solution)/shard_map/ppermute | solution.py:481
  51.2 1.9 %collective-permute-start.4 = (f32[29,8,128]{2,1,0:T(8,128)S(1)}, f32[29,8,128]{2,1,0:T(8,128)S(1)}, u32[]{:S(2)}, u32[]{:S(2)}) collective-permute-start(f32[29,8,128]{2,1,0:T(8,128)S(1)} %get-tuple-element.37.own), channel_id=1, source_target_pairs={{0,32},{8,40},{16,48},{24,56},{32,64},{40,72},{48,80},{56,88},{64,... | collective-permute-start | bytes 356360 | tf_op jit(solution)/shard_map/ppermute | solution.py:481
  53.1 0.5 collective-permute-done.5.nxt
  53.6 5.6 %collective-permute-done.4.prev = f32[29,8,128]{2,1,0:T(8,128)S(1)} collective-permute-done((f32[29,8,128]{2,1,0:T(8,128)S(1)}, f32[29,8,128]{2,1,0:T(8,128)S(1)}, u32[]{:S(2)}, u32[]{:S(2)}) %collective-permute-start.4) | collective-permute-done | bytes 118816 | tf_op jit(solution)/shard_map/ppermute | solution.py:481
  59.1 0.5 shard_map.53
  59.6 3.7 %collective-permute-start.7 = (f32[6,8,128]{2,1,0:T(8,128)S(1)}, f32[6,8,128]{2,1,0:T(8,128)S(1)}, u32[]{:S(2)}, u32[]{:S(2)}) collective-permute-start(f32[6,8,128]{2,1,0:T(8,128)S(1)} %get-tuple-element.39.own3), channel_id=1, source_target_pairs={{0,448},{8,456},{16,464},{24,472},{32,480},{40,488},{48,496},{56,5... | collective-permute-start | bytes 73736 | tf_op jit(solution)/shard_map/ppermute | solution.py:481
  63.4 3.0 %collective-permute-start.6 = (f32[6,8,128]{2,1,0:T(8,128)S(1)}, f32[6,8,128]{2,1,0:T(8,128)S(1)}, u32[]{:S(2)}, u32[]{:S(2)}) collective-permute-start(f32[6,8,128]{2,1,0:T(8,128)S(1)} %get-tuple-element.39.own3), channel_id=1, source_target_pairs={{0,64},{8,72},{16,80},{24,88},{32,96},{40,104},{48,112},{56,120},{... | collective-permute-start | bytes 73736 | tf_op jit(solution)/shard_map/ppermute | solution.py:481
  66.4 0.3 shard_map.54
  66.7 5.5 %collective-permute-done.6.left3 = f32[6,8,128]{2,1,0:T(8,128)S(1)} collective-permute-done((f32[6,8,128]{2,1,0:T(8,128)S(1)}, f32[6,8,128]{2,1,0:T(8,128)S(1)}, u32[]{:S(2)}, u32[]{:S(2)}) %collective-permute-start.6) | collective-permute-done | bytes 24608 | tf_op jit(solution)/shard_map/ppermute | solution.py:481
  72.1 2.8 %shard_map.55 = (f32[8,32,128]{2,1,0:T(8,128)}, f32[8,32,128]{2,1,0:T(8,128)}) custom-call(f32[6,8,128]{2,1,0:T(8,128)S(1)} %get-tuple-element.39.own3, f32[6,8,128]{2,1,0:T(8,128)S(1)} %collective-permute-done.6.left3, f32[6,8,128]{2,1,0:T(8,128)S(1)} %collective-permute-done.7.right3, f32[24,8,128]{2,1,0:T(8,128)S(1)} %get-tuple-element.40.t2x, ...), custom_call_target="tpu_custom_call" | custom-call | tf_op jit(solution)/shard_map/pallas_call | solution.py:522
  (9 shorter events, 0.1 us)
Async XLA Ops:
  0.6 0.9 %copy-start.1 = (f32[8,32,128]{2,1,0:T(8,128)S(1)}, f32[8,32,128]{2,1,0:T(8,128)}, u32[]{:S(2)}) copy-start(f32[8,32,128]{2,1,0:T(8,128)} %k.3) | copy-start | bytes 393220
  2.4 14.4 %copy-start.2 = (f32[8,32,128]{2,1,0:T(8,128)S(1)}, f32[8,32,128]{2,1,0:T(8,128)}, u32[]{:S(2)}) copy-start(f32[8,32,128]{2,1,0:T(8,128)} %f.3) | copy-start | bytes 393220
  2.4 14.4 %copy-start = (f32[8,32,128]{2,1,0:T(8,128)S(1)}, f32[8,32,128]{2,1,0:T(8,128)}, u32[]{:S(2)}) copy-start(f32[8,32,128]{2,1,0:T(8,128)} %s.3) | copy-start | bytes 393220
  2.4 10.1 %collective-permute-start = (f32[24,8,128]{2,1,0:T(8,128)S(1)}, f32[24,8,128]{2,1,0:T(8,128)S(1)}, u32[]{:S(2)}, u32[]{:S(2)}) collective-permute-start(f32[24,8,128]{2,1,0:T(8,128)S(1)} %pad_maximum_fusion), channel_id=1, source_target_pairs={{2,0},{4,2},{6,4},{3,1},{5,3},{7,5},{10,8},{12,10},{14,12},{11,9},... | collective-permute-start | bytes 294920 | tf_op jit(solution)/shard_map/ppermute | solution.py:476
  10.3 6.5 %collective-permute-start.1 = (f32[24,8,128]{2,1,0:T(8,128)S(1)}, f32[24,8,128]{2,1,0:T(8,128)S(1)}, u32[]{:S(2)}, u32[]{:S(2)}) collective-permute-start(f32[24,8,128]{2,1,0:T(8,128)S(1)} %pad_maximum_fusion.1), channel_id=1, source_target_pairs={{0,2},{2,4},{4,6},{1,3},{3,5},{5,7},{8,10},{10,12},{12,14},{9,11},... | collective-permute-start | bytes 294920 | tf_op jit(solution)/shard_map/ppermute | solution.py:476
  17.2 5.4 %collective-permute-start.2 = (f32[552,128]{1,0:T(8,128)S(1)}, f32[552,128]{1,0:T(8,128)S(1)}, u32[]{:S(2)}, u32[]{:S(2)}) collective-permute-start(f32[552,128]{1,0:T(8,128)S(1)} %get-tuple-element.34), channel_id=1, source_target_pairs={{0,8},{8,16},{16,24},{24,32},{32,40},{40,48},{48,56},{56,64},{64,7... | collective-permute-start | bytes 847880 | tf_op jit(solution)/shard_map/ppermute | solution.py:476
  18.5 8.5 %collective-permute-start.3 = (f32[552,128]{1,0:T(8,128)S(1)}, f32[552,128]{1,0:T(8,128)S(1)}, u32[]{:S(2)}, u32[]{:S(2)}) collective-permute-start(f32[552,128]{1,0:T(8,128)S(1)} %get-tuple-element.35), channel_id=1, source_target_pairs={{8,0},{16,8},{24,16},{32,24},{40,32},{48,40},{56,48},{64,56},{72,6... | collective-permute-start | bytes 847880 | tf_op jit(solution)/shard_map/ppermute | solution.py:476
  42.3 11.3 %collective-permute-start.5 = (f32[29,8,128]{2,1,0:T(8,128)S(1)}, f32[29,8,128]{2,1,0:T(8,128)S(1)}, u32[]{:S(2)}, u32[]{:S(2)}) collective-permute-start(f32[29,8,128]{2,1,0:T(8,128)S(1)} %get-tuple-element.38), channel_id=1, source_target_pairs={{0,480},{8,488},{16,496},{24,504},{32,0},{40,8},{48,16},{56,24},{6... | collective-permute-start | bytes 356360 | tf_op jit(solution)/shard_map/ppermute | solution.py:481
  51.2 7.9 %collective-permute-start.4 = (f32[29,8,128]{2,1,0:T(8,128)S(1)}, f32[29,8,128]{2,1,0:T(8,128)S(1)}, u32[]{:S(2)}, u32[]{:S(2)}) collective-permute-start(f32[29,8,128]{2,1,0:T(8,128)S(1)} %get-tuple-element.37.own), channel_id=1, source_target_pairs={{0,32},{8,40},{16,48},{24,56},{32,64},{40,72},{48,80},{56,88},{64,... | collective-permute-start | bytes 356360 | tf_op jit(solution)/shard_map/ppermute | solution.py:481
  59.6 7.0 %collective-permute-start.7 = (f32[6,8,128]{2,1,0:T(8,128)S(1)}, f32[6,8,128]{2,1,0:T(8,128)S(1)}, u32[]{:S(2)}, u32[]{:S(2)}) collective-permute-start(f32[6,8,128]{2,1,0:T(8,128)S(1)} %get-tuple-element.39.own3), channel_id=1, source_target_pairs={{0,448},{8,456},{16,464},{24,472},{32,480},{40,488},{48,496},{56,5... | collective-permute-start | bytes 73736 | tf_op jit(solution)/shard_map/ppermute | solution.py:481
  63.4 8.8 %collective-permute-start.6 = (f32[6,8,128]{2,1,0:T(8,128)S(1)}, f32[6,8,128]{2,1,0:T(8,128)S(1)}, u32[]{:S(2)}, u32[]{:S(2)}) collective-permute-start(f32[6,8,128]{2,1,0:T(8,128)S(1)} %get-tuple-element.39.own3), channel_id=1, source_target_pairs={{0,64},{8,72},{16,80},{24,88},{32,96},{40,104},{48,112},{56,120},{... | collective-permute-start | bytes 73736 | tf_op jit(solution)/shard_map/ppermute | solution.py:481

commit v6 on v5

--- a/solution.py
+++ b/solution.py
@@ -288,7 +288,12 @@
         slot[4 * x + before, 2 + n] = jnp.where(sub < 4, r, roll(f, 4, 0))
 
 
-def ring_kernel(g, to_next, to_prev):
+EDGE = 19
+TO_NEXT = ((2, 6), (1, 7), (2, 6))
+TO_PREV = ((0, 6), (0, 7), (0, 6))
+
+
+def ring_kernel(g, own, to_next, to_prev):
     for x in range(4):
         t = [g[4 * x + j, 0] for j in range(4)]
         e0, o0 = exchange(t[0], t[1], 1)
@@ -300,33 +305,40 @@
         e1, o1 = exchange(t[2], t[3], 1)
         s0 = jnp.where(bit(e0, 2), e0, e1)
         s1 = jnp.where(bit(o0, 2), o0, o1)
-        for out in (to_next, to_prev):
-            for at, v in ((0, f0), (1, f1), (8, k0), (9, k1), (16, s0), (17, s1)):
-                out[at + 2 * x] = v
+        for at, v in ((0, f0), (1, f1), (8, k0), (9, k1), (16, s0), (17, s1)):
+            own[at + 2 * x] = v
+    for out, parts in ((to_next, TO_NEXT), (to_prev, TO_PREV)):
+        n = 0
+        for i, (first, count) in enumerate(parts):
+            for p in range(first, first + count):
+                out[n] = own[8 * i + p]
+                n += 1
     j = lax.axis_index("gy")
     x = lax.axis_index("gx") % 4
     for out, step in ((to_next, 3), (to_prev, 1)):
         at = 4 * ((x + step) % 4)
         for i in range(3):
-            out[24 + i] = g[at + j, 2 + i]
-        out[27] = g[at + (j + 1) % 4, 2]
-        out[28] = g[at + (j + 3) % 4, 2]
+            out[EDGE + i] = g[at + j, 2 + i]
+        out[EDGE + 3] = g[at + (j + 1) % 4, 2]
+        out[EDGE + 4] = g[at + (j + 3) % 4, 2]
 
 
 def coarse_kernel(
     prev, own, nxt, msg, tx, ty, tyh, tz, tzh, st, gain, v2, r2, ke, fe
 ):
-    for b, ref in enumerate((prev, own, nxt)):
-        for p in range(8):
-            fe[8 * b + p] = ref[p]
-            ke[8 * b + p] = ref[8 + p]
-            st[8 * b + p] = ref[16 + p]
+    whole = ((0, 8),) * 3
+    for b, (ref, parts) in enumerate(((prev, TO_NEXT), (own, whole), (nxt, TO_PREV))):
+        n = 0
+        for target, (first, count) in zip((fe, ke, st), parts):
+            for p in range(first, first + count):
+                target[8 * b + p] = ref[n]
+                n += 1
     op = Level(2, tx, ty, tz, tzh, st, gain, tyh)
     z = lax.axis_index("gx") // 4
-    op.build(ke, 1, 22, 8 * z - 8, 2 * lax.axis_size("gx"))
-    op.first_sweep(v2, fe, 1, 22)
-    op.sweep(v2, fe, 2, 21)
-    op.defect(r2, v2, fe, 3, 20)
+    op.build(ke, 2, 21, 8 * z - 8, 2 * lax.axis_size("gx"))
+    op.first_sweep(v2, fe, 2, 21)
+    op.sweep(v2, fe, 3, 20)
+    op.defect(r2, v2, fe, 4, 19)
     for i, (ref, scale) in enumerate(((r2, None), (ke, 0.125), (st, None))):
         cells = [restrict_packed(ref, 4 + 2 * c) for c in range(8)]
         if scale is not None:
@@ -348,7 +360,7 @@
         inside = (x + step >= 0) & (x + step < 4)
         tiles = ((j, 2), (j, 3), (j, 4), (after, 2), (before, 2))
         return [
-            split(jnp.where(inside, slots[at + y, t], outer[24 + n]), 1)
+            split(jnp.where(inside, slots[at + y, t], outer[EDGE + n]), 1)
             for n, (y, t) in enumerate(tiles)
         ]
 
@@ -481,10 +493,19 @@
     return lax.ppermute(x, axis, [(i, (i + k) % n) for i in range(n)])
 
 
+def stacked(*parts):
+    out = jnp.zeros((sum(p.shape[0] for p in parts),) + parts[0].shape[1:], F32)
+    at = 0
+    for p in parts:
+        out = lax.dynamic_update_slice(out, p, (at, 0, 0))
+        at += p.shape[0]
+    return out
+
+
 def body(permeability, storage, source_term):
     k, s, f = permeability, storage, source_term
-    above = shifted(jnp.concatenate([k[:, :8], f[:, :8], s[:, :8]]), "gy", -1)
-    below = shifted(jnp.concatenate([k[:, 24:], f[:, 24:], s[:, 24:]]), "gy", 1)
+    above = shifted(stacked(k[:, :8], f[:, :8], s[:, :8]), "gy", -1)
+    below = shifted(stacked(k[:, 24:], f[:, 24:], s[:, 24:]), "gy", 1)
     own = (k, f, s, above, below)
     to_left, to_right = call(
         own_kernel, [(MESSAGE_ROWS, 128)] * 2, [(8, 48, 128)] * 10, own
@@ -500,11 +521,11 @@
     n = lax.axis_size("gx") * lax.axis_size("gy")
     groups = [[16 * a + b for b in range(16)] for a in range(n // 16)]
     slots = lax.all_to_all(slot, ("gx", "gy"), 0, 0, axis_index_groups=groups)
-    to_next, to_prev = call(ring_kernel, [(29, 8, 128)] * 2, [], (slots,))
+    ring, to_next, to_prev = call(ring_kernel, [(24, 8, 128)] * 3, [], (slots,))
     prev, nxt = turned(to_next, "gx", 4), turned(to_prev, "gx", -4)
     low = (24, 8, 128)
     msg3, t2x, t2y, t2yh, t2z, t2h, s2, g2, v2, r2 = call(
-        coarse_kernel, [(6, 8, 128)] + [low] * 9, [low] * 2, (prev, to_next, nxt)
+        coarse_kernel, [(6, 8, 128)] + [low] * 9, [low] * 2, (prev, ring, nxt)
     )
     w1, q1 = call(
         halo_kernel, [mid] * 2, [mid], (slots, prev, nxt, f1, t1x, t1y, t1z, t1h, s1, g1)

time: 75.4 us -> 73.8 us (0.979)
  waiting for transfers between devices: 23.3 us -> 17.4 us
  blocking collectives: 13.7 us -> 16.4 us
  starting transfers between devices: 30 us -> 31.6 us
    ppermute x4, waiting for transfers between devices: 11.5 us -> 7.82 us  [turned(): return lax.ppermute(x, axis, [(i, (i + k) % n) for i in range(n)])]
    all_to_all x1, blocking collectives: 13.7 us -> 16.4 us  [body(): slots = lax.all_to_all(slot, ('gx', 'gy'), 0, 0, axis_index_groups=groups)]
    ppermute x4, waiting for transfers between devices: 11.8 us -> 9.56 us  [shifted(): lax.ppermute(x, axis, [(i, i + k) for i in range(n) if 0 <= i + k < n])]
    ppermute x4, starting transfers between devices: 17.6 us -> 19.1 us  [turned(): return lax.ppermute(x, axis, [(i, (i + k) % n) for i in range(n)])]
    slice x2 -> x1, local copies, waits for them, and re-layouts: 1.6 us -> 0.78 us  [body(): below = shifted(stacked(k[:, 24:], f[:, 24:], s[:, 24:]), 'gy', 1)]
    unnamed x6, local copies, waits for them, and re-layouts: 0.12 us -> 0.93 us
where the time goes in v6:
time: 73.8 us; the launch traced here: 73.3 us
  starting transfers between devices  31.6 us (43%)
  waiting for transfers between devices  17.4 us (24%)
  blocking collectives  16.4 us (22%)
  Pallas kernels  5.52 us (7%)
  local copies, waits for them, and re-layouts  1.74 us (2%)
  between operations  0.75 us (1%)
    ppermute x4, starting transfers between devices, turned(): return lax.ppermute(x, axis, [(i, (i + k) % n) for i in range(n)])  19.1 us
    all_to_all x1, blocking collectives, body(): slots = lax.all_to_all(slot, ('gx', 'gy'), 0, 0, axis_index_groups=groups)  16.4 us
    ppermute x4, starting transfers between devices, shifted(): lax.ppermute(x, axis, [(i, i + k) for i in range(n) if 0 <= i + k < n])  12.5 us
    ppermute x4, waiting for transfers between devices, shifted(): lax.ppermute(x, axis, [(i, i + k) for i in range(n) if 0 <= i + k < n])  9.56 us
    ppermute x4, waiting for transfers between devices, turned(): return lax.ppermute(x, axis, [(i, (i + k) % n) for i in range(n)])  7.82 us
    pallas_call x1, Pallas kernels, body(): pl.pallas_call(up_kernel, out_shape=[jax.ShapeDtypeStruct(own, F32)] * 2,...  2.81 us
    pallas_call x5, Pallas kernels, call(): pl.pallas_call(kernel, out_shape=[jax.ShapeDtypeStruct(s, F32) for s in o...  2.7 us
  transfers between devices with their start and end apart: 8, of which 7 were waited for; matrix products, arithmetic and copies ran while one was open for 0% of the time, Pallas kernels for 0%

profile of v6, /device:TPU:8, one launch (start us, length us, event | category | flops | bytes accessed | tf_op | source)
XLA Modules:
  0.0 73.3 jit_solution(12020011270136380424)
XLA Ops:
  0.6 0.8 %fusion = (f32[8,8,128]{2,1,0:T(8,128)S(1)}, f32[8,8,128]{2,1,0:T(8,128)S(1)}) fusion(f32[8,32,128]{2,1,0:T(8,128)} %k.3), kind=kLoop, calls=%fused_computation.4 | loop fusion | bytes 131072 | tf_op jit(solution)/shard_map/slice | solution.py:508
  1.5 0.9 %copy-done.1 = f32[8,32,128]{2,1,0:T(8,128)S(1)} copy-done((f32[8,32,128]{2,1,0:T(8,128)S(1)}, f32[8,32,128]{2,1,0:T(8,128)}, u32[]{:S(2)}) %copy-start.1) | copy-done | bytes 131096
  2.4 3.5 %collective-permute-start.1 = (f32[24,8,128]{2,1,0:T(8,128)S(1)}, f32[24,8,128]{2,1,0:T(8,128)S(1)}, u32[]{:S(2)}, u32[]{:S(2)}) collective-permute-start(f32[24,8,128]{2,1,0:T(8,128)S(1)} %get-tuple-element.68), channel_id=1, source_target_pairs={{0,2},{2,4},{4,6},{1,3},{3,5},{5,7},{8,10},{10,12},{12,14},{9,11},... | collective-permute-start | bytes 294920 | tf_op jit(solution)/shard_map/ppermute | solution.py:488
  5.9 5.5 %collective-permute-start = (f32[24,8,128]{2,1,0:T(8,128)S(1)}, f32[24,8,128]{2,1,0:T(8,128)S(1)}, u32[]{:S(2)}, u32[]{:S(2)}) collective-permute-start(f32[24,8,128]{2,1,0:T(8,128)S(1)} %get-tuple-element.69), channel_id=1, source_target_pairs={{2,0},{4,2},{6,4},{3,1},{5,3},{7,5},{10,8},{12,10},{14,12},{11,9},... | collective-permute-start | bytes 294920 | tf_op jit(solution)/shard_map/ppermute | solution.py:488
  11.4 0.7 collective-permute-done.1.below
  12.1 1.5 %collective-permute-done.above = f32[24,8,128]{2,1,0:T(8,128)S(1)} collective-permute-done((f32[24,8,128]{2,1,0:T(8,128)S(1)}, f32[24,8,128]{2,1,0:T(8,128)S(1)}, u32[]{:S(2)}, u32[]{:S(2)}) %collective-permute-start) | collective-permute-done | bytes 98336 | tf_op jit(solution)/shard_map/ppermute | solution.py:488
  13.6 0.4 shard_map.50
  14.1 2.2 %collective-permute-start.2 = (f32[552,128]{1,0:T(8,128)S(1)}, f32[552,128]{1,0:T(8,128)S(1)}, u32[]{:S(2)}, u32[]{:S(2)}) collective-permute-start(f32[552,128]{1,0:T(8,128)S(1)} %get-tuple-element.35), channel_id=1, source_target_pairs={{0,8},{8,16},{16,24},{24,32},{32,40},{40,48},{48,56},{56,64},{64,7... | collective-permute-start | bytes 847880 | tf_op jit(solution)/shard_map/ppermute | solution.py:488
  16.2 1.3 %collective-permute-start.3 = (f32[552,128]{1,0:T(8,128)S(1)}, f32[552,128]{1,0:T(8,128)S(1)}, u32[]{:S(2)}, u32[]{:S(2)}) collective-permute-start(f32[552,128]{1,0:T(8,128)S(1)} %get-tuple-element.36), channel_id=1, source_target_pairs={{8,0},{16,8},{24,16},{32,24},{40,32},{48,40},{56,48},{64,56},{72,6... | collective-permute-start | bytes 847880 | tf_op jit(solution)/shard_map/ppermute | solution.py:488
  17.5 3.2 %collective-permute-done.2.xl = f32[552,128]{1,0:T(8,128)S(1)} collective-permute-done((f32[552,128]{1,0:T(8,128)S(1)}, f32[552,128]{1,0:T(8,128)S(1)}, u32[]{:S(2)}, u32[]{:S(2)}) %collective-permute-start.2) | collective-permute-done | bytes 282656 | tf_op jit(solution)/shard_map/ppermute | solution.py:488
  20.8 4.1 %collective-permute-done.3.xr = f32[552,128]{1,0:T(8,128)S(1)} collective-permute-done((f32[552,128]{1,0:T(8,128)S(1)}, f32[552,128]{1,0:T(8,128)S(1)}, u32[]{:S(2)}, u32[]{:S(2)}) %collective-permute-start.3) | collective-permute-done | bytes 282656 | tf_op jit(solution)/shard_map/ppermute | solution.py:488
  24.9 1.4 %shard_map.51 = (f32[16,5,8,128]{3,2,1,0:T(8,128)S(1)}, f32[24,48,128]{2,1,0:T(8,128)S(1)}, f32[24,48,128]{2,1,0:T(8,128)S(1)}, f32[24,48,128]{2,1,0:T(8,128)S(1...) custom-call(f32[8,32,128]{2,1,0:T(8,128)S(1)} %copy-done, ...), custom_call_target="tpu_custom_call" | custom-call | tf_op jit(solution)/shard_map/pallas_call | solution.py:478
  26.3 16.4 %all_to_all.5.g.slots = f32[16,5,8,128]{3,2,1,0:T(8,128)S(1)} all-to-all(f32[16,5,8,128]{3,2,1,0:T(8,128)S(1)} %get-tuple-element.37), channel_id=1, replica_groups={{0,2,4,6,8,10,12,14,16,18,20,22,24,26,28,30},{32,34,36,38,40,42,44,46,4..., dimensions={0} | all-to-all | bytes 655360 | tf_op jit(solution)/shard_map/all_to_all | solution.py:523
  42.7 0.2 shard_map.52
  42.8 3.8 %collective-permute-start.4 = (f32[24,8,128]{2,1,0:T(8,128)S(1)}, f32[24,8,128]{2,1,0:T(8,128)S(1)}, u32[]{:S(2)}, u32[]{:S(2)}) collective-permute-start(f32[24,8,128]{2,1,0:T(8,128)S(1)} %get-tuple-element.38), channel_id=1, source_target_pairs={{0,32},{8,40},{16,48},{24,56},{32,64},{40,72},{48,80},{56,88},{64,... | collective-permute-start | bytes 294920 | tf_op jit(solution)/shard_map/ppermute | solution.py:493
  46.7 7.0 %collective-permute-start.5 = (f32[24,8,128]{2,1,0:T(8,128)S(1)}, f32[24,8,128]{2,1,0:T(8,128)S(1)}, u32[]{:S(2)}, u32[]{:S(2)}) collective-permute-start(f32[24,8,128]{2,1,0:T(8,128)S(1)} %get-tuple-element.40), channel_id=1, source_target_pairs={{0,480},{8,488},{16,496},{24,504},{32,0},{40,8},{48,16},{56,24},{6... | collective-permute-start | bytes 294920 | tf_op jit(solution)/shard_map/ppermute | solution.py:493
  53.7 0.7 collective-permute-done.4.prev
  54.3 1.5 %collective-permute-done.5.nxt = f32[24,8,128]{2,1,0:T(8,128)S(1)} collective-permute-done((f32[24,8,128]{2,1,0:T(8,128)S(1)}, f32[24,8,128]{2,1,0:T(8,128)S(1)}, u32[]{:S(2)}, u32[]{:S(2)}) %collective-permute-start.5) | collective-permute-done | bytes 98336 | tf_op jit(solution)/shard_map/ppermute | solution.py:493
  55.9 0.5 shard_map.53
  56.4 6.3 %collective-permute-start.7 = (f32[6,8,128]{2,1,0:T(8,128)S(1)}, f32[6,8,128]{2,1,0:T(8,128)S(1)}, u32[]{:S(2)}, u32[]{:S(2)}) collective-permute-start(f32[6,8,128]{2,1,0:T(8,128)S(1)} %get-tuple-element.41.own3), channel_id=1, source_target_pairs={{0,448},{8,456},{16,464},{24,472},{32,480},{40,488},{48,496},{56,5... | collective-permute-start | bytes 73736 | tf_op jit(solution)/shard_map/ppermute | solution.py:493
  62.7 1.9 %collective-permute-start.6 = (f32[6,8,128]{2,1,0:T(8,128)S(1)}, f32[6,8,128]{2,1,0:T(8,128)S(1)}, u32[]{:S(2)}, u32[]{:S(2)}) collective-permute-start(f32[6,8,128]{2,1,0:T(8,128)S(1)} %get-tuple-element.41.own3), channel_id=1, source_target_pairs={{0,64},{8,72},{16,80},{24,88},{32,96},{40,104},{48,112},{56,120},{... | collective-permute-start | bytes 73736 | tf_op jit(solution)/shard_map/ppermute | solution.py:493
  64.6 0.3 shard_map.54
  64.9 5.6 %collective-permute-done.6.left3 = f32[6,8,128]{2,1,0:T(8,128)S(1)} collective-permute-done((f32[6,8,128]{2,1,0:T(8,128)S(1)}, f32[6,8,128]{2,1,0:T(8,128)S(1)}, u32[]{:S(2)}, u32[]{:S(2)}) %collective-permute-start.6) | collective-permute-done | bytes 24608 | tf_op jit(solution)/shard_map/ppermute | solution.py:493
  70.5 2.8 %shard_map.55 = (f32[8,32,128]{2,1,0:T(8,128)}, f32[8,32,128]{2,1,0:T(8,128)}) custom-call(f32[6,8,128]{2,1,0:T(8,128)S(1)} %get-tuple-element.41.own3, f32[6,8,128]{2,1,0:T(8,128)S(1)} %collective-permute-done.6.left3, f32[6,8,128]{2,1,0:T(8,128)S(1)} %collective-permute-done.7.right3, f32[24,8,128]{2,1,0:T(8,128)S(1)} %get-tuple-element.42.t2x, ...), custom_call_target="tpu_custom_call" | custom-call | tf_op jit(solution)/shard_map/pallas_call | solution.py:543
  (10 shorter events, 0.1 us)
Async XLA Ops:
  1.4 0.9 %copy-start.1 = (f32[8,32,128]{2,1,0:T(8,128)S(1)}, f32[8,32,128]{2,1,0:T(8,128)}, u32[]{:S(2)}) copy-start(f32[8,32,128]{2,1,0:T(8,128)} %f.3) | copy-start | bytes 393220
  1.4 1.0 %copy-start.2 = (f32[8,32,128]{2,1,0:T(8,128)S(1)}, f32[8,32,128]{2,1,0:T(8,128)}, u32[]{:S(2)}) copy-start(f32[8,32,128]{2,1,0:T(8,128)} %s.3) | copy-start | bytes 393220
  2.3 11.3 %copy-start = (f32[8,32,128]{2,1,0:T(8,128)S(1)}, f32[8,32,128]{2,1,0:T(8,128)}, u32[]{:S(2)}) copy-start(f32[8,32,128]{2,1,0:T(8,128)} %k.3) | copy-start | bytes 393220
  2.4 9.7 %collective-permute-start.1 = (f32[24,8,128]{2,1,0:T(8,128)S(1)}, f32[24,8,128]{2,1,0:T(8,128)S(1)}, u32[]{:S(2)}, u32[]{:S(2)}) collective-permute-start(f32[24,8,128]{2,1,0:T(8,128)S(1)} %get-tuple-element.68), channel_id=1, source_target_pairs={{0,2},{2,4},{4,6},{1,3},{3,5},{5,7},{8,10},{10,12},{12,14},{9,11},... | collective-permute-start | bytes 294920 | tf_op jit(solution)/shard_map/ppermute | solution.py:488
  5.9 7.7 %collective-permute-start = (f32[24,8,128]{2,1,0:T(8,128)S(1)}, f32[24,8,128]{2,1,0:T(8,128)S(1)}, u32[]{:S(2)}, u32[]{:S(2)}) collective-permute-start(f32[24,8,128]{2,1,0:T(8,128)S(1)} %get-tuple-element.69), channel_id=1, source_target_pairs={{2,0},{4,2},{6,4},{3,1},{5,3},{7,5},{10,8},{12,10},{14,12},{11,9},... | collective-permute-start | bytes 294920 | tf_op jit(solution)/shard_map/ppermute | solution.py:488
  14.1 6.7 %collective-permute-start.2 = (f32[552,128]{1,0:T(8,128)S(1)}, f32[552,128]{1,0:T(8,128)S(1)}, u32[]{:S(2)}, u32[]{:S(2)}) collective-permute-start(f32[552,128]{1,0:T(8,128)S(1)} %get-tuple-element.35), channel_id=1, source_target_pairs={{0,8},{8,16},{16,24},{24,32},{32,40},{40,48},{48,56},{56,64},{64,7... | collective-permute-start | bytes 847880 | tf_op jit(solution)/shard_map/ppermute | solution.py:488
  16.2 8.7 %collective-permute-start.3 = (f32[552,128]{1,0:T(8,128)S(1)}, f32[552,128]{1,0:T(8,128)S(1)}, u32[]{:S(2)}, u32[]{:S(2)}) collective-permute-start(f32[552,128]{1,0:T(8,128)S(1)} %get-tuple-element.36), channel_id=1, source_target_pairs={{8,0},{16,8},{24,16},{32,24},{40,32},{48,40},{56,48},{64,56},{72,6... | collective-permute-start | bytes 847880 | tf_op jit(solution)/shard_map/ppermute | solution.py:488
  42.8 11.5 %collective-permute-start.4 = (f32[24,8,128]{2,1,0:T(8,128)S(1)}, f32[24,8,128]{2,1,0:T(8,128)S(1)}, u32[]{:S(2)}, u32[]{:S(2)}) collective-permute-start(f32[24,8,128]{2,1,0:T(8,128)S(1)} %get-tuple-element.38), channel_id=1, source_target_pairs={{0,32},{8,40},{16,48},{24,56},{32,64},{40,72},{48,80},{56,88},{64,... | collective-permute-start | bytes 294920 | tf_op jit(solution)/shard_map/ppermute | solution.py:493
  46.7 9.2 %collective-permute-start.5 = (f32[24,8,128]{2,1,0:T(8,128)S(1)}, f32[24,8,128]{2,1,0:T(8,128)S(1)}, u32[]{:S(2)}, u32[]{:S(2)}) collective-permute-start(f32[24,8,128]{2,1,0:T(8,128)S(1)} %get-tuple-element.40), channel_id=1, source_target_pairs={{0,480},{8,488},{16,496},{24,504},{32,0},{40,8},{48,16},{56,24},{6... | collective-permute-start | bytes 294920 | tf_op jit(solution)/shard_map/ppermute | solution.py:493
  56.4 8.5 %collective-permute-start.7 = (f32[6,8,128]{2,1,0:T(8,128)S(1)}, f32[6,8,128]{2,1,0:T(8,128)S(1)}, u32[]{:S(2)}, u32[]{:S(2)}) collective-permute-start(f32[6,8,128]{2,1,0:T(8,128)S(1)} %get-tuple-element.41.own3), channel_id=1, source_target_pairs={{0,448},{8,456},{16,464},{24,472},{32,480},{40,488},{48,496},{56,5... | collective-permute-start | bytes 73736 | tf_op jit(solution)/shard_map/ppermute | solution.py:493
  62.7 7.8 %collective-permute-start.6 = (f32[6,8,128]{2,1,0:T(8,128)S(1)}, f32[6,8,128]{2,1,0:T(8,128)S(1)}, u32[]{:S(2)}, u32[]{:S(2)}) collective-permute-start(f32[6,8,128]{2,1,0:T(8,128)S(1)} %get-tuple-element.41.own3), channel_id=1, source_target_pairs={{0,64},{8,72},{16,80},{24,88},{32,96},{40,104},{48,112},{56,120},{... | collective-permute-start | bytes 73736 | tf_op jit(solution)/shard_map/ppermute | solution.py:493

commit v7 on v6

--- a/solution.py
+++ b/solution.py
@@ -493,20 +493,13 @@
     return lax.ppermute(x, axis, [(i, (i + k) % n) for i in range(n)])
 
 
-def stacked(*parts):
-    out = jnp.zeros((sum(p.shape[0] for p in parts),) + parts[0].shape[1:], F32)
-    at = 0
-    for p in parts:
-        out = lax.dynamic_update_slice(out, p, (at, 0, 0))
-        at += p.shape[0]
-    return out
-
-
 def body(permeability, storage, source_term):
     k, s, f = permeability, storage, source_term
-    above = shifted(stacked(k[:, :8], f[:, :8], s[:, :8]), "gy", -1)
-    below = shifted(stacked(k[:, 24:], f[:, 24:], s[:, 24:]), "gy", 1)
-    own = (k, f, s, above, below)
+    parts = (f[:, :8], s[:, :8], f[:, 24:], s[:, 24:])
+    (fa, sa, fb, sb), kk = lax.optimization_barrier((parts, k))
+    above = shifted(jnp.concatenate([kk[:, :8], fa, sa]), "gy", -1)
+    below = shifted(jnp.concatenate([kk[:, 24:], fb, sb]), "gy", 1)
+    own = (kk, f, s, above, below)
     to_left, to_right = call(
         own_kernel, [(MESSAGE_ROWS, 128)] * 2, [(8, 48, 128)] * 10, own
     )

time: 73.8 us -> 72.4 us (0.981)
  blocking collectives: 16.4 us -> 13.7 us
  waiting for transfers between devices: 17.4 us -> 19.6 us
  local copies, waits for them, and re-layouts: 1.74 us -> 0.97 us
    all_to_all x1, blocking collectives: 16.4 us -> 13.7 us  [body(): slots = lax.all_to_all(slot, ('gx', 'gy'), 0, 0, axis_index_groups=groups)]
    ppermute x4, waiting for transfers between devices: 9.56 us -> 11.8 us  [shifted(): lax.ppermute(x, axis, [(i, i + k) for i in range(n) if 0 <= i + k < n])]
    unnamed x6, local copies, waits for them, and re-layouts: 0.93 us -> 0.11 us
where the time goes in v7:
time: 72.4 us; the launch traced here: 72 us
  starting transfers between devices  31.5 us (44%)
  waiting for transfers between devices  19.6 us (27%)
  blocking collectives  13.7 us (19%)
  Pallas kernels  5.52 us (8%)
  local copies, waits for them, and re-layouts  0.97 us (1%)
  between operations  0.76 us (1%)
    ppermute x4, starting transfers between devices, turned(): return lax.ppermute(x, axis, [(i, (i + k) % n) for i in range(n)])  19.1 us
    all_to_all x1, blocking collectives, body(): slots = lax.all_to_all(slot, ('gx', 'gy'), 0, 0, axis_index_groups=groups)  13.7 us
    ppermute x4, starting transfers between devices, shifted(): lax.ppermute(x, axis, [(i, i + k) for i in range(n) if 0 <= i + k < n])  12.4 us
    ppermute x4, waiting for transfers between devices, shifted(): lax.ppermute(x, axis, [(i, i + k) for i in range(n) if 0 <= i + k < n])  11.8 us
    ppermute x4, waiting for transfers between devices, turned(): return lax.ppermute(x, axis, [(i, (i + k) % n) for i in range(n)])  7.82 us
    pallas_call x1, Pallas kernels, body(): pl.pallas_call(up_kernel, out_shape=[jax.ShapeDtypeStruct(own, F32)] * 2,...  2.81 us
    pallas_call x5, Pallas kernels, call(): pl.pallas_call(kernel, out_shape=[jax.ShapeDtypeStruct(s, F32) for s in o...  2.7 us
  transfers between devices with their start and end apart: 8, of which 7 were waited for; matrix products, arithmetic and copies ran while one was open for 0% of the time, Pallas kernels for 0%

profile of v7, /device:TPU:8, one launch (start us, length us, event | category | flops | bytes accessed | tf_op | source)
XLA Modules:
  0.0 72.0 jit_solution(11677452210467809420)
XLA Ops:
  0.6 0.9 %fusion.1 = (f32[8,8,128]{2,1,0:T(8,128)S(1)}, f32[8,8,128]{2,1,0:T(8,128)S(1)}, f32[8,8,128]{2,1,0:T(8,128)S(1)}, f32[8,8,128]{2,1,0:T(8,128)S(1)}) fusion(f32[8,32,128]{2,1,0:T(8,128)} %s.3, f32[8,32,128]{2,1,0:T(8,128)} %f.3), kind=kLoop, calls=%fused_computation.3 | loop fusion | bytes 262144 | tf_op jit(solution)/shard_map/slice | solution.py:498
  1.5 0.1 copy-done
  1.6 7.9 %collective-permute-start = (f32[24,8,128]{2,1,0:T(8,128)S(1)}, f32[24,8,128]{2,1,0:T(8,128)S(1)}, u32[]{:S(2)}, u32[]{:S(2)}) collective-permute-start(f32[24,8,128]{2,1,0:T(8,128)S(1)} %pad_maximum_fusion), channel_id=1, source_target_pairs={{2,0},{4,2},{6,4},{3,1},{5,3},{7,5},{10,8},{12,10},{14,12},{11,9},... | collective-permute-start | bytes 294920 | tf_op jit(solution)/shard_map/ppermute | solution.py:488
  9.5 1.9 %collective-permute-start.1 = (f32[24,8,128]{2,1,0:T(8,128)S(1)}, f32[24,8,128]{2,1,0:T(8,128)S(1)}, u32[]{:S(2)}, u32[]{:S(2)}) collective-permute-start(f32[24,8,128]{2,1,0:T(8,128)S(1)} %pad_maximum_fusion.1), channel_id=1, source_target_pairs={{0,2},{2,4},{4,6},{1,3},{3,5},{5,7},{8,10},{10,12},{12,14},{9,11},... | collective-permute-start | bytes 294920 | tf_op jit(solution)/shard_map/ppermute | solution.py:488
  11.4 0.2 collective-permute-done.above
  11.7 4.3 %collective-permute-done.1.below = f32[24,8,128]{2,1,0:T(8,128)S(1)} collective-permute-done((f32[24,8,128]{2,1,0:T(8,128)S(1)}, f32[24,8,128]{2,1,0:T(8,128)S(1)}, u32[]{:S(2)}, u32[]{:S(2)}) %collective-permute-start.1) | collective-permute-done | bytes 98336 | tf_op jit(solution)/shard_map/ppermute | solution.py:488
  16.0 0.4 shard_map.50
  16.5 1.3 %collective-permute-start.2 = (f32[552,128]{1,0:T(8,128)S(1)}, f32[552,128]{1,0:T(8,128)S(1)}, u32[]{:S(2)}, u32[]{:S(2)}) collective-permute-start(f32[552,128]{1,0:T(8,128)S(1)} %get-tuple-element.45), channel_id=1, source_target_pairs={{0,8},{8,16},{16,24},{24,32},{32,40},{40,48},{48,56},{56,64},{64,7... | collective-permute-start | bytes 847880 | tf_op jit(solution)/shard_map/ppermute | solution.py:488
  17.8 1.3 %collective-permute-start.3 = (f32[552,128]{1,0:T(8,128)S(1)}, f32[552,128]{1,0:T(8,128)S(1)}, u32[]{:S(2)}, u32[]{:S(2)}) collective-permute-start(f32[552,128]{1,0:T(8,128)S(1)} %get-tuple-element.46), channel_id=1, source_target_pairs={{8,0},{16,8},{24,16},{32,24},{40,32},{48,40},{56,48},{64,56},{72,6... | collective-permute-start | bytes 847880 | tf_op jit(solution)/shard_map/ppermute | solution.py:488
  19.1 2.8 %collective-permute-done.2.xl = f32[552,128]{1,0:T(8,128)S(1)} collective-permute-done((f32[552,128]{1,0:T(8,128)S(1)}, f32[552,128]{1,0:T(8,128)S(1)}, u32[]{:S(2)}, u32[]{:S(2)}) %collective-permute-start.2) | collective-permute-done | bytes 282656 | tf_op jit(solution)/shard_map/ppermute | solution.py:488
  21.9 4.4 %collective-permute-done.3.xr = f32[552,128]{1,0:T(8,128)S(1)} collective-permute-done((f32[552,128]{1,0:T(8,128)S(1)}, f32[552,128]{1,0:T(8,128)S(1)}, u32[]{:S(2)}, u32[]{:S(2)}) %collective-permute-start.3) | collective-permute-done | bytes 282656 | tf_op jit(solution)/shard_map/ppermute | solution.py:488
  26.3 1.4 %shard_map.51 = (f32[16,5,8,128]{3,2,1,0:T(8,128)S(1)}, f32[24,48,128]{2,1,0:T(8,128)S(1)}, f32[24,48,128]{2,1,0:T(8,128)S(1)}, f32[24,48,128]{2,1,0:T(8,128)S(1...) custom-call(f32[8,32,128]{2,1,0:T(8,128)S(1)} %copy-done, ...), custom_call_target="tpu_custom_call" | custom-call | tf_op jit(solution)/shard_map/pallas_call | solution.py:478
  27.7 13.7 %all_to_all.5.g.slots = f32[16,5,8,128]{3,2,1,0:T(8,128)S(1)} all-to-all(f32[16,5,8,128]{3,2,1,0:T(8,128)S(1)} %get-tuple-element.47), channel_id=1, replica_groups={{0,2,4,6,8,10,12,14,16,18,20,22,24,26,28,30},{32,34,36,38,40,42,44,46,4..., dimensions={0} | all-to-all | bytes 655360 | tf_op jit(solution)/shard_map/all_to_all | solution.py:516
  41.4 0.2 shard_map.52
  41.5 3.8 %collective-permute-start.4 = (f32[24,8,128]{2,1,0:T(8,128)S(1)}, f32[24,8,128]{2,1,0:T(8,128)S(1)}, u32[]{:S(2)}, u32[]{:S(2)}) collective-permute-start(f32[24,8,128]{2,1,0:T(8,128)S(1)} %get-tuple-element.48), channel_id=1, source_target_pairs={{0,32},{8,40},{16,48},{24,56},{32,64},{40,72},{48,80},{56,88},{64,... | collective-permute-start | bytes 294920 | tf_op jit(solution)/shard_map/ppermute | solution.py:493
  45.3 7.0 %collective-permute-start.5 = (f32[24,8,128]{2,1,0:T(8,128)S(1)}, f32[24,8,128]{2,1,0:T(8,128)S(1)}, u32[]{:S(2)}, u32[]{:S(2)}) collective-permute-start(f32[24,8,128]{2,1,0:T(8,128)S(1)} %get-tuple-element.50), channel_id=1, source_target_pairs={{0,480},{8,488},{16,496},{24,504},{32,0},{40,8},{48,16},{56,24},{6... | collective-permute-start | bytes 294920 | tf_op jit(solution)/shard_map/ppermute | solution.py:493
  52.4 0.7 collective-permute-done.4.prev
  53.0 1.5 %collective-permute-done.5.nxt = f32[24,8,128]{2,1,0:T(8,128)S(1)} collective-permute-done((f32[24,8,128]{2,1,0:T(8,128)S(1)}, f32[24,8,128]{2,1,0:T(8,128)S(1)}, u32[]{:S(2)}, u32[]{:S(2)}) %collective-permute-start.5) | collective-permute-done | bytes 98336 | tf_op jit(solution)/shard_map/ppermute | solution.py:493
  54.6 0.5 shard_map.53
  55.0 6.3 %collective-permute-start.7 = (f32[6,8,128]{2,1,0:T(8,128)S(1)}, f32[6,8,128]{2,1,0:T(8,128)S(1)}, u32[]{:S(2)}, u32[]{:S(2)}) collective-permute-start(f32[6,8,128]{2,1,0:T(8,128)S(1)} %get-tuple-element.51.own3), channel_id=1, source_target_pairs={{0,448},{8,456},{16,464},{24,472},{32,480},{40,488},{48,496},{56,5... | collective-permute-start | bytes 73736 | tf_op jit(solution)/shard_map/ppermute | solution.py:493
  61.4 1.9 %collective-permute-start.6 = (f32[6,8,128]{2,1,0:T(8,128)S(1)}, f32[6,8,128]{2,1,0:T(8,128)S(1)}, u32[]{:S(2)}, u32[]{:S(2)}) collective-permute-start(f32[6,8,128]{2,1,0:T(8,128)S(1)} %get-tuple-element.51.own3), channel_id=1, source_target_pairs={{0,64},{8,72},{16,80},{24,88},{32,96},{40,104},{48,112},{56,120},{... | collective-permute-start | bytes 73736 | tf_op jit(solution)/shard_map/ppermute | solution.py:493
  63.3 0.3 shard_map.54
  63.6 5.6 %collective-permute-done.6.left3 = f32[6,8,128]{2,1,0:T(8,128)S(1)} collective-permute-done((f32[6,8,128]{2,1,0:T(8,128)S(1)}, f32[6,8,128]{2,1,0:T(8,128)S(1)}, u32[]{:S(2)}, u32[]{:S(2)}) %collective-permute-start.6) | collective-permute-done | bytes 24608 | tf_op jit(solution)/shard_map/ppermute | solution.py:493
  69.2 2.8 %shard_map.55 = (f32[8,32,128]{2,1,0:T(8,128)}, f32[8,32,128]{2,1,0:T(8,128)}) custom-call(f32[6,8,128]{2,1,0:T(8,128)S(1)} %get-tuple-element.51.own3, f32[6,8,128]{2,1,0:T(8,128)S(1)} %collective-permute-done.6.left3, f32[6,8,128]{2,1,0:T(8,128)S(1)} %collective-permute-done.7.right3, f32[24,8,128]{2,1,0:T(8,128)S(1)} %get-tuple-element.52.t2x, ...), custom_call_target="tpu_custom_call" | custom-call | tf_op jit(solution)/shard_map/pallas_call | solution.py:536
  (9 shorter events, 0.0 us)
Async XLA Ops:
  0.6 1.0 %copy-start = (f32[8,32,128]{2,1,0:T(8,128)S(1)}, f32[8,32,128]{2,1,0:T(8,128)}, u32[]{:S(2)}) copy-start(f32[8,32,128]{2,1,0:T(8,128)} %k.1) | copy-start | bytes 393220
  1.6 14.4 %copy-start.2 = (f32[8,32,128]{2,1,0:T(8,128)S(1)}, f32[8,32,128]{2,1,0:T(8,128)}, u32[]{:S(2)}) copy-start(f32[8,32,128]{2,1,0:T(8,128)} %s.3) | copy-start | bytes 393220
  1.6 14.4 %copy-start.1 = (f32[8,32,128]{2,1,0:T(8,128)S(1)}, f32[8,32,128]{2,1,0:T(8,128)}, u32[]{:S(2)}) copy-start(f32[8,32,128]{2,1,0:T(8,128)} %f.3) | copy-start | bytes 393220
  1.6 10.1 %collective-permute-start = (f32[24,8,128]{2,1,0:T(8,128)S(1)}, f32[24,8,128]{2,1,0:T(8,128)S(1)}, u32[]{:S(2)}, u32[]{:S(2)}) collective-permute-start(f32[24,8,128]{2,1,0:T(8,128)S(1)} %pad_maximum_fusion), channel_id=1, source_target_pairs={{2,0},{4,2},{6,4},{3,1},{5,3},{7,5},{10,8},{12,10},{14,12},{11,9},... | collective-permute-start | bytes 294920 | tf_op jit(solution)/shard_map/ppermute | solution.py:488
  9.5 6.5 %collective-permute-start.1 = (f32[24,8,128]{2,1,0:T(8,128)S(1)}, f32[24,8,128]{2,1,0:T(8,128)S(1)}, u32[]{:S(2)}, u32[]{:S(2)}) collective-permute-start(f32[24,8,128]{2,1,0:T(8,128)S(1)} %pad_maximum_fusion.1), channel_id=1, source_target_pairs={{0,2},{2,4},{4,6},{1,3},{3,5},{5,7},{8,10},{10,12},{12,14},{9,11},... | collective-permute-start | bytes 294920 | tf_op jit(solution)/shard_map/ppermute | solution.py:488
  16.5 5.4 %collective-permute-start.2 = (f32[552,128]{1,0:T(8,128)S(1)}, f32[552,128]{1,0:T(8,128)S(1)}, u32[]{:S(2)}, u32[]{:S(2)}) collective-permute-start(f32[552,128]{1,0:T(8,128)S(1)} %get-tuple-element.45), channel_id=1, source_target_pairs={{0,8},{8,16},{16,24},{24,32},{32,40},{40,48},{48,56},{56,64},{64,7... | collective-permute-start | bytes 847880 | tf_op jit(solution)/shard_map/ppermute | solution.py:488
  17.8 8.5 %collective-permute-start.3 = (f32[552,128]{1,0:T(8,128)S(1)}, f32[552,128]{1,0:T(8,128)S(1)}, u32[]{:S(2)}, u32[]{:S(2)}) collective-permute-start(f32[552,128]{1,0:T(8,128)S(1)} %get-tuple-element.46), channel_id=1, source_target_pairs={{8,0},{16,8},{24,16},{32,24},{40,32},{48,40},{56,48},{64,56},{72,6... | collective-permute-start | bytes 847880 | tf_op jit(solution)/shard_map/ppermute | solution.py:488
  41.5 11.5 %collective-permute-start.4 = (f32[24,8,128]{2,1,0:T(8,128)S(1)}, f32[24,8,128]{2,1,0:T(8,128)S(1)}, u32[]{:S(2)}, u32[]{:S(2)}) collective-permute-start(f32[24,8,128]{2,1,0:T(8,128)S(1)} %get-tuple-element.48), channel_id=1, source_target_pairs={{0,32},{8,40},{16,48},{24,56},{32,64},{40,72},{48,80},{56,88},{64,... | collective-permute-start | bytes 294920 | tf_op jit(solution)/shard_map/ppermute | solution.py:493
  45.3 9.2 %collective-permute-start.5 = (f32[24,8,128]{2,1,0:T(8,128)S(1)}, f32[24,8,128]{2,1,0:T(8,128)S(1)}, u32[]{:S(2)}, u32[]{:S(2)}) collective-permute-start(f32[24,8,128]{2,1,0:T(8,128)S(1)} %get-tuple-element.50), channel_id=1, source_target_pairs={{0,480},{8,488},{16,496},{24,504},{32,0},{40,8},{48,16},{56,24},{6... | collective-permute-start | bytes 294920 | tf_op jit(solution)/shard_map/ppermute | solution.py:493
  55.0 8.5 %collective-permute-start.7 = (f32[6,8,128]{2,1,0:T(8,128)S(1)}, f32[6,8,128]{2,1,0:T(8,128)S(1)}, u32[]{:S(2)}, u32[]{:S(2)}) collective-permute-start(f32[6,8,128]{2,1,0:T(8,128)S(1)} %get-tuple-element.51.own3), channel_id=1, source_target_pairs={{0,448},{8,456},{16,464},{24,472},{32,480},{40,488},{48,496},{56,5... | collective-permute-start | bytes 73736 | tf_op jit(solution)/shard_map/ppermute | solution.py:493
  61.4 7.8 %collective-permute-start.6 = (f32[6,8,128]{2,1,0:T(8,128)S(1)}, f32[6,8,128]{2,1,0:T(8,128)S(1)}, u32[]{:S(2)}, u32[]{:S(2)}) collective-permute-start(f32[6,8,128]{2,1,0:T(8,128)S(1)} %get-tuple-element.51.own3), channel_id=1, source_target_pairs={{0,64},{8,72},{16,80},{24,88},{32,96},{40,104},{48,112},{56,120},{... | collective-permute-start | bytes 73736 | tf_op jit(solution)/shard_map/ppermute | solution.py:493

commit v8 on v7

--- a/solution.py
+++ b/solution.py
@@ -167,7 +167,7 @@
     ref[p, pl.ds(1, half, stride=2), :] = e
 
 
-FINE_ROWS = 10 * 48
+FINE_ROWS = 8 * 48 + 2 * 40
 MESSAGE_ROWS = FINE_ROWS + 3 * 24
 
 
@@ -192,6 +192,11 @@
     def put(ref, n, v):
         ref[pl.ds(48 * n, 48), :] = v
 
+    def put_near(ref, n, v):
+        at = 8 * 48 + 40 * n
+        ref[pl.ds(at, 32), :] = v[:32]
+        ref[pl.ds(at + 32, 8), :] = jnp.where(rows(v[:8]) < 4, v[32:40], v[40:])
+
     for ref, at in sides:
         for n in range(3):
             put(ref, n, ke[at[n]])
@@ -201,13 +206,13 @@
         put(ref, 7, ve[at[2]])
     op.sweep(ve, fe, 2, 5)
     for ref, at in sides:
-        put(ref, 8, ve[at[2]])
+        put_near(ref, 0, ve[at[2]])
         ve[at[1]] = jnp.zeros((48, 128), F32)
     op.defect(re, ve, fe, 2, 5)
     k1 = [restrict(ke, 2 * q, 48, 0) * 0.125 for q in range(4)]
     s1 = [restrict(st, 2 * q, 48, 0) for q in (1, 2)]
     for ref, at in sides:
-        put(ref, 9, re[at[2]])
+        put_near(ref, 1, re[at[2]])
         far = k1[2:] if at[0] == 0 else k1[:2]
         near, mid, last = (k1[1], s1[0], s1[1]) if at[0] == 0 else (k1[2], s1[1], s1[0])
         share = restrict_plane(re, at[3], 0)
@@ -228,6 +233,11 @@
 
     def got(ref, n):
         return ref[pl.ds(48 * n, 48), :]
+
+    def got_near(ref, n):
+        at = 8 * 48 + 40 * n
+        halo = ref[pl.ds(at + 32, 8), :]
+        return jnp.concatenate([ref[pl.ds(at, 32), :], halo, halo], axis=0)
 
     for ref, at in sides:
         for n in range(3):
@@ -241,10 +251,10 @@
     op.first_sweep(ve, fe, 6, 17)
     op.sweep(ve, fe, 6, 17)
     for ref, at in sides:
-        ve[at[2]] = got(ref, 8)
+        ve[at[2]] = got_near(ref, 0)
     op.defect(re, ve, fe, 6, 17)
-    re[5] = got(xl, 9) + tx[6] * ve[6]
-    re[18] = got(xr, 9) + tx[18] * ve[17]
+    re[5] = got_near(xl, 1) + tx[6] * ve[6]
+    re[18] = got_near(xr, 1) + tx[18] * ve[17]
     for q in range(3, 9):
         k1[q] = restrict(ke, 2 * q, 48, 0) * 0.125
         s1[q] = restrict(st, 2 * q, 48, 0)

time: 72.4 us -> 72.2 us (level)
  no operation moved by 1% of the time
where the time goes in v8:
time: 72.2 us; the launch traced here: 71.8 us
  starting transfers between devices  31.5 us (44%)
  waiting for transfers between devices  19.5 us (27%)
  blocking collectives  13.6 us (19%)
  Pallas kernels  5.51 us (8%)
  local copies, waits for them, and re-layouts  0.97 us (1%)
  between operations  0.76 us (1%)
    ppermute x4, starting transfers between devices, turned(): return lax.ppermute(x, axis, [(i, (i + k) % n) for i in range(n)])  19.1 us
    all_to_all x1, blocking collectives, body(): slots = lax.all_to_all(slot, ('gx', 'gy'), 0, 0, axis_index_groups=groups)  13.6 us
    ppermute x4, starting transfers between devices, shifted(): lax.ppermute(x, axis, [(i, i + k) for i in range(n) if 0 <= i + k < n])  12.4 us
    ppermute x4, waiting for transfers between devices, shifted(): lax.ppermute(x, axis, [(i, i + k) for i in range(n) if 0 <= i + k < n])  11.7 us
    ppermute x4, waiting for transfers between devices, turned(): return lax.ppermute(x, axis, [(i, (i + k) % n) for i in range(n)])  7.82 us
    pallas_call x1, Pallas kernels, body(): pl.pallas_call(up_kernel, out_shape=[jax.ShapeDtypeStruct(own, F32)] * 2,...  2.81 us
    pallas_call x5, Pallas kernels, call(): pl.pallas_call(kernel, out_shape=[jax.ShapeDtypeStruct(s, F32) for s in o...  2.7 us
  transfers between devices with their start and end apart: 8, of which 7 were waited for; matrix products, arithmetic and copies ran while one was open for 0% of the time, Pallas kernels for 0%

profile of v8, /device:TPU:8, one launch (start us, length us, event | category | flops | bytes accessed | tf_op | source)
XLA Modules:
  0.0 71.8 jit_solution(15243966343767688378)
XLA Ops:
  0.6 0.9 %fusion.1 = (f32[8,8,128]{2,1,0:T(8,128)S(1)}, f32[8,8,128]{2,1,0:T(8,128)S(1)}, f32[8,8,128]{2,1,0:T(8,128)S(1)}, f32[8,8,128]{2,1,0:T(8,128)S(1)}) fusion(f32[8,32,128]{2,1,0:T(8,128)} %s.3, f32[8,32,128]{2,1,0:T(8,128)} %f.3), kind=kLoop, calls=%fused_computation.3 | loop fusion | bytes 262144 | tf_op jit(solution)/shard_map/slice | solution.py:508
  1.5 0.1 copy-done
  1.6 7.9 %collective-permute-start = (f32[24,8,128]{2,1,0:T(8,128)S(1)}, f32[24,8,128]{2,1,0:T(8,128)S(1)}, u32[]{:S(2)}, u32[]{:S(2)}) collective-permute-start(f32[24,8,128]{2,1,0:T(8,128)S(1)} %pad_maximum_fusion), channel_id=1, source_target_pairs={{2,0},{4,2},{6,4},{3,1},{5,3},{7,5},{10,8},{12,10},{14,12},{11,9},... | collective-permute-start | bytes 294920 | tf_op jit(solution)/shard_map/ppermute | solution.py:498
  9.5 1.9 %collective-permute-start.1 = (f32[24,8,128]{2,1,0:T(8,128)S(1)}, f32[24,8,128]{2,1,0:T(8,128)S(1)}, u32[]{:S(2)}, u32[]{:S(2)}) collective-permute-start(f32[24,8,128]{2,1,0:T(8,128)S(1)} %pad_maximum_fusion.1), channel_id=1, source_target_pairs={{0,2},{2,4},{4,6},{1,3},{3,5},{5,7},{8,10},{10,12},{12,14},{9,11},... | collective-permute-start | bytes 294920 | tf_op jit(solution)/shard_map/ppermute | solution.py:498
  11.4 0.2 collective-permute-done.above
  11.7 4.3 %collective-permute-done.1.below = f32[24,8,128]{2,1,0:T(8,128)S(1)} collective-permute-done((f32[24,8,128]{2,1,0:T(8,128)S(1)}, f32[24,8,128]{2,1,0:T(8,128)S(1)}, u32[]{:S(2)}, u32[]{:S(2)}) %collective-permute-start.1) | collective-permute-done | bytes 98336 | tf_op jit(solution)/shard_map/ppermute | solution.py:498
  16.0 0.4 shard_map.50
  16.5 1.3 %collective-permute-start.2 = (f32[536,128]{1,0:T(8,128)S(1)}, f32[536,128]{1,0:T(8,128)S(1)}, u32[]{:S(2)}, u32[]{:S(2)}) collective-permute-start(f32[536,128]{1,0:T(8,128)S(1)} %get-tuple-element.45), channel_id=1, source_target_pairs={{0,8},{8,16},{16,24},{24,32},{32,40},{40,48},{48,56},{56,64},{64,7... | collective-permute-start | bytes 823304 | tf_op jit(solution)/shard_map/ppermute | solution.py:498
  17.8 1.3 %collective-permute-start.3 = (f32[536,128]{1,0:T(8,128)S(1)}, f32[536,128]{1,0:T(8,128)S(1)}, u32[]{:S(2)}, u32[]{:S(2)}) collective-permute-start(f32[536,128]{1,0:T(8,128)S(1)} %get-tuple-element.46), channel_id=1, source_target_pairs={{8,0},{16,8},{24,16},{32,24},{40,32},{48,40},{56,48},{64,56},{72,6... | collective-permute-start | bytes 823304 | tf_op jit(solution)/shard_map/ppermute | solution.py:498
  19.1 2.7 %collective-permute-done.2.xl = f32[536,128]{1,0:T(8,128)S(1)} collective-permute-done((f32[536,128]{1,0:T(8,128)S(1)}, f32[536,128]{1,0:T(8,128)S(1)}, u32[]{:S(2)}, u32[]{:S(2)}) %collective-permute-start.2) | collective-permute-done | bytes 274464 | tf_op jit(solution)/shard_map/ppermute | solution.py:498
  21.8 4.4 %collective-permute-done.3.xr = f32[536,128]{1,0:T(8,128)S(1)} collective-permute-done((f32[536,128]{1,0:T(8,128)S(1)}, f32[536,128]{1,0:T(8,128)S(1)}, u32[]{:S(2)}, u32[]{:S(2)}) %collective-permute-start.3) | collective-permute-done | bytes 274464 | tf_op jit(solution)/shard_map/ppermute | solution.py:498
  26.2 1.4 %shard_map.51 = (f32[16,5,8,128]{3,2,1,0:T(8,128)S(1)}, f32[24,48,128]{2,1,0:T(8,128)S(1)}, f32[24,48,128]{2,1,0:T(8,128)S(1)}, f32[24,48,128]{2,1,0:T(8,128)S(1...) custom-call(f32[8,32,128]{2,1,0:T(8,128)S(1)} %copy-done, ...), custom_call_target="tpu_custom_call" | custom-call | tf_op jit(solution)/shard_map/pallas_call | solution.py:488
  27.6 13.6 %all_to_all.5.g.slots = f32[16,5,8,128]{3,2,1,0:T(8,128)S(1)} all-to-all(f32[16,5,8,128]{3,2,1,0:T(8,128)S(1)} %get-tuple-element.47), channel_id=1, replica_groups={{0,2,4,6,8,10,12,14,16,18,20,22,24,26,28,30},{32,34,36,38,40,42,44,46,4..., dimensions={0} | all-to-all | bytes 655360 | tf_op jit(solution)/shard_map/all_to_all | solution.py:526
  41.2 0.2 shard_map.52
  41.3 3.8 %collective-permute-start.4 = (f32[24,8,128]{2,1,0:T(8,128)S(1)}, f32[24,8,128]{2,1,0:T(8,128)S(1)}, u32[]{:S(2)}, u32[]{:S(2)}) collective-permute-start(f32[24,8,128]{2,1,0:T(8,128)S(1)} %get-tuple-element.48), channel_id=1, source_target_pairs={{0,32},{8,40},{16,48},{24,56},{32,64},{40,72},{48,80},{56,88},{64,... | collective-permute-start | bytes 294920 | tf_op jit(solution)/shard_map/ppermute | solution.py:503
  45.2 7.0 %collective-permute-start.5 = (f32[24,8,128]{2,1,0:T(8,128)S(1)}, f32[24,8,128]{2,1,0:T(8,128)S(1)}, u32[]{:S(2)}, u32[]{:S(2)}) collective-permute-start(f32[24,8,128]{2,1,0:T(8,128)S(1)} %get-tuple-element.50), channel_id=1, source_target_pairs={{0,480},{8,488},{16,496},{24,504},{32,0},{40,8},{48,16},{56,24},{6... | collective-permute-start | bytes 294920 | tf_op jit(solution)/shard_map/ppermute | solution.py:503
  52.2 0.7 collective-permute-done.4.prev
  52.9 1.5 %collective-permute-done.5.nxt = f32[24,8,128]{2,1,0:T(8,128)S(1)} collective-permute-done((f32[24,8,128]{2,1,0:T(8,128)S(1)}, f32[24,8,128]{2,1,0:T(8,128)S(1)}, u32[]{:S(2)}, u32[]{:S(2)}) %collective-permute-start.5) | collective-permute-done | bytes 98336 | tf_op jit(solution)/shard_map/ppermute | solution.py:503
  54.4 0.5 shard_map.53
  54.9 6.3 %collective-permute-start.7 = (f32[6,8,128]{2,1,0:T(8,128)S(1)}, f32[6,8,128]{2,1,0:T(8,128)S(1)}, u32[]{:S(2)}, u32[]{:S(2)}) collective-permute-start(f32[6,8,128]{2,1,0:T(8,128)S(1)} %get-tuple-element.51.own3), channel_id=1, source_target_pairs={{0,448},{8,456},{16,464},{24,472},{32,480},{40,488},{48,496},{56,5... | collective-permute-start | bytes 73736 | tf_op jit(solution)/shard_map/ppermute | solution.py:503
  61.2 1.9 %collective-permute-start.6 = (f32[6,8,128]{2,1,0:T(8,128)S(1)}, f32[6,8,128]{2,1,0:T(8,128)S(1)}, u32[]{:S(2)}, u32[]{:S(2)}) collective-permute-start(f32[6,8,128]{2,1,0:T(8,128)S(1)} %get-tuple-element.51.own3), channel_id=1, source_target_pairs={{0,64},{8,72},{16,80},{24,88},{32,96},{40,104},{48,112},{56,120},{... | collective-permute-start | bytes 73736 | tf_op jit(solution)/shard_map/ppermute | solution.py:503
  63.1 0.3 shard_map.54
  63.4 5.6 %collective-permute-done.6.left3 = f32[6,8,128]{2,1,0:T(8,128)S(1)} collective-permute-done((f32[6,8,128]{2,1,0:T(8,128)S(1)}, f32[6,8,128]{2,1,0:T(8,128)S(1)}, u32[]{:S(2)}, u32[]{:S(2)}) %collective-permute-start.6) | collective-permute-done | bytes 24608 | tf_op jit(solution)/shard_map/ppermute | solution.py:503
  69.0 2.8 %shard_map.55 = (f32[8,32,128]{2,1,0:T(8,128)}, f32[8,32,128]{2,1,0:T(8,128)}) custom-call(f32[6,8,128]{2,1,0:T(8,128)S(1)} %get-tuple-element.51.own3, f32[6,8,128]{2,1,0:T(8,128)S(1)} %collective-permute-done.6.left3, f32[6,8,128]{2,1,0:T(8,128)S(1)} %collective-permute-done.7.right3, f32[24,8,128]{2,1,0:T(8,128)S(1)} %get-tuple-element.52.t2x, ...), custom_call_target="tpu_custom_call" | custom-call | tf_op jit(solution)/shard_map/pallas_call | solution.py:546
  (9 shorter events, 0.0 us)
Async XLA Ops:
  0.6 1.0 %copy-start = (f32[8,32,128]{2,1,0:T(8,128)S(1)}, f32[8,32,128]{2,1,0:T(8,128)}, u32[]{:S(2)}) copy-start(f32[8,32,128]{2,1,0:T(8,128)} %k.1) | copy-start | bytes 393220
  1.6 14.4 %copy-start.2 = (f32[8,32,128]{2,1,0:T(8,128)S(1)}, f32[8,32,128]{2,1,0:T(8,128)}, u32[]{:S(2)}) copy-start(f32[8,32,128]{2,1,0:T(8,128)} %s.3) | copy-start | bytes 393220
  1.6 14.4 %copy-start.1 = (f32[8,32,128]{2,1,0:T(8,128)S(1)}, f32[8,32,128]{2,1,0:T(8,128)}, u32[]{:S(2)}) copy-start(f32[8,32,128]{2,1,0:T(8,128)} %f.3) | copy-start | bytes 393220
  1.6 10.1 %collective-permute-start = (f32[24,8,128]{2,1,0:T(8,128)S(1)}, f32[24,8,128]{2,1,0:T(8,128)S(1)}, u32[]{:S(2)}, u32[]{:S(2)}) collective-permute-start(f32[24,8,128]{2,1,0:T(8,128)S(1)} %pad_maximum_fusion), channel_id=1, source_target_pairs={{2,0},{4,2},{6,4},{3,1},{5,3},{7,5},{10,8},{12,10},{14,12},{11,9},... | collective-permute-start | bytes 294920 | tf_op jit(solution)/shard_map/ppermute | solution.py:498
  9.5 6.5 %collective-permute-start.1 = (f32[24,8,128]{2,1,0:T(8,128)S(1)}, f32[24,8,128]{2,1,0:T(8,128)S(1)}, u32[]{:S(2)}, u32[]{:S(2)}) collective-permute-start(f32[24,8,128]{2,1,0:T(8,128)S(1)} %pad_maximum_fusion.1), channel_id=1, source_target_pairs={{0,2},{2,4},{4,6},{1,3},{3,5},{5,7},{8,10},{10,12},{12,14},{9,11},... | collective-permute-start | bytes 294920 | tf_op jit(solution)/shard_map/ppermute | solution.py:498
  16.5 5.3 %collective-permute-start.2 = (f32[536,128]{1,0:T(8,128)S(1)}, f32[536,128]{1,0:T(8,128)S(1)}, u32[]{:S(2)}, u32[]{:S(2)}) collective-permute-start(f32[536,128]{1,0:T(8,128)S(1)} %get-tuple-element.45), channel_id=1, source_target_pairs={{0,8},{8,16},{16,24},{24,32},{32,40},{40,48},{48,56},{56,64},{64,7... | collective-permute-start | bytes 823304 | tf_op jit(solution)/shard_map/ppermute | solution.py:498
  17.8 8.4 %collective-permute-start.3 = (f32[536,128]{1,0:T(8,128)S(1)}, f32[536,128]{1,0:T(8,128)S(1)}, u32[]{:S(2)}, u32[]{:S(2)}) collective-permute-start(f32[536,128]{1,0:T(8,128)S(1)} %get-tuple-element.46), channel_id=1, source_target_pairs={{8,0},{16,8},{24,16},{32,24},{40,32},{48,40},{56,48},{64,56},{72,6... | collective-permute-start | bytes 823304 | tf_op jit(solution)/shard_map/ppermute | solution.py:498
  41.3 11.5 %collective-permute-start.4 = (f32[24,8,128]{2,1,0:T(8,128)S(1)}, f32[24,8,128]{2,1,0:T(8,128)S(1)}, u32[]{:S(2)}, u32[]{:S(2)}) collective-permute-start(f32[24,8,128]{2,1,0:T(8,128)S(1)} %get-tuple-element.48), channel_id=1, source_target_pairs={{0,32},{8,40},{16,48},{24,56},{32,64},{40,72},{48,80},{56,88},{64,... | collective-permute-start | bytes 294920 | tf_op jit(solution)/shard_map/ppermute | solution.py:503
  45.2 9.2 %collective-permute-start.5 = (f32[24,8,128]{2,1,0:T(8,128)S(1)}, f32[24,8,128]{2,1,0:T(8,128)S(1)}, u32[]{:S(2)}, u32[]{:S(2)}) collective-permute-start(f32[24,8,128]{2,1,0:T(8,128)S(1)} %get-tuple-element.50), channel_id=1, source_target_pairs={{0,480},{8,488},{16,496},{24,504},{32,0},{40,8},{48,16},{56,24},{6... | collective-permute-start | bytes 294920 | tf_op jit(solution)/shard_map/ppermute | solution.py:503
  54.9 8.5 %collective-permute-start.7 = (f32[6,8,128]{2,1,0:T(8,128)S(1)}, f32[6,8,128]{2,1,0:T(8,128)S(1)}, u32[]{:S(2)}, u32[]{:S(2)}) collective-permute-start(f32[6,8,128]{2,1,0:T(8,128)S(1)} %get-tuple-element.51.own3), channel_id=1, source_target_pairs={{0,448},{8,456},{16,464},{24,472},{32,480},{40,488},{48,496},{56,5... | collective-permute-start | bytes 73736 | tf_op jit(solution)/shard_map/ppermute | solution.py:503
  61.2 7.8 %collective-permute-start.6 = (f32[6,8,128]{2,1,0:T(8,128)S(1)}, f32[6,8,128]{2,1,0:T(8,128)S(1)}, u32[]{:S(2)}, u32[]{:S(2)}) collective-permute-start(f32[6,8,128]{2,1,0:T(8,128)S(1)} %get-tuple-element.51.own3), channel_id=1, source_target_pairs={{0,64},{8,72},{16,80},{24,88},{32,96},{40,104},{48,112},{56,120},{... | collective-permute-start | bytes 73736 | tf_op jit(solution)/shard_map/ppermute | solution.py:503
